TPU v7x, 512 devices: a whole 4x8x8 slice. The times are simulated.
512 devices in a mesh: dp: 32 (over x, y), expert: 8 (over z), tensor: 2 (over core).
Axes of the slice: x: 4, y: 8, z: 8, core: 2. Of those that a mesh axis runs over, the one named last changes fastest.
Arguments:
- tokens: bfloat16 [32768, 2560], P(('dp', 'expert'), 'tensor'), may hold values from -6 to 6
- target: bfloat16 [32768, 2560], P(('dp', 'expert'), 'tensor'), may hold values from -6 to 6
- expert_ids: int32 [32768], P(('dp', 'expert')), may hold values from 0 to 127, as said below
- doc_lengths: int32 [256, 8], P(('dp', 'expert')), may hold values from 1 to 16, as said below
- w_gate: bfloat16 [8, 2560, 8192], P('expert', 'tensor', 'dp'), may hold values from -0.125 to 0.125
- w_up: bfloat16 [8, 2560, 8192], P('expert', 'tensor', 'dp'), may hold values from -0.125 to 0.125
- w_down: bfloat16 [8, 8192, 2560], P('expert', 'dp', 'tensor'), may hold values from -0.0625 to 0.0625
Outputs:
- grad_tokens: bfloat16 [32768, 2560], P(('dp', 'expert'), 'tensor')
- grad_gate: bfloat16 [8, 2560, 8192], P('expert', 'tensor', 'dp')
- grad_up: bfloat16 [8, 2560, 8192], P('expert', 'tensor', 'dp')
- grad_down: bfloat16 [8, 8192, 2560], P('expert', 'dp', 'tensor')
Inputs may be any that keep to these rules, and one draw needn't show every extreme that they name: `expert_ids`: among the 128 tokens of one packed row no id appears more than 2 times, and in every row one id below 8 appears exactly 2 times. `doc_lengths`: every row holds a document of 16 tokens; the lengths of a row sum to at most 128.
All inputs are finite; a program needn't handle non-finite values.
Results may differ from a plain program's by a relative error of at most 0.03.
Values may be sent and summed in bfloat16 or wider, within the bound.
No kernel may reach another device: no remote copies, remote signals or barrier semaphores. Data moves between devices by JAX's collectives and lax.ppermute only.
A program may use at most 64 MiB of HBM per device.

v0:
```python
import jax
import jax.numpy as jnp
from jax import lax
from jax.sharding import PartitionSpec as P

CAP = 2


def silu_slope(gate_val):
    sig = jax.nn.sigmoid(gate_val)
    return sig * (1.0 + gate_val * (1.0 - sig))


def local(tokens, target, expert_ids, doc_lengths, w_gate, w_up, w_down):
    row_len, features = tokens.shape
    win_count = lax.axis_size("expert")
    dp_count = lax.axis_size("dp")
    slot_count = win_count * CAP
    total_rows = dp_count * slot_count
    contract_rows = (((0,), (0,)), ((), ()))
    contract_cols = (((1,), (1,)), ((), ()))
    live_mask = (jnp.arange(row_len) < jnp.sum(doc_lengths)).astype(jnp.float32)
    one_hot = (expert_ids[:, None] == jnp.arange(win_count)[None, :]).astype(jnp.int32)
    order_rank = jnp.cumsum(one_hot, axis=0) - 1
    placed = (one_hot[:, :, None] == 1) & (order_rank[:, :, None] == jnp.arange(CAP)[None, None, :])
    select = placed.reshape(row_len, slot_count).astype(jnp.bfloat16)

    def to_slots(values):
        moved = lax.dot_general(select, values, contract_rows, preferred_element_type=jnp.float32)
        return moved.astype(jnp.bfloat16).reshape(win_count, CAP, features)

    def from_slots(slots):
        return jnp.dot(
            select, slots.reshape(slot_count, features), preferred_element_type=jnp.float32
        )

    arrived = lax.all_to_all(to_slots(tokens), "expert", split_axis=0, concat_axis=0, tiled=True)
    row_data = lax.all_gather(arrived, "dp", axis=0, tiled=True).reshape(total_rows, features)
    gate_part = jnp.dot(row_data, w_gate[0], preferred_element_type=jnp.float32)
    up_part = jnp.dot(row_data, w_up[0], preferred_element_type=jnp.float32)
    gate_val, up_val = (
        lax.psum(gate_part.astype(jnp.bfloat16), "tensor").astype(jnp.float32),
        lax.psum(up_part.astype(jnp.bfloat16), "tensor").astype(jnp.float32),
    )
    hidden = (jax.nn.silu(gate_val) * up_val).astype(jnp.bfloat16)
    expert_rows = lax.psum_scatter(
        jnp.dot(hidden, w_down[0], preferred_element_type=jnp.float32).astype(jnp.bfloat16),
        "dp",
        scatter_dimension=0,
        tiled=True,
    )
    home_rows = lax.all_to_all(
        expert_rows.reshape(win_count, CAP, features),
        "expert",
        split_axis=0,
        concat_axis=0,
        tiled=True,
    )
    output = tokens.astype(jnp.float32) + from_slots(home_rows)
    residual_grad = (live_mask[:, None] * (output - target.astype(jnp.float32))).astype(
        jnp.bfloat16
    )
    grads_arrived = lax.all_to_all(
        to_slots(residual_grad), "expert", split_axis=0, concat_axis=0, tiled=True
    )
    grad_rows = lax.all_gather(grads_arrived, "dp", axis=0, tiled=True).reshape(
        total_rows, features
    )
    hidden_part = lax.dot_general(
        grad_rows, w_down[0], contract_cols, preferred_element_type=jnp.float32
    )
    hidden_grad = lax.psum(hidden_part.astype(jnp.bfloat16), "tensor").astype(jnp.float32)
    gate_grad = (hidden_grad * up_val * silu_slope(gate_val)).astype(jnp.bfloat16)
    up_grad = (hidden_grad * jax.nn.silu(gate_val)).astype(jnp.bfloat16)
    grad_down = lax.dot_general(
        hidden, grad_rows, contract_rows, preferred_element_type=jnp.float32
    ).astype(jnp.bfloat16)
    grad_gate = lax.dot_general(
        row_data, gate_grad, contract_rows, preferred_element_type=jnp.float32
    ).astype(jnp.bfloat16)
    grad_up = lax.dot_general(
        row_data, up_grad, contract_rows, preferred_element_type=jnp.float32
    ).astype(jnp.bfloat16)
    first = lax.dot_general(gate_grad, w_gate[0], contract_cols, preferred_element_type=jnp.float32)
    second = lax.dot_general(up_grad, w_up[0], contract_cols, preferred_element_type=jnp.float32)
    input_rows = lax.psum_scatter(
        (first + second).astype(jnp.bfloat16), "dp", scatter_dimension=0, tiled=True
    )
    home_grads = lax.all_to_all(
        input_rows.reshape(win_count, CAP, features),
        "expert",
        split_axis=0,
        concat_axis=0,
        tiled=True,
    )
    grad_tokens = (residual_grad.astype(jnp.float32) + from_slots(home_grads)).astype(jnp.bfloat16)
    return (grad_tokens, grad_gate[None], grad_up[None], grad_down[None])


def solution(mesh):
    placed = (
        P(("dp", "expert"), "tensor"),
        P(("dp", "expert"), "tensor"),
        P(("dp", "expert")),
        P(("dp", "expert"), None),
        P("expert", "tensor", "dp"),
        P("expert", "tensor", "dp"),
        P("expert", "dp", "tensor"),
    )
    return jax.shard_map(
        local,
        mesh=mesh,
        in_specs=placed,
        out_specs=(
            P(("dp", "expert"), "tensor"),
            P("expert", "tensor", "dp"),
            P("expert", "tensor", "dp"),
            P("expert", "dp", "tensor"),
        ),
        check_vma=False,
    )
```

profile of v0, /device:TPU:6, one launch (start us, length us, event | category | flops | bytes accessed | tf_op | source)
XLA Modules:
  0.0 768.0 jit_solution(17965501575403241029)
XLA Ops:
  9.7 18.3 %all_to_all.20 = bf16[8,2,1280]{2,1,0:T(2,128)(2,1)} all-to-all(bf16[8,2,1280]{2,1,0:T(2,128)(2,1)S(1)} %reshape.85), channel_id=1, replica_groups=mesh['dp'=32,'expert'=8,'tensor'=2] {'expert'}, dimensions={0} | all-to-all | bytes 81920 | tf_op jit(solution)/shard_map/all_to_all | solution.py:37
  28.1 76.9 %all-gather.3.cloned.1.call-done = bf16[256,2,1280]{2,1,0:T(2,128)(2,1)} async-done(((bf16[8,2,1280]{2,1,0:T(2,128)(2,1)}), bf16[256,2,1280]{2,1,0:T(2,128)(2,1)}) %all-gather.3.cloned.1.call-update) | async-done | bytes 1310736 | tf_op jit(solution)/shard_map/all_gather | solution.py:38
  105.1 3.2 reshape.86
  110.8 34.5 %all-reduce.6.cloned.1.call-done = (bf16[512,256]{1,0:T(8,128)(2,1)}, bf16[512,256]{1,0:T(8,128)(2,1)}) async-done(((bf16[512,256]{1,0:T(8,128)(2,1)}, bf16[512,256]{1,0:T(8,128)(2,1)}), (bf16[512,256]{1,0:T(8,128)(2,1)}, bf16[512,256]{1,0:T(8,128)(2,1)})) %all-reduce.6.cloned.1.call-update) | async-done | bytes 524304 | tf_op jit(solution)/shard_map/psum | solution.py:43
  145.3 2.7 convolution_convert_fusion
  149.3 222.7 %reduce-scatter.3.cloned.1.call-done = bf16[16,1280]{1,0:T(8,128)(2,1)} async-done(((bf16[512,1280]{1,0:T(8,128)(2,1)}), bf16[16,1280]{1,0:T(8,128)(2,1)}) %reduce-scatter.3.cloned.1.call-update) | async-done | bytes 40976 | tf_op jit(solution)/shard_map/reduce_scatter | solution.py:46
  371.9 1.4 reshape.87
  373.4 7.4 all-to-all-start.1
  381.5 7.4 all-to-all-done.1
  388.9 1.3 fusion.8
  390.4 11.2 %all_to_all.21 = bf16[8,2,1280]{2,1,0:T(2,128)(2,1)} all-to-all(bf16[8,2,1280]{2,1,0:T(2,128)(2,1)S(1)} %reshape.88), channel_id=1, replica_groups=mesh['dp'=32,'expert'=8,'tensor'=2] {'expert'}, dimensions={0} | all-to-all | bytes 81920 | tf_op jit(solution)/shard_map/all_to_all | solution.py:63
  401.6 75.0 %all-gather.5.cloned.1.call-done = bf16[256,2,1280]{2,1,0:T(2,128)(2,1)} async-done(((bf16[8,2,1280]{2,1,0:T(2,128)(2,1)}), bf16[256,2,1280]{2,1,0:T(2,128)(2,1)}) %all-gather.5.cloned.1.call-update) | async-done | bytes 1310736 | tf_op jit(solution)/shard_map/all_gather | solution.py:66
  476.6 4.1 reshape.89
  480.7 2.6 convolution_convert_fusion.6
  483.3 33.9 %all-reduce.4.cloned.1.call-done = bf16[512,256]{1,0:T(8,128)(2,1)} async-done(((bf16[512,256]{1,0:T(8,128)(2,1)}), bf16[512,256]{1,0:T(8,128)(2,1)}) %all-reduce.4.cloned.1.call-update) | async-done | bytes 262160 | tf_op jit(solution)/shard_map/psum | solution.py:72
  517.3 2.0 fusion.14
  519.2 1.7 fusion
  521.9 2.7 fusion.3
  524.6 1.6 fusion.1
  526.2 217.0 %reduce-scatter.5.cloned.1.call-done = bf16[16,1280]{1,0:T(8,128)(2,1)} async-done(((bf16[512,1280]{1,0:T(8,128)(2,1)}), bf16[16,1280]{1,0:T(8,128)(2,1)}) %reduce-scatter.5.cloned.1.call-update) | async-done | bytes 40976 | tf_op jit(solution)/shard_map/reduce_scatter | solution.py:86
  743.2 1.4 reshape.90
  744.6 7.4 all-to-all-start.3
  752.0 1.5 fusion.2
  753.5 6.6 all-to-all-done.3
  (49 shorter events, 9.3 us)
Async XLA Ops:
  7.2 138.1 %copy-start = (bf16[1,256,1280]{2,1,0:T(8,128)(2,1)S(1)}, bf16[1,256,1280]{2,1,0:T(8,128)(2,1)}, u32[]{:S(2)}) copy-start(bf16[1,256,1280]{2,1,0:T(8,128)(2,1)} %param.13) | copy-start | bytes 1966084
  7.2 97.9 %all-gather.3.cloned.1.call-start = ((), (), s32[]{:S(2)}) async-start(), calls=%async_computation.6 | async-start | bytes 1351680 | tf_op jit(solution)/shard_map/all_gather | solution.py:38
  28.1 80.2 %copy-start.2 = (bf16[1,1280,256]{2,1,0:T(8,128)(2,1)S(1)}, bf16[1,1280,256]{2,1,0:T(8,128)(2,1)}, u32[]{:S(2)}) copy-start(bf16[1,1280,256]{2,1,0:T(8,128)(2,1)} %param.12) | copy-start | bytes 1966084
  28.1 117.2 %all-reduce.6.cloned.1.call-start = ((), (), s32[]{:S(2)}) async-start(), calls=%async_computation.11 | async-start | bytes 1048576 | tf_op jit(solution)/shard_map/psum | solution.py:43
  108.3 1.2 copy-start.5
  110.8 261.2 %reduce-scatter.3.cloned.1.call-start = ((), (), s32[]{:S(2)}) async-start(), calls=%async_computation.7 | async-start | bytes 1351680 | tf_op jit(solution)/shard_map/reduce_scatter | solution.py:46
  148.0 0.7 copy-start.7
  148.0 240.9 %copy-start.1 = (bf16[128,1280]{1,0:T(8,128)(2,1)S(1)}, bf16[128,1280]{1,0:T(8,128)(2,1)}, u32[]{:S(2)}) copy-start(bf16[128,1280]{1,0:T(8,128)(2,1)} %param.7) | copy-start | bytes 983044
  373.4 15.5 %all-to-all-start.1 = ((bf16[8,2,1280]{2,1,0:T(2,128)(2,1)}), bf16[8,2,1280]{2,1,0:T(2,128)(2,1)S(1)}, u32[]{:S(2)}, u32[]{:S(2)}) async-start(bf16[8,2,1280]{2,1,0:T(2,128)(2,1)} %reshape.87), calls=%async_computation.2 | async-start | bytes 81920 | tf_op jit(solution)/shard_map/all_to_all | solution.py:52
  380.8 95.8 %all-gather.5.cloned.1.call-start = ((), (), s32[]{:S(2)}) async-start(), calls=%async_computation.8 | async-start | bytes 1351680 | tf_op jit(solution)/shard_map/all_gather | solution.py:66
  401.6 115.7 %all-reduce.4.cloned.1.call-start = ((), (), s32[]{:S(2)}) async-start(), calls=%async_computation.9 | async-start | bytes 524288 | tf_op jit(solution)/shard_map/psum | solution.py:72
  480.7 36.6 %copy-start.3 = (bf16[512,256]{1,0:T(8,128)(2,1)S(1)}, bf16[512,256]{1,0:T(8,128)(2,1)}, u32[]{:S(2)}) copy-start(bf16[512,256]{1,0:T(8,128)(2,1)} %get-tuple-element.5) | copy-start | bytes 786436
  483.3 259.9 %reduce-scatter.5.cloned.1.call-start = ((), (), s32[]{:S(2)}) async-start(), calls=%async_computation.10 | async-start | bytes 1351680 | tf_op jit(solution)/shard_map/reduce_scatter | solution.py:86
  517.3 2.0 copy-start.4
  520.9 0.9 copy-start.6
  744.6 15.5 %all-to-all-start.3 = ((bf16[8,2,1280]{2,1,0:T(2,128)(2,1)}), bf16[8,2,1280]{2,1,0:T(2,128)(2,1)S(1)}, u32[]{:S(2)}, u32[]{:S(2)}) async-start(bf16[8,2,1280]{2,1,0:T(2,128)(2,1)} %reshape.90), calls=%async_computation.5 | async-start | bytes 81920 | tf_op jit(solution)/shard_map/all_to_all | solution.py:89
Sparse Core Ops, SparseCore 0:
  28.2 76.8 all-gather.2
  110.9 34.3 all-reduce.5
  150.3 221.5 reduce-scatter.2
  401.7 74.8 all-gather.4
  483.4 33.8 all-reduce.3
  521.5 221.6 reduce-scatter.4
where the time goes:
time: 769 us; the launch traced here: 768 us
  waiting for transfers between devices  674 us (88%)
  blocking collectives  29.5 us (4%)
  matrix products  20.8 us (3%)
  starting transfers between devices  15 us (2%)
  between operations  14.2 us (2%)
  local copies, waits for them, and re-layouts  12 us (2%)
    reduce_scatter x1, waiting for transfers between devices, local(): lax.psum_scatter(jnp.dot(hidden, w_down[0], preferred_element_type=jnp.fl...  223 us
    reduce_scatter x1, waiting for transfers between devices, local(): lax.psum_scatter((first + second).astype(jnp.bfloat16), 'dp', scatter_dim...  217 us
    all_gather x1, waiting for transfers between devices, local(): lax.all_gather(arrived, 'dp', axis=0, tiled=True)  76.9 us
    all_gather x1, waiting for transfers between devices, local(): lax.all_gather(grads_arrived, 'dp', axis=0, tiled=True)  75 us
    psum x1, waiting for transfers between devices, local(): lax.psum(up_part.astype(jnp.bfloat16), 'tensor').astype(jnp.float32)  34.5 us
    psum x1, waiting for transfers between devices, local(): lax.psum(hidden_part.astype(jnp.bfloat16), 'tensor').astype(jnp.float32)  33.9 us
    all_to_all x1, blocking collectives, local(): lax.all_to_all(to_slots(tokens), 'expert', split_axis=0, concat_axis=0, t...  18.3 us
  transfers between devices with their start and end apart: 8, of which 8 were waited for; matrix products, arithmetic and copies ran while one was open for 1% of the time, Pallas kernels for 0%

commit v1 on v0

v1 whole, which is shorter than its diff:
```python
import jax
import jax.numpy as jnp
from jax import lax
from jax.sharding import Mesh, PartitionSpec as P

CAP = 2
NX, NY, NZ = 4, 8, 8
F32, BF16 = jnp.float32, jnp.bfloat16
CONTRACT_ROWS = (((0,), (0,)), ((), ()))
CONTRACT_COLS = (((1,), (1,)), ((), ()))


def silu_slope(gate_val):
    sig = jax.nn.sigmoid(gate_val)
    return sig * (1.0 + gate_val * (1.0 - sig))


def ring(value, axis, size, shift):
    return lax.ppermute(value, axis, [(i, (i + shift) % size) for i in range(size)])


def swap_add(part):
    mine = part.astype(BF16)
    other = lax.ppermute(mine, "c", [(0, 1), (1, 0)])
    return mine.astype(F32) + other.astype(F32)


def spread(rows):
    blocks = jnp.broadcast_to(rows[None], (NY,) + rows.shape)
    column = lax.all_to_all(blocks, "y", 0, 0, tiled=True).reshape(NY * rows.shape[0], rows.shape[1])
    return [column] + [ring(column, "x", NX, s) for s in SHIFTS]


SHIFTS = (1, 3, 2)


def gather_x(parts):
    total = parts[0].astype(F32)
    for s, part in zip(SHIFTS, parts[1:]):
        total = total + ring(part.astype(BF16), "x", NX, NX - s).astype(F32)
    return total


def local(tokens, target, expert_ids, doc_lengths, w_gate, w_up, w_down):
    row_len, features = tokens.shape
    slot_count = NZ * CAP
    w_gate, w_up, w_down = w_gate[0], w_up[0], w_down[0]
    live = jnp.arange(row_len) < jnp.sum(doc_lengths)
    one_hot = (expert_ids[:, None] == jnp.arange(NZ)[None, :]).astype(jnp.int32)
    order_rank = jnp.cumsum(one_hot, axis=0) - 1
    placed = (one_hot[:, :, None] == 1) & (order_rank[:, :, None] == jnp.arange(CAP)[None, None, :])
    placed = placed & live[:, None, None]
    select = placed.reshape(row_len, slot_count).astype(BF16)

    def to_slots(values):
        moved = lax.dot_general(select, values, CONTRACT_ROWS, preferred_element_type=F32)
        return moved.astype(BF16).reshape(NZ, CAP, features)

    both = jnp.concatenate([to_slots(tokens), to_slots(target)], axis=1)
    arrived = lax.all_to_all(both, "z", 0, 0, tiled=True)
    my_rows = arrived[:, :CAP].reshape(slot_count, features)
    my_target = arrived[:, CAP:].reshape(slot_count, features)

    chunks = spread(my_rows)
    gates, ups, hiddens, parts = [], [], [], []
    for rows in chunks:
        gate_part = jnp.dot(rows, w_gate, preferred_element_type=F32)
        up_part = jnp.dot(rows, w_up, preferred_element_type=F32)
        summed = swap_add(jnp.concatenate([gate_part, up_part], axis=1))
        gate_val, up_val = summed[:, : w_gate.shape[1]], summed[:, w_gate.shape[1] :]
        hidden = (jax.nn.silu(gate_val) * up_val).astype(BF16)
        gates.append(gate_val)
        ups.append(up_val)
        hiddens.append(hidden)
        parts.append(jnp.dot(hidden, w_down, preferred_element_type=F32).astype(BF16))
    column = gather_x(parts).astype(BF16).reshape(NY, slot_count, features)
    pieces = lax.all_to_all(column, "y", 0, 0, tiled=True)
    expert_rows = jnp.sum(pieces.astype(F32), axis=0).astype(BF16)
    residual = (my_rows.astype(F32) + expert_rows.astype(F32) - my_target.astype(F32)).astype(BF16)

    grad_chunks = spread(residual)
    gate_grads, up_grads, parts = [], [], []
    for i, grads in enumerate(grad_chunks):
        hidden_grad = swap_add(lax.dot_general(grads, w_down, CONTRACT_COLS, preferred_element_type=F32))
        gate_grad = (hidden_grad * ups[i] * silu_slope(gates[i])).astype(BF16)
        up_grad = (hidden_grad * jax.nn.silu(gates[i])).astype(BF16)
        gate_grads.append(gate_grad)
        up_grads.append(up_grad)
        first = lax.dot_general(gate_grad, w_gate, CONTRACT_COLS, preferred_element_type=F32)
        second = lax.dot_general(up_grad, w_up, CONTRACT_COLS, preferred_element_type=F32)
        parts.append((first + second).astype(BF16))
    mine = (jnp.arange(NY * slot_count) // slot_count) == lax.axis_index("y")
    column = gather_x(parts) + jnp.where(mine[:, None], grad_chunks[0].astype(F32), 0.0)
    pieces = lax.all_to_all(
        column.astype(BF16).reshape(NY * NZ, CAP, features), ("y", "z"), 0, 0, tiled=True
    )
    slots = jnp.sum(pieces.reshape(NY, slot_count, features).astype(F32), axis=0).astype(BF16)

    all_rows = jnp.concatenate(chunks, axis=0)
    all_grads = jnp.concatenate(grad_chunks, axis=0)

    def weight_grad(left, right):
        return lax.dot_general(left, right, CONTRACT_ROWS, preferred_element_type=F32).astype(BF16)

    grad_down = weight_grad(jnp.concatenate(hiddens, axis=0), all_grads)
    grad_gate = weight_grad(all_rows, jnp.concatenate(gate_grads, axis=0))
    grad_up = weight_grad(all_rows, jnp.concatenate(up_grads, axis=0))

    routed = jnp.dot(select, slots, preferred_element_type=F32)
    unrouted = live & ~jnp.any(placed, axis=(1, 2))
    own = jnp.where(unrouted[:, None], tokens.astype(F32) - target.astype(F32), 0.0)
    grad_tokens = (own + routed).astype(BF16)
    return (grad_tokens, grad_gate[None], grad_up[None], grad_down[None])


def solution(mesh):
    cube = Mesh(mesh.devices.reshape(NX, NY, NZ, 2), ("x", "y", "z", "c"))
    token_spec = P(("x", "y", "z"), "c")
    in_spec, out_spec = P("z", "c", ("x", "y")), P("z", ("x", "y"), "c")
    return jax.shard_map(
        local,
        mesh=cube,
        in_specs=(token_spec, token_spec, P(("x", "y", "z")), P(("x", "y", "z"), None), in_spec, in_spec, out_spec),
        out_specs=(token_spec, in_spec, in_spec, out_spec),
        check_vma=False,
    )
```

time: 769 us -> 206 us (0.27)
  waiting for transfers between devices: 674 us -> 67.6 us
  starting transfers between devices: 15 us -> 67.3 us
  between operations: 14.2 us -> 1.63 us
  blocking collectives: 29.5 us -> 37.7 us
    reduce_scatter x2 -> x0, waiting for transfers between devices: 440 us -> none  [the longest x1 223 us: local(): lax.psum_scatter(jnp.dot(hidden, w_down[0], preferred_element_type=jnp.fl...]
    all_gather x2 -> x0, waiting for transfers between devices: 152 us -> none  [the longest x1 76.9 us: local(): lax.all_gather(arrived, 'dp', axis=0, tiled=True)]
    psum x2 -> x0, waiting for transfers between devices: 68.4 us -> none  [the longest x1 34.5 us: local(): lax.psum(up_part.astype(jnp.bfloat16), 'tensor').astype(jnp.float32)]
    ppermute x0 -> x20, starting transfers between devices: none -> 55.8 us  [the longest x12 39.3 us: ring(): lax.ppermute(value, axis, [(i, (i + shift) % size) for i in range(size)])]
    ppermute x0 -> x20, waiting for transfers between devices: none -> 37.3 us  [the longest x12 37.3 us: ring(): lax.ppermute(value, axis, [(i, (i + shift) % size) for i in range(size)])]
    all_to_all x2 -> x3, waiting for transfers between devices: 14 us -> 30.3 us  [the longest x1 11.1 us: spread(): lax.all_to_all(blocks, 'y', 0, 0, tiled=True)]
    reshape x6 -> x5, local copies, waits for them, and re-layouts: 10.2 us -> 1.05 us  [the longest x1 0.85 us: local(): column.astype(BF16).reshape(NY * NZ, CAP, features)]
    all_to_all x2, blocking collectives: 29.5 us -> 37.7 us  [the longest x1 19 us: spread(): lax.all_to_all(blocks, 'y', 0, 0, tiled=True)]
  transfers between devices with their start and end apart: 8 -> 23, of which waited for: 8 -> 11; matrix products, arithmetic and copies ran while one was open for 1% -> 7% of each run, Pallas kernels for 0% -> 0%
where the time goes in v1:
time: 206 us; the launch traced here: 202 us
  waiting for transfers between devices  67.6 us (33%)
  starting transfers between devices  67.3 us (33%)
  blocking collectives  37.7 us (18%)
  matrix products  15.1 us (7%)
  other arithmetic  6.4 us (3%)
  local copies, waits for them, and re-layouts  6.02 us (3%)
    ppermute x12, starting transfers between devices, ring(): lax.ppermute(value, axis, [(i, (i + shift) % size) for i in range(size)])  39.3 us
    ppermute x12, waiting for transfers between devices, ring(): lax.ppermute(value, axis, [(i, (i + shift) % size) for i in range(size)])  37.3 us
    all_to_all x1, blocking collectives, spread(): lax.all_to_all(blocks, 'y', 0, 0, tiled=True)  19 us
    all_to_all x1, blocking collectives, local(): arrived = lax.all_to_all(both, 'z', 0, 0, tiled=True)  18.7 us
    ppermute x8, starting transfers between devices, swap_add(): other = lax.ppermute(mine, 'c', [(0, 1), (1, 0)])  16.5 us
    all_to_all x1, waiting for transfers between devices, spread(): lax.all_to_all(blocks, 'y', 0, 0, tiled=True)  11.1 us
    all_to_all x1, waiting for transfers between devices, local(): pieces = lax.all_to_all(column, 'y', 0, 0, tiled=True)  10.5 us
    all_to_all x1, waiting for transfers between devices, local(): lax.all_to_all(column.astype(BF16).reshape(NY * NZ, CAP, features), ('y',...  8.8 us
  transfers between devices with their start and end apart: 23, of which 11 were waited for; matrix products, arithmetic and copies ran while one was open for 7% of the time, Pallas kernels for 0%

profile of v1, /device:TPU:6, one launch (start us, length us, event | category | flops | bytes accessed | tf_op | source)
XLA Modules:
  0.0 201.8 jit_solution(9285017598358570275)
XLA Ops:
  5.4 18.7 %all_to_all.25 = bf16[8,4,1280]{2,1,0:T(4,128)(2,1)S(1)} all-to-all(bf16[8,4,1280]{2,1,0:T(4,128)(2,1)S(1)} %pad_maximum_fusion.7), channel_id=1, replica_groups=mesh['x'=4,'y'=8,'z'=8,'c'=2] {'z'}, dimensions={0} | all-to-all | bytes 163840 | tf_op jit(solution)/shard_map/all_to_all | solution.py:60
  24.2 19.0 %all_to_all.26 = bf16[8,16,1280]{2,1,0:T(8,128)(2,1)S(1)} all-to-all(bf16[8,16,1280]{2,1,0:T(8,128)(2,1)S(1)} %broadcast_in_dim.48), channel_id=1, replica_groups=mesh['x'=4,'y'=8,'z'=8,'c'=2] {'y'}, dimensions={0} | all-to-all | bytes 655360 | tf_op jit(solution)/shard_map/all_to_all | solution.py:30
  46.5 2.4 %collective-permute-start.1 = (bf16[128,1280]{1,0:T(8,128)(2,1)S(1)}, bf16[128,1280]{1,0:T(8,128)(2,1)S(1)}, u32[]{:S(2)}, u32[]{:S(2)}) collective-permute-start(bf16[128,1280]{1,0:T(8,128)(2,1)S(1)} %bitcast.101), channel_id=1, source_target_pairs={{0,128},{128,256},{256,384},{384,0},{1,129},{129,257},{257,385},{3... | collective-permute-start | bytes 983048 | tf_op jit(solution)/shard_map/ppermute | solution.py:19
  48.9 3.5 %collective-permute-start.4 = (bf16[128,1280]{1,0:T(8,128)(2,1)S(1)}, bf16[128,1280]{1,0:T(8,128)(2,1)S(1)}, u32[]{:S(2)}, u32[]{:S(2)}) collective-permute-start(bf16[128,1280]{1,0:T(8,128)(2,1)S(1)} %bitcast.102), channel_id=1, source_target_pairs={{0,384},{128,0},{256,128},{384,256},{1,385},{129,1},{257,129},{385... | collective-permute-start | bytes 983048 | tf_op jit(solution)/shard_map/ppermute | solution.py:19
  52.4 3.3 %collective-permute-start.7 = (bf16[128,1280]{1,0:T(8,128)(2,1)S(1)}, bf16[128,1280]{1,0:T(8,128)(2,1)S(1)}, u32[]{:S(2)}, u32[]{:S(2)}) collective-permute-start(bf16[128,1280]{1,0:T(8,128)(2,1)S(1)} %bitcast.103), channel_id=1, source_target_pairs={{0,256},{128,384},{256,0},{384,128},{1,257},{129,385},{257,1},{385... | collective-permute-start | bytes 983048 | tf_op jit(solution)/shard_map/ppermute | solution.py:19
  55.7 3.2 %collective-permute-done.1 = bf16[128,1280]{1,0:T(8,128)(2,1)S(1)} collective-permute-done((bf16[128,1280]{1,0:T(8,128)(2,1)S(1)}, bf16[128,1280]{1,0:T(8,128)(2,1)S(1)}, u32[]{:S(2)}, u32[]{:S(2)}) %collective-permute-start.1) | collective-permute-done | bytes 327712 | tf_op jit(solution)/shard_map/ppermute | solution.py:19
  61.6 7.3 %collective-permute-done.4 = bf16[128,1280]{1,0:T(8,128)(2,1)S(1)} collective-permute-done((bf16[128,1280]{1,0:T(8,128)(2,1)S(1)}, bf16[128,1280]{1,0:T(8,128)(2,1)S(1)}, u32[]{:S(2)}, u32[]{:S(2)}) %collective-permute-start.4) | collective-permute-done | bytes 327712 | tf_op jit(solution)/shard_map/ppermute | solution.py:19
  72.3 2.4 %collective-permute-start.8 = (bf16[128,512]{1,0:T(8,128)(2,1)S(1)}, bf16[128,512]{1,0:T(8,128)(2,1)S(1)}, u32[]{:S(2)}, u32[]{:S(2)}) collective-permute-start(bf16[128,512]{1,0:T(8,128)(2,1)S(1)} %pad_maximum_fusion.6), channel_id=1, source_target_pairs={{0,1},{1,0},{2,3},{3,2},{4,5},{5,4},{6,7},{7,6},{8,9},{9,8},{10,11... | collective-permute-start | bytes 393224 | tf_op jit(solution)/shard_map/ppermute | solution.py:24
  77.8 5.1 %collective-permute-start.6 = (bf16[128,1280]{1,0:T(8,128)(2,1)S(1)}, bf16[128,1280]{1,0:T(8,128)(2,1)S(1)}, u32[]{:S(2)}, u32[]{:S(2)}) collective-permute-start(bf16[128,1280]{1,0:T(8,128)(2,1)S(1)} %convolution_convert_fusion.4), channel_id=1, source_target_pairs={{0,128},{128,256},{256,384},{384,0},{1,129},{129,257},{257,385},{3... | collective-permute-start | bytes 983048 | tf_op jit(solution)/shard_map/ppermute | solution.py:19
  85.9 2.3 %collective-permute-done.3 = bf16[128,1280]{1,0:T(8,128)(2,1)S(1)} collective-permute-done((bf16[128,1280]{1,0:T(8,128)(2,1)S(1)}, bf16[128,1280]{1,0:T(8,128)(2,1)S(1)}, u32[]{:S(2)}, u32[]{:S(2)}) %collective-permute-start.3) | collective-permute-done | bytes 327712 | tf_op jit(solution)/shard_map/ppermute | solution.py:19
  88.2 8.6 %collective-permute-done.6 = bf16[128,1280]{1,0:T(8,128)(2,1)S(1)} collective-permute-done((bf16[128,1280]{1,0:T(8,128)(2,1)S(1)}, bf16[128,1280]{1,0:T(8,128)(2,1)S(1)}, u32[]{:S(2)}, u32[]{:S(2)}) %collective-permute-start.6) | collective-permute-done | bytes 327712 | tf_op jit(solution)/shard_map/ppermute | solution.py:19
  97.6 3.4 %all-to-all-start.2 = ((bf16[8,16,1280]{2,1,0:T(8,128)(2,1)}), bf16[8,16,1280]{2,1,0:T(8,128)(2,1)S(1)}, u32[]{:S(2)}, u32[]{:S(2)}) async-start(bf16[8,16,1280]{2,1,0:T(8,128)(2,1)} %bitcast.106), calls=%async_computation.2 | async-start | bytes 655360 | tf_op jit(solution)/shard_map/all_to_all | solution.py:77
  101.8 10.5 %all-to-all-done.2 = bf16[8,16,1280]{2,1,0:T(8,128)(2,1)S(1)} async-done(((bf16[8,16,1280]{2,1,0:T(8,128)(2,1)}), bf16[8,16,1280]{2,1,0:T(8,128)(2,1)S(1)}, u32[]{:S(2)}, u32[]{:S(2)}) %all-to-all-start.2) | async-done | bytes 327712 | tf_op jit(solution)/shard_map/all_to_all | solution.py:77
  114.0 3.4 %all-to-all-start.3 = ((bf16[8,16,1280]{2,1,0:T(8,128)(2,1)}), bf16[8,16,1280]{2,1,0:T(8,128)(2,1)S(1)}, u32[]{:S(2)}, u32[]{:S(2)}) async-start(bf16[8,16,1280]{2,1,0:T(8,128)(2,1)} %broadcast_in_dim.49), calls=%async_computation.3 | async-start | bytes 655360 | tf_op jit(solution)/shard_map/all_to_all | solution.py:30
  117.4 11.1 %all-to-all-done.3 = bf16[8,16,1280]{2,1,0:T(8,128)(2,1)S(1)} async-done(((bf16[8,16,1280]{2,1,0:T(8,128)(2,1)}), bf16[8,16,1280]{2,1,0:T(8,128)(2,1)S(1)}, u32[]{:S(2)}, u32[]{:S(2)}) %all-to-all-start.3) | async-done | bytes 327712 | tf_op jit(solution)/shard_map/all_to_all | solution.py:30
  128.5 6.9 %collective-permute-start.11 = (bf16[128,1280]{1,0:T(8,128)(2,1)S(1)}, bf16[128,1280]{1,0:T(8,128)(2,1)S(1)}, u32[]{:S(2)}, u32[]{:S(2)}) collective-permute-start(bf16[128,1280]{1,0:T(8,128)(2,1)S(1)} %bitcast.93), channel_id=1, source_target_pairs={{0,128},{128,256},{256,384},{384,0},{1,129},{129,257},{257,385},{3... | collective-permute-start | bytes 983048 | tf_op jit(solution)/shard_map/ppermute | solution.py:19
  137.4 3.4 %collective-permute-start.17 = (bf16[128,1280]{1,0:T(8,128)(2,1)S(1)}, bf16[128,1280]{1,0:T(8,128)(2,1)S(1)}, u32[]{:S(2)}, u32[]{:S(2)}) collective-permute-start(bf16[128,1280]{1,0:T(8,128)(2,1)S(1)} %bitcast.95), channel_id=1, source_target_pairs={{0,256},{128,384},{256,0},{384,128},{1,257},{129,385},{257,1},{385... | collective-permute-start | bytes 983048 | tf_op jit(solution)/shard_map/ppermute | solution.py:19
  145.8 5.4 %collective-permute-done.14 = bf16[128,1280]{1,0:T(8,128)(2,1)S(1)} collective-permute-done((bf16[128,1280]{1,0:T(8,128)(2,1)S(1)}, bf16[128,1280]{1,0:T(8,128)(2,1)S(1)}, u32[]{:S(2)}, u32[]{:S(2)}) %collective-permute-start.14) | collective-permute-done | bytes 327712 | tf_op jit(solution)/shard_map/ppermute | solution.py:19
  154.0 2.4 %collective-permute-start.18 = (bf16[128,256]{1,0:T(8,128)(2,1)S(1)}, bf16[128,256]{1,0:T(8,128)(2,1)S(1)}, u32[]{:S(2)}, u32[]{:S(2)}) collective-permute-start(bf16[128,256]{1,0:T(8,128)(2,1)S(1)} %convolution_convert_fusion.9), channel_id=1, source_target_pairs={{0,1},{1,0},{2,3},{3,2},{4,5},{5,4},{6,7},{7,6},{8,9},{9,8},{10,11... | collective-permute-start | bytes 196616 | tf_op jit(solution)/shard_map/ppermute | solution.py:24
  160.6 5.1 %collective-permute-start.16 = (bf16[128,1280]{1,0:T(8,128)(2,1)S(1)}, bf16[128,1280]{1,0:T(8,128)(2,1)S(1)}, u32[]{:S(2)}, u32[]{:S(2)}) collective-permute-start(bf16[128,1280]{1,0:T(8,128)(2,1)S(1)} %fusion.11), channel_id=1, source_target_pairs={{0,128},{128,256},{256,384},{384,0},{1,129},{129,257},{257,385},{3... | collective-permute-start | bytes 983048 | tf_op jit(solution)/shard_map/ppermute | solution.py:19
  170.3 9.3 %collective-permute-done.16 = bf16[128,1280]{1,0:T(8,128)(2,1)S(1)} collective-permute-done((bf16[128,1280]{1,0:T(8,128)(2,1)S(1)}, bf16[128,1280]{1,0:T(8,128)(2,1)S(1)}, u32[]{:S(2)}, u32[]{:S(2)}) %collective-permute-start.16) | collective-permute-done | bytes 327712 | tf_op jit(solution)/shard_map/ppermute | solution.py:19
  181.0 4.6 %all-to-all-start.4 = ((bf16[64,2,1280]{2,1,0:T(2,128)(2,1)}), bf16[64,2,1280]{2,1,0:T(2,128)(2,1)S(1)}, u32[]{:S(2)}, u32[]{:S(2)}) async-start(bf16[64,2,1280]{2,1,0:T(2,128)(2,1)} %reshape.136), calls=%async_computation.4 | async-start | bytes 655360 | tf_op jit(solution)/shard_map/all_to_all | solution.py:94
  186.3 2.5 %fusion.2 = bf16[1,256,1280]{2,1,0:T(8,128)(2,1)} fusion(bf16[128,1280]{1,0:T(8,128)(2,1)} %copy-done.17, bf16[128,1280]{1,0:T(8,128)(2,1)} %copy-done.16, bf16[128,1280]{1,0:T(8,128)(2,1)S(1)} %copy-done.15, bf16[128,1280]{1,0:T(8,128)(2,1)S(1)} %bitcast.98, bf16[128,256]{1,0:T(8,128)(2,1)S(1)} %copy-done.23, bf16[128,256]{1,0:T(8,128)(2,1)S(1)} %copy-done.21, ...), kind=kOutput, calls=%fused_computation.10 | convolution fusion | flops 342163456 | bytes 2228224 | tf_op jit(solution)/shard_map/dot_general | solution.py:103
  191.7 8.8 %all-to-all-done.4 = bf16[64,2,1280]{2,1,0:T(2,128)(2,1)S(1)} async-done(((bf16[64,2,1280]{2,1,0:T(2,128)(2,1)}), bf16[64,2,1280]{2,1,0:T(2,128)(2,1)S(1)}, u32[]{:S(2)}, u32[]{:S(2)}) %all-to-all-start.4) | async-done | bytes 327712 | tf_op jit(solution)/shard_map/all_to_all | solution.py:94
  (176 shorter events, 47.6 us)
Async XLA Ops:
  0.6 74.2 %copy-start = (bf16[1,256,1280]{2,1,0:T(8,128)(2,1)S(1)}, bf16[1,256,1280]{2,1,0:T(8,128)(2,1)}, u32[]{:S(2)}) copy-start(bf16[1,256,1280]{2,1,0:T(8,128)(2,1)} %param.13) | copy-start | bytes 1966084
  44.6 11.1 %collective-permute-start = (bf16[128,512]{1,0:T(8,128)(2,1)S(1)}, bf16[128,512]{1,0:T(8,128)(2,1)S(1)}, u32[]{:S(2)}, u32[]{:S(2)}) collective-permute-start(bf16[128,512]{1,0:T(8,128)(2,1)S(1)} %pad_maximum_fusion.3), channel_id=1, source_target_pairs={{0,1},{1,0},{2,3},{3,2},{4,5},{5,4},{6,7},{7,6},{8,9},{9,8},{10,11... | collective-permute-start | bytes 393224 | tf_op jit(solution)/shard_map/ppermute | solution.py:24
  46.5 12.4 %collective-permute-start.1 = (bf16[128,1280]{1,0:T(8,128)(2,1)S(1)}, bf16[128,1280]{1,0:T(8,128)(2,1)S(1)}, u32[]{:S(2)}, u32[]{:S(2)}) collective-permute-start(bf16[128,1280]{1,0:T(8,128)(2,1)S(1)} %bitcast.101), channel_id=1, source_target_pairs={{0,128},{128,256},{256,384},{384,0},{1,129},{129,257},{257,385},{3... | collective-permute-start | bytes 983048 | tf_op jit(solution)/shard_map/ppermute | solution.py:19
  48.9 20.0 %collective-permute-start.4 = (bf16[128,1280]{1,0:T(8,128)(2,1)S(1)}, bf16[128,1280]{1,0:T(8,128)(2,1)S(1)}, u32[]{:S(2)}, u32[]{:S(2)}) collective-permute-start(bf16[128,1280]{1,0:T(8,128)(2,1)S(1)} %bitcast.102), channel_id=1, source_target_pairs={{0,384},{128,0},{256,128},{384,256},{1,385},{129,1},{257,129},{385... | collective-permute-start | bytes 983048 | tf_op jit(solution)/shard_map/ppermute | solution.py:19
  52.4 19.2 %collective-permute-start.7 = (bf16[128,1280]{1,0:T(8,128)(2,1)S(1)}, bf16[128,1280]{1,0:T(8,128)(2,1)S(1)}, u32[]{:S(2)}, u32[]{:S(2)}) collective-permute-start(bf16[128,1280]{1,0:T(8,128)(2,1)S(1)} %bitcast.103), channel_id=1, source_target_pairs={{0,256},{128,384},{256,0},{384,128},{1,257},{129,385},{257,1},{385... | collective-permute-start | bytes 983048 | tf_op jit(solution)/shard_map/ppermute | solution.py:19
  59.7 15.0 %collective-permute-start.2 = (bf16[128,512]{1,0:T(8,128)(2,1)S(1)}, bf16[128,512]{1,0:T(8,128)(2,1)S(1)}, u32[]{:S(2)}, u32[]{:S(2)}) collective-permute-start(bf16[128,512]{1,0:T(8,128)(2,1)S(1)} %pad_maximum_fusion.4), channel_id=1, source_target_pairs={{0,1},{1,0},{2,3},{3,2},{4,5},{5,4},{6,7},{7,6},{8,9},{9,8},{10,11... | collective-permute-start | bytes 393224 | tf_op jit(solution)/shard_map/ppermute | solution.py:24
  69.6 7.8 %collective-permute-start.5 = (bf16[128,512]{1,0:T(8,128)(2,1)S(1)}, bf16[128,512]{1,0:T(8,128)(2,1)S(1)}, u32[]{:S(2)}, u32[]{:S(2)}) collective-permute-start(bf16[128,512]{1,0:T(8,128)(2,1)S(1)} %pad_maximum_fusion.5), channel_id=1, source_target_pairs={{0,1},{1,0},{2,3},{3,2},{4,5},{5,4},{6,7},{7,6},{8,9},{9,8},{10,11... | collective-permute-start | bytes 393224 | tf_op jit(solution)/shard_map/ppermute | solution.py:24
  72.3 10.6 %collective-permute-start.8 = (bf16[128,512]{1,0:T(8,128)(2,1)S(1)}, bf16[128,512]{1,0:T(8,128)(2,1)S(1)}, u32[]{:S(2)}, u32[]{:S(2)}) collective-permute-start(bf16[128,512]{1,0:T(8,128)(2,1)S(1)} %pad_maximum_fusion.6), channel_id=1, source_target_pairs={{0,1},{1,0},{2,3},{3,2},{4,5},{5,4},{6,7},{7,6},{8,9},{9,8},{10,11... | collective-permute-start | bytes 393224 | tf_op jit(solution)/shard_map/ppermute | solution.py:24
  75.5 12.7 %collective-permute-start.3 = (bf16[128,1280]{1,0:T(8,128)(2,1)S(1)}, bf16[128,1280]{1,0:T(8,128)(2,1)S(1)}, u32[]{:S(2)}, u32[]{:S(2)}) collective-permute-start(bf16[128,1280]{1,0:T(8,128)(2,1)S(1)} %convolution_convert_fusion.5), channel_id=1, source_target_pairs={{0,384},{128,0},{256,128},{384,256},{1,385},{129,1},{257,129},{385... | collective-permute-start | bytes 983048 | tf_op jit(solution)/shard_map/ppermute | solution.py:19
  77.8 19.0 %collective-permute-start.6 = (bf16[128,1280]{1,0:T(8,128)(2,1)S(1)}, bf16[128,1280]{1,0:T(8,128)(2,1)S(1)}, u32[]{:S(2)}, u32[]{:S(2)}) collective-permute-start(bf16[128,1280]{1,0:T(8,128)(2,1)S(1)} %convolution_convert_fusion.4), channel_id=1, source_target_pairs={{0,128},{128,256},{256,384},{384,0},{1,129},{129,257},{257,385},{3... | collective-permute-start | bytes 983048 | tf_op jit(solution)/shard_map/ppermute | solution.py:19
  83.3 13.5 %collective-permute-start.9 = (bf16[128,1280]{1,0:T(8,128)(2,1)S(1)}, bf16[128,1280]{1,0:T(8,128)(2,1)S(1)}, u32[]{:S(2)}, u32[]{:S(2)}) collective-permute-start(bf16[128,1280]{1,0:T(8,128)(2,1)S(1)} %convolution_convert_fusion.3), channel_id=1, source_target_pairs={{0,256},{128,384},{256,0},{384,128},{1,257},{129,385},{257,1},{385... | collective-permute-start | bytes 983048 | tf_op jit(solution)/shard_map/ppermute | solution.py:19
  97.6 14.6 %all-to-all-start.2 = ((bf16[8,16,1280]{2,1,0:T(8,128)(2,1)}), bf16[8,16,1280]{2,1,0:T(8,128)(2,1)S(1)}, u32[]{:S(2)}, u32[]{:S(2)}) async-start(bf16[8,16,1280]{2,1,0:T(8,128)(2,1)} %bitcast.106), calls=%async_computation.2 | async-start | bytes 655360 | tf_op jit(solution)/shard_map/all_to_all | solution.py:77
  114.0 14.5 %all-to-all-start.3 = ((bf16[8,16,1280]{2,1,0:T(8,128)(2,1)}), bf16[8,16,1280]{2,1,0:T(8,128)(2,1)S(1)}, u32[]{:S(2)}, u32[]{:S(2)}) async-start(bf16[8,16,1280]{2,1,0:T(8,128)(2,1)} %broadcast_in_dim.49), calls=%async_computation.3 | async-start | bytes 655360 | tf_op jit(solution)/shard_map/all_to_all | solution.py:30
  128.5 15.0 %collective-permute-start.11 = (bf16[128,1280]{1,0:T(8,128)(2,1)S(1)}, bf16[128,1280]{1,0:T(8,128)(2,1)S(1)}, u32[]{:S(2)}, u32[]{:S(2)}) collective-permute-start(bf16[128,1280]{1,0:T(8,128)(2,1)S(1)} %bitcast.93), channel_id=1, source_target_pairs={{0,128},{128,256},{256,384},{384,0},{1,129},{129,257},{257,385},{3... | collective-permute-start | bytes 983048 | tf_op jit(solution)/shard_map/ppermute | solution.py:19
  135.4 15.8 %collective-permute-start.14 = (bf16[128,1280]{1,0:T(8,128)(2,1)S(1)}, bf16[128,1280]{1,0:T(8,128)(2,1)S(1)}, u32[]{:S(2)}, u32[]{:S(2)}) collective-permute-start(bf16[128,1280]{1,0:T(8,128)(2,1)S(1)} %bitcast.94), channel_id=1, source_target_pairs={{0,384},{128,0},{256,128},{384,256},{1,385},{129,1},{257,129},{385... | collective-permute-start | bytes 983048 | tf_op jit(solution)/shard_map/ppermute | solution.py:19
  137.4 16.3 %collective-permute-start.17 = (bf16[128,1280]{1,0:T(8,128)(2,1)S(1)}, bf16[128,1280]{1,0:T(8,128)(2,1)S(1)}, u32[]{:S(2)}, u32[]{:S(2)}) collective-permute-start(bf16[128,1280]{1,0:T(8,128)(2,1)S(1)} %bitcast.95), channel_id=1, source_target_pairs={{0,256},{128,384},{256,0},{384,128},{1,257},{129,385},{257,1},{385... | collective-permute-start | bytes 983048 | tf_op jit(solution)/shard_map/ppermute | solution.py:19
  141.1 27.7 %collective-permute-start.10 = (bf16[128,256]{1,0:T(8,128)(2,1)S(1)}, bf16[128,256]{1,0:T(8,128)(2,1)S(1)}, u32[]{:S(2)}, u32[]{:S(2)}) collective-permute-start(bf16[128,256]{1,0:T(8,128)(2,1)S(1)} %convolution_convert_fusion.12), channel_id=1, source_target_pairs={{0,1},{1,0},{2,3},{3,2},{4,5},{5,4},{6,7},{7,6},{8,9},{9,8},{10,11... | collective-permute-start | bytes 196616 | tf_op jit(solution)/shard_map/ppermute | solution.py:24
  143.9 12.6 %collective-permute-start.12 = (bf16[128,256]{1,0:T(8,128)(2,1)S(1)}, bf16[128,256]{1,0:T(8,128)(2,1)S(1)}, u32[]{:S(2)}, u32[]{:S(2)}) collective-permute-start(bf16[128,256]{1,0:T(8,128)(2,1)S(1)} %convolution_convert_fusion.11), channel_id=1, source_target_pairs={{0,1},{1,0},{2,3},{3,2},{4,5},{5,4},{6,7},{7,6},{8,9},{9,8},{10,11... | collective-permute-start | bytes 196616 | tf_op jit(solution)/shard_map/ppermute | solution.py:24
  151.6 7.9 %collective-permute-start.15 = (bf16[128,256]{1,0:T(8,128)(2,1)S(1)}, bf16[128,256]{1,0:T(8,128)(2,1)S(1)}, u32[]{:S(2)}, u32[]{:S(2)}) collective-permute-start(bf16[128,256]{1,0:T(8,128)(2,1)S(1)} %convolution_convert_fusion.10), channel_id=1, source_target_pairs={{0,1},{1,0},{2,3},{3,2},{4,5},{5,4},{6,7},{7,6},{8,9},{9,8},{10,11... | collective-permute-start | bytes 196616 | tf_op jit(solution)/shard_map/ppermute | solution.py:24
  154.0 11.7 %collective-permute-start.18 = (bf16[128,256]{1,0:T(8,128)(2,1)S(1)}, bf16[128,256]{1,0:T(8,128)(2,1)S(1)}, u32[]{:S(2)}, u32[]{:S(2)}) collective-permute-start(bf16[128,256]{1,0:T(8,128)(2,1)S(1)} %convolution_convert_fusion.9), channel_id=1, source_target_pairs={{0,1},{1,0},{2,3},{3,2},{4,5},{5,4},{6,7},{7,6},{8,9},{9,8},{10,11... | collective-permute-start | bytes 196616 | tf_op jit(solution)/shard_map/ppermute | solution.py:24
  157.6 12.7 %collective-permute-start.13 = (bf16[128,1280]{1,0:T(8,128)(2,1)S(1)}, bf16[128,1280]{1,0:T(8,128)(2,1)S(1)}, u32[]{:S(2)}, u32[]{:S(2)}) collective-permute-start(bf16[128,1280]{1,0:T(8,128)(2,1)S(1)} %fusion.10), channel_id=1, source_target_pairs={{0,384},{128,0},{256,128},{384,256},{1,385},{129,1},{257,129},{385... | collective-permute-start | bytes 983048 | tf_op jit(solution)/shard_map/ppermute | solution.py:19
  160.6 19.0 %collective-permute-start.16 = (bf16[128,1280]{1,0:T(8,128)(2,1)S(1)}, bf16[128,1280]{1,0:T(8,128)(2,1)S(1)}, u32[]{:S(2)}, u32[]{:S(2)}) collective-permute-start(bf16[128,1280]{1,0:T(8,128)(2,1)S(1)} %fusion.11), channel_id=1, source_target_pairs={{0,128},{128,256},{256,384},{384,0},{1,129},{129,257},{257,385},{3... | collective-permute-start | bytes 983048 | tf_op jit(solution)/shard_map/ppermute | solution.py:19
  166.9 12.7 %collective-permute-start.19 = (bf16[128,1280]{1,0:T(8,128)(2,1)S(1)}, bf16[128,1280]{1,0:T(8,128)(2,1)S(1)}, u32[]{:S(2)}, u32[]{:S(2)}) collective-permute-start(bf16[128,1280]{1,0:T(8,128)(2,1)S(1)} %fusion.12), channel_id=1, source_target_pairs={{0,256},{128,384},{256,0},{384,128},{1,257},{129,385},{257,1},{385... | collective-permute-start | bytes 983048 | tf_op jit(solution)/shard_map/ppermute | solution.py:19
  181.0 19.6 %all-to-all-start.4 = ((bf16[64,2,1280]{2,1,0:T(2,128)(2,1)}), bf16[64,2,1280]{2,1,0:T(2,128)(2,1)S(1)}, u32[]{:S(2)}, u32[]{:S(2)}) async-start(bf16[64,2,1280]{2,1,0:T(2,128)(2,1)} %reshape.136), calls=%async_computation.4 | async-start | bytes 655360 | tf_op jit(solution)/shard_map/all_to_all | solution.py:94
  (37 other events, 132.0 us)

commit v2 on v1

v2 whole, which is shorter than its diff:
```python
import jax
import jax.numpy as jnp
from jax import lax
from jax.experimental import pallas as pl
from jax.experimental.pallas import tpu as pltpu
from jax.sharding import Mesh, PartitionSpec as P

CAP = 2
NX, NY, NZ = 4, 8, 8
F32, BF16 = jnp.float32, jnp.bfloat16
CONTRACT_ROWS = (((0,), (0,)), ((), ()))
CONTRACT_COLS = (((1,), (1,)), ((), ()))
SWAP = [(0, 1), (1, 0)]
PAIR = [(0, 1), (1, 0), (2, 3), (3, 2)]
CROSS = [(0, 3), (3, 0), (1, 2), (2, 1)]


def silu_slope(gate_val):
    sig = jax.nn.sigmoid(gate_val)
    return sig * (1.0 + gate_val * (1.0 - sig))


def iota(shape, dim):
    return lax.broadcasted_iota(jnp.int32, shape, dim)


def one_hot(mask):
    return jnp.where(mask, 1.0, 0.0).astype(BF16)


def slot_matrix(ids, lengths, count, per_expert):
    tokens = ids.shape[1]
    slot = iota((count, tokens), 0)
    mine = ids == slot // per_expert
    before = iota((tokens, tokens), 0) < iota((tokens, tokens), 1)
    rank = jnp.dot(one_hot(mine), one_hot(before), preferred_element_type=F32)
    live = iota((count, tokens), 1) < jnp.sum(lengths, axis=1, keepdims=True)
    return mine & live & (rank == (slot % CAP).astype(F32))


def dispatch_kernel(ids_ref, lengths_ref, tokens_ref, target_ref, out_ref):
    experts, lines, half = out_ref.shape
    chosen = slot_matrix(ids_ref[...], lengths_ref[...], experts * lines, lines)
    line = iota(chosen.shape, 0) % lines
    from_target = line % (2 * CAP) >= CAP
    pick_tokens, pick_target = one_hot(chosen & ~from_target), one_hot(chosen & from_target)

    def moved(cols):
        out = jnp.dot(pick_tokens, tokens_ref[:, cols], preferred_element_type=F32)
        return out + jnp.dot(pick_target, target_ref[:, cols], preferred_element_type=F32)

    first = iota((experts * lines, half), 0) % lines < 2 * CAP
    both = jnp.where(first, moved(slice(0, half)), moved(slice(half, 2 * half)))
    out_ref[...] = both.reshape(experts, lines, half).astype(BF16)


def arrive_kernel(arrived_ref, blocks_ref, rows_ref, target_ref):
    experts, lines, half = arrived_ref.shape
    count = rows_ref.shape[0]
    arrived = arrived_ref[...].astype(F32).reshape(experts * lines, half).astype(BF16)
    row, line = iota((count, experts * lines), 0), iota((count, experts * lines), 1)

    def rows(offset):
        parts = []
        for start in (offset, offset + 2 * CAP):
            pick = one_hot(line == row // CAP * lines + row % CAP + start)
            parts.append(jnp.dot(pick, arrived, preferred_element_type=F32).astype(BF16))
        return jnp.concatenate(parts, axis=1)

    mine = rows(0)
    rows_ref[...] = mine
    target_ref[...] = rows(CAP)
    blocks_ref[...] = jnp.broadcast_to(mine[None], blocks_ref.shape)


def settle_kernel(pieces_ref, rows_ref, target_ref, blocks_ref):
    total = pieces_ref[0].astype(F32)
    for i in range(1, pieces_ref.shape[0]):
        total += pieces_ref[i].astype(F32)
    output = rows_ref[...].astype(F32) + total.astype(BF16).astype(F32)
    residual = (output - target_ref[...].astype(F32)).astype(BF16)
    blocks_ref[...] = jnp.broadcast_to(residual[None], blocks_ref.shape)


def combine_kernel(ids_ref, lengths_ref, tokens_ref, target_ref, pieces_ref, out_ref):
    row_len = tokens_ref.shape[0]
    count = pieces_ref.shape[1]
    chosen = one_hot(slot_matrix(ids_ref[...], lengths_ref[...], count, CAP))
    slots = pieces_ref[0].astype(F32)
    for i in range(1, pieces_ref.shape[0]):
        slots += pieces_ref[i].astype(F32)
    routed = lax.dot_general(chosen, slots.astype(BF16), CONTRACT_ROWS, preferred_element_type=F32)
    taken = lax.dot_general(chosen, jnp.ones((count, 128), BF16), CONTRACT_ROWS, preferred_element_type=F32)[:, :1]
    live = iota((row_len, 1), 0) < jnp.sum(lengths_ref[...], axis=1, keepdims=True)
    own = tokens_ref[...].astype(F32) - target_ref[...].astype(F32)
    out_ref[...] = (jnp.where(live & (taken == 0.0), own, 0.0) + routed).astype(BF16)


def array(*shape, dtype=BF16):
    return jax.ShapeDtypeStruct(shape, dtype)


def swap(value):
    return lax.ppermute(value, "c", SWAP)


def pair(value):
    return lax.ppermute(value, "x", PAIR)


def cross(value):
    return lax.ppermute(value, "x", CROSS)


def after(value, early):
    return lax.optimization_barrier((value, early))


def over_y(blocks):
    return lax.all_to_all(blocks, "y", 0, 0, tiled=True)


def times(left, right):
    return jnp.dot(left, right, preferred_element_type=F32)


def times_t(left, right):
    return lax.dot_general(left, right, CONTRACT_COLS, preferred_element_type=F32)


def stack(*parts):
    return jnp.concatenate(parts, axis=0)


def beside(*parts):
    return jnp.concatenate(parts, axis=1)


def weight_grad(left, right):
    return lax.dot_general(left, right, CONTRACT_ROWS, preferred_element_type=F32).astype(BF16)


def local(tokens, target, expert_ids, doc_lengths, w_gate, w_up, w_down):
    row_len, features = tokens.shape
    slot_count = NZ * CAP
    column_rows = NY * slot_count
    gate_w, up_w, down_w = w_gate[0], w_up[0], w_down[0]
    units = gate_w.shape[1]
    ids = expert_ids.reshape(1, row_len)

    message = pl.pallas_call(dispatch_kernel, out_shape=array(NZ, 4 * CAP, features // 2))(
        ids, doc_lengths, tokens, target
    )
    arrived = lax.all_to_all(message, "z", 0, 0, tiled=True)
    blocks, my_rows, my_target = pl.pallas_call(
        arrive_kernel,
        out_shape=(array(NY, slot_count, features), array(slot_count, features), array(slot_count, features)),
    )(arrived)

    blocks, gate_w_p = after(blocks, pair(gate_w))
    column = over_y(blocks).reshape(column_rows, features)
    column, up_w_p = after(column, pair(up_w))

    def products(rows):
        return beside(*[times(rows, w).astype(BF16) for w in (gate_w, up_w, gate_w_p, up_w_p)])

    crossed = cross(column)
    part = stack(products(column), products(crossed))
    part, down_w_p = after(part, pair(down_w))
    sums = part.astype(F32) + swap(part).astype(F32)
    gate, up, gate_p, up_p = jnp.split(sums, 4, axis=1)
    hidden = (jax.nn.silu(gate) * up).astype(BF16)
    hidden_p = (jax.nn.silu(gate_p) * up_p).astype(BF16)

    def column_sum(product):
        theirs = cross(product(slice(column_rows, None)).astype(BF16))
        return product(slice(0, column_rows)) + theirs.astype(F32)

    column_out = column_sum(lambda s: times(hidden[s], down_w) + times(hidden_p[s], down_w_p)).astype(BF16)
    column_out, pair_column = after(column_out, pair(column))
    pieces = over_y(column_out.reshape(NY, slot_count, features))
    blocks = pl.pallas_call(settle_kernel, out_shape=array(NY, slot_count, features))(pieces, my_rows, my_target)
    blocks, pair_crossed = after(blocks, pair(crossed))

    grad_column = over_y(blocks).reshape(column_rows, features)
    grad_column, pair_hidden = after(grad_column, pair(hidden_p))
    grad_crossed = cross(grad_column)
    part = stack(
        *[beside(*[times_t(g, w).astype(BF16) for w in (down_w, down_w_p)]) for g in (grad_column, grad_crossed)]
    )
    part, pair_grad_column = after(part, pair(grad_column))
    sums = part.astype(F32) + swap(part).astype(F32)
    back, back_p = jnp.split(sums, 2, axis=1)
    gate_grad = (back * up * silu_slope(gate)).astype(BF16)
    up_grad = (back * jax.nn.silu(gate)).astype(BF16)
    gate_grad_p = (back_p * up_p * silu_slope(gate_p)).astype(BF16)
    up_grad_p = (back_p * jax.nn.silu(gate_p)).astype(BF16)

    def input_part(s):
        own = times_t(gate_grad[s], gate_w) + times_t(up_grad[s], up_w)
        return own + times_t(gate_grad_p[s], gate_w_p) + times_t(up_grad_p[s], up_w_p)

    mine = (jnp.arange(column_rows) // slot_count) == lax.axis_index("y")
    column_in = column_sum(input_part) + jnp.where(mine[:, None], grad_column.astype(F32), 0.0)
    column_in, pair_grad_crossed = after(column_in.astype(BF16), pair(grad_crossed))
    pair_in = pair(beside(gate_grad_p, up_grad_p))
    pieces = lax.all_to_all(column_in.reshape(NY * NZ, CAP, features), ("y", "z"), 0, 0, tiled=True)
    grad_tokens = pl.pallas_call(combine_kernel, out_shape=array(row_len, features))(
        ids, doc_lengths, tokens, target, pieces.reshape(NY, slot_count, features)
    )

    rows = stack(column, crossed, pair_column, pair_crossed)
    grads = stack(grad_column, grad_crossed, pair_grad_column, pair_grad_crossed)
    grad_down = weight_grad(stack(hidden, pair_hidden), grads)
    grad_gate = weight_grad(rows, stack(gate_grad, pair_in[:, :units]))
    grad_up = weight_grad(rows, stack(up_grad, pair_in[:, units:]))
    return (grad_tokens, grad_gate[None], grad_up[None], grad_down[None])


def solution(mesh):
    cube = Mesh(mesh.devices.reshape(NX, NY, NZ, 2), ("x", "y", "z", "c"))
    token_spec = P(("x", "y", "z"), "c")
    in_spec, out_spec = P("z", "c", ("x", "y")), P("z", ("x", "y"), "c")
    return jax.shard_map(
        local,
        mesh=cube,
        in_specs=(token_spec, token_spec, P(("x", "y", "z")), P(("x", "y", "z"), None), in_spec, in_spec, out_spec),
        out_specs=(token_spec, in_spec, in_spec, out_spec),
        check_vma=False,
    )
```

time: 206 us -> 178 us (0.86); the launches traced: 202 us -> 177 us
  blocking collectives: 37.7 us -> 0 us
  Pallas kernels: 0 us -> 8.2 us
  other arithmetic: 6.4 us -> 0.79 us
  starting transfers between devices: 67.3 us -> 71.9 us
  matrix products: 15.1 us -> 18.8 us
  local copies, waits for them, and re-layouts: 6.02 us -> 8.6 us
    all_to_all x2 -> x0, blocking collectives: 37.7 us -> none  [the longest x1 19 us: spread(): lax.all_to_all(blocks, 'y', 0, 0, tiled=True)]
    all_to_all x3 -> x5, starting transfers between devices: 11.5 us -> 31.7 us  [the longest x3 15.3 us: over_y(): return lax.all_to_all(blocks, 'y', 0, 0, tiled=True)]
    ppermute x20 -> x15, starting transfers between devices: 55.8 us -> 40.3 us  [the longest x9 23.2 us: pair(): return lax.ppermute(value, 'x', PAIR)]
    pallas_call x0 -> x4, Pallas kernels: none -> 8.2 us  [the longest x1 2.45 us: local(): pl.pallas_call(combine_kernel, out_shape=array(row_len, features))]
    ppermute x20 -> x15, waiting for transfers between devices: 37.3 us -> 29.2 us  [the longest x4 20.1 us: cross(): return lax.ppermute(value, 'x', CROSS)]
    all_to_all x3 -> x5, waiting for transfers between devices: 30.3 us -> 37.9 us  [the longest x3 23.2 us: over_y(): return lax.all_to_all(blocks, 'y', 0, 0, tiled=True)]
    convert_element_type x11 -> x2, other arithmetic: 3.12 us -> 0.44 us  [the longest x1 0.29 us: local(): gate_grad_p = (back_p * up_p * silu_slope(gate_p)).astype(BF16)]
    dot_general x27 -> x24, matrix products: 9.83 us -> 12.3 us  [the longest x12 7.35 us: times_t(): lax.dot_general(left, right, CONTRACT_COLS, preferred_element_type=F32)]
  transfers between devices with their start and end apart: 23 -> 20, of which waited for: 11 -> 13; matrix products, arithmetic and copies ran while one was open for 7% -> 13% of each run, Pallas kernels for 0% -> 3%
where the time goes in v2:
time: 178 us; the launch traced here: 177 us
  starting transfers between devices  71.9 us (40%)
  waiting for transfers between devices  67.1 us (38%)
  matrix products  18.8 us (11%)
  local copies, waits for them, and re-layouts  8.6 us (5%)
  Pallas kernels  8.2 us (5%)
    all_to_all x3, waiting for transfers between devices, over_y(): return lax.all_to_all(blocks, 'y', 0, 0, tiled=True)  23.2 us
    ppermute x9, starting transfers between devices, pair(): return lax.ppermute(value, 'x', PAIR)  23.2 us
    ppermute x4, waiting for transfers between devices, cross(): return lax.ppermute(value, 'x', CROSS)  20.1 us
    all_to_all x3, starting transfers between devices, over_y(): return lax.all_to_all(blocks, 'y', 0, 0, tiled=True)  15.3 us
    ppermute x4, starting transfers between devices, cross(): return lax.ppermute(value, 'x', CROSS)  13.3 us
    all_to_all x1, starting transfers between devices, local(): arrived = lax.all_to_all(message, 'z', 0, 0, tiled=True)  10.3 us
    all_to_all x1, waiting for transfers between devices, local(): lax.all_to_all(column_in.reshape(NY * NZ, CAP, features), ('y', 'z'), 0,...  9.24 us
    dot_general x12, matrix products, times_t(): lax.dot_general(left, right, CONTRACT_COLS, preferred_element_type=F32)  7.35 us
  transfers between devices with their start and end apart: 20, of which 13 were waited for; matrix products, arithmetic and copies ran while one was open for 13% of the time, Pallas kernels for 3%

profile of v2, /device:TPU:6, one launch (start us, length us, event | category | flops | bytes accessed | tf_op | source)
XLA Modules:
  0.0 176.5 jit_solution(12194350425383492511)
XLA Ops:
  0.6 2.9 %collective-permute-start = (bf16[1280,256]{1,0:T(8,128)(2,1)}, bf16[1280,256]{1,0:T(8,128)(2,1)S(1)}, u32[]{:S(2)}, u32[]{:S(2)}) collective-permute-start(bf16[1280,256]{1,0:T(8,128)(2,1)} %bitcast.71), channel_id=1, source_target_pairs={{0,128},{128,0},{256,384},{384,256},{1,129},{129,1},{257,385},{385... | collective-permute-start | bytes 1966088 | tf_op jit(solution)/shard_map/ppermute | solution.py:108
  5.7 10.3 %all-to-all-start = ((bf16[8,8,640]{2,1,0:T(8,128)(2,1)}), bf16[8,8,640]{2,1,0:T(8,128)(2,1)S(1)}, u32[]{:S(2)}, u32[]{:S(2)}) async-start(bf16[8,8,640]{2,1,0:T(8,128)(2,1)} %shard_map.102), calls=%async_computation | async-start | bytes 163840 | tf_op jit(solution)/shard_map/all_to_all | solution.py:154
  16.0 3.1 %collective-permute-start.1 = (bf16[1280,256]{1,0:T(8,128)(2,1)}, bf16[1280,256]{1,0:T(8,128)(2,1)S(1)}, u32[]{:S(2)}, u32[]{:S(2)}) collective-permute-start(bf16[1280,256]{1,0:T(8,128)(2,1)} %bitcast.72), channel_id=1, source_target_pairs={{0,128},{128,0},{256,384},{384,256},{1,129},{129,1},{257,385},{385... | collective-permute-start | bytes 1966088 | tf_op jit(solution)/shard_map/ppermute | solution.py:108
  19.1 5.5 %all-to-all-done.arrived_ref = bf16[8,8,640]{2,1,0:T(8,128)(2,1)S(1)} async-done(((bf16[8,8,640]{2,1,0:T(8,128)(2,1)}), bf16[8,8,640]{2,1,0:T(8,128)(2,1)S(1)}, u32[]{:S(2)}, u32[]{:S(2)}) %all-to-all-start) | async-done | bytes 81952 | tf_op jit(solution)/shard_map/all_to_all | solution.py:154
  27.0 7.1 %all-to-all-start.1 = ((bf16[8,16,1280]{2,1,0:T(8,128)(2,1)}), bf16[8,16,1280]{2,1,0:T(8,128)(2,1)S(1)}, u32[]{:S(2)}, u32[]{:S(2)}) async-start(bf16[8,16,1280]{2,1,0:T(8,128)(2,1)} %get-tuple-element.24), calls=%async_computation.1 | async-start | bytes 655360 | tf_op jit(solution)/shard_map/all_to_all | solution.py:120
  34.1 3.1 %collective-permute-start.3 = (bf16[256,1280]{1,0:T(8,128)(2,1)S(1)}, bf16[256,1280]{1,0:T(8,128)(2,1)S(1)}, u32[]{:S(2)}, u32[]{:S(2)}) collective-permute-start(bf16[256,1280]{1,0:T(8,128)(2,1)S(1)} %bitcast.70), channel_id=1, source_target_pairs={{0,128},{128,0},{256,384},{384,256},{1,129},{129,1},{257,385},{385... | collective-permute-start | bytes 1966088 | tf_op jit(solution)/shard_map/ppermute | solution.py:108
  37.2 8.4 %all-to-all-done.1 = bf16[8,16,1280]{2,1,0:T(8,128)(2,1)S(1)} async-done(((bf16[8,16,1280]{2,1,0:T(8,128)(2,1)}), bf16[8,16,1280]{2,1,0:T(8,128)(2,1)S(1)}, u32[]{:S(2)}, u32[]{:S(2)}) %all-to-all-start.1) | async-done | bytes 327712 | tf_op jit(solution)/shard_map/all_to_all | solution.py:120
  45.7 3.2 %collective-permute-start.2 = (bf16[128,1280]{1,0:T(8,128)(2,1)S(1)}, bf16[128,1280]{1,0:T(8,128)(2,1)S(1)}, u32[]{:S(2)}, u32[]{:S(2)}) collective-permute-start(bf16[128,1280]{1,0:T(8,128)(2,1)S(1)} %bitcast.63), channel_id=1, source_target_pairs={{0,384},{384,0},{128,256},{256,128},{1,385},{385,1},{129,257},{257... | collective-permute-start | bytes 983048 | tf_op jit(solution)/shard_map/ppermute | solution.py:112
  51.0 5.0 %collective-permute-done.2 = bf16[128,1280]{1,0:T(8,128)(2,1)S(1)} collective-permute-done((bf16[128,1280]{1,0:T(8,128)(2,1)S(1)}, bf16[128,1280]{1,0:T(8,128)(2,1)S(1)}, u32[]{:S(2)}, u32[]{:S(2)}) %collective-permute-start.2) | collective-permute-done | bytes 327712 | tf_op jit(solution)/shard_map/ppermute | solution.py:112
  62.9 3.0 %collective-permute-start.5 = (bf16[128,1280]{1,0:T(8,128)(2,1)S(1)}, bf16[128,1280]{1,0:T(8,128)(2,1)S(1)}, u32[]{:S(2)}, u32[]{:S(2)}) collective-permute-start(bf16[128,1280]{1,0:T(8,128)(2,1)S(1)} %fusion.9), channel_id=1, source_target_pairs={{0,384},{384,0},{128,256},{256,128},{1,385},{385,1},{129,257},{257... | collective-permute-start | bytes 983048 | tf_op jit(solution)/shard_map/ppermute | solution.py:112
  68.2 7.6 %collective-permute-done.5 = bf16[128,1280]{1,0:T(8,128)(2,1)S(1)} collective-permute-done((bf16[128,1280]{1,0:T(8,128)(2,1)S(1)}, bf16[128,1280]{1,0:T(8,128)(2,1)S(1)}, u32[]{:S(2)}, u32[]{:S(2)}) %collective-permute-start.5) | collective-permute-done | bytes 327712 | tf_op jit(solution)/shard_map/ppermute | solution.py:112
  78.1 4.1 %all-to-all-start.2 = ((bf16[8,16,1280]{2,1,0:T(8,128)(2,1)}), bf16[8,16,1280]{2,1,0:T(8,128)(2,1)}, u32[]{:S(2)}, u32[]{:S(2)}) async-start(bf16[8,16,1280]{2,1,0:T(8,128)(2,1)} %bitcast.73), calls=%async_computation.2 | async-start | bytes 655360 | tf_op jit(solution)/shard_map/all_to_all | solution.py:120
  84.4 10.5 %all-to-all-done.2.pieces_ref = bf16[8,16,1280]{2,1,0:T(8,128)(2,1)} async-done(((bf16[8,16,1280]{2,1,0:T(8,128)(2,1)}), bf16[8,16,1280]{2,1,0:T(8,128)(2,1)}, u32[]{:S(2)}, u32[]{:S(2)}) %all-to-all-start.2) | async-done | bytes 327712 | tf_op jit(solution)/shard_map/all_to_all | solution.py:120
  96.6 4.1 %all-to-all-start.3 = ((bf16[8,16,1280]{2,1,0:T(8,128)(2,1)}), bf16[8,16,1280]{2,1,0:T(8,128)(2,1)}, u32[]{:S(2)}, u32[]{:S(2)}) async-start(bf16[8,16,1280]{2,1,0:T(8,128)(2,1)} %shard_map.104), calls=%async_computation.3 | async-start | bytes 655360 | tf_op jit(solution)/shard_map/all_to_all | solution.py:120
  104.4 3.2 %collective-permute-done.8 = bf16[256,256]{1,0:T(8,128)(2,1)S(1)} collective-permute-done((bf16[256,256]{1,0:T(8,128)(2,1)S(1)}, bf16[256,256]{1,0:T(8,128)(2,1)S(1)}, u32[]{:S(2)}, u32[]{:S(2)}) %collective-permute-start.8) | collective-permute-done | bytes 131104 | tf_op jit(solution)/shard_map/ppermute | solution.py:108
  107.6 4.3 %all-to-all-done.3 = bf16[8,16,1280]{2,1,0:T(8,128)(2,1)} async-done(((bf16[8,16,1280]{2,1,0:T(8,128)(2,1)}), bf16[8,16,1280]{2,1,0:T(8,128)(2,1)}, u32[]{:S(2)}, u32[]{:S(2)}) %all-to-all-start.3) | async-done | bytes 327712 | tf_op jit(solution)/shard_map/all_to_all | solution.py:120
  111.9 4.0 %collective-permute-start.9 = (bf16[128,1280]{1,0:T(8,128)(2,1)}, bf16[128,1280]{1,0:T(8,128)(2,1)S(1)}, u32[]{:S(2)}, u32[]{:S(2)}) collective-permute-start(bf16[128,1280]{1,0:T(8,128)(2,1)} %bitcast.6), channel_id=1, source_target_pairs={{0,384},{384,0},{128,256},{256,128},{1,385},{385,1},{129,257},{257... | collective-permute-start | bytes 983048 | tf_op jit(solution)/shard_map/ppermute | solution.py:112
  123.0 3.4 %collective-permute-done.10 = bf16[128,1280]{1,0:T(8,128)(2,1)S(1)} collective-permute-done((bf16[128,1280]{1,0:T(8,128)(2,1)}, bf16[128,1280]{1,0:T(8,128)(2,1)S(1)}, u32[]{:S(2)}, u32[]{:S(2)}) %collective-permute-start.10) | collective-permute-done | bytes 327712 | tf_op jit(solution)/shard_map/ppermute | solution.py:108
  136.1 3.0 %collective-permute-start.12 = (bf16[128,1280]{1,0:T(8,128)(2,1)S(1)}, bf16[128,1280]{1,0:T(8,128)(2,1)S(1)}, u32[]{:S(2)}, u32[]{:S(2)}) collective-permute-start(bf16[128,1280]{1,0:T(8,128)(2,1)S(1)} %fusion.11), channel_id=1, source_target_pairs={{0,384},{384,0},{128,256},{256,128},{1,385},{385,1},{129,257},{257... | collective-permute-start | bytes 983048 | tf_op jit(solution)/shard_map/ppermute | solution.py:112
  140.0 3.0 %collective-permute-start.14 = (bf16[256,512]{1,0:T(8,128)(2,1)S(1)}, bf16[256,512]{1,0:T(8,128)(2,1)S(1)}, u32[]{:S(2)}, u32[]{:S(2)}) collective-permute-start(bf16[256,512]{1,0:T(8,128)(2,1)S(1)} %pad_maximum_fusion), channel_id=1, source_target_pairs={{0,128},{128,0},{256,384},{384,256},{1,129},{129,1},{257,385},{385... | collective-permute-start | bytes 786440 | tf_op jit(solution)/shard_map/ppermute | solution.py:108
  142.9 6.1 %collective-permute-done.12 = bf16[128,1280]{1,0:T(8,128)(2,1)S(1)} collective-permute-done((bf16[128,1280]{1,0:T(8,128)(2,1)S(1)}, bf16[128,1280]{1,0:T(8,128)(2,1)S(1)}, u32[]{:S(2)}, u32[]{:S(2)}) %collective-permute-start.12) | collective-permute-done | bytes 327712 | tf_op jit(solution)/shard_map/ppermute | solution.py:112
  151.3 6.1 %all-to-all-start.4 = ((bf16[64,2,1280]{2,1,0:T(2,128)(2,1)}), bf16[64,2,1280]{2,1,0:T(2,128)(2,1)S(1)}, u32[]{:S(2)}, u32[]{:S(2)}) async-start(bf16[64,2,1280]{2,1,0:T(2,128)(2,1)} %reshape.44), calls=%async_computation.4 | async-start | bytes 655360 | tf_op jit(solution)/shard_map/all_to_all | solution.py:207
  157.4 2.8 %fusion.6 = bf16[1,1280,256]{2,1,0:T(8,128)(2,1)} fusion(bf16[512,1280]{1,0:T(8,128)(2,1)} %constant_dynamic-update-slice_fusion, bf16[256,256]{1,0:T(8,128)(2,1)S(1)} %get-tuple-element.48, bf16[256,256]{1,0:T(8,128)(2,1)S(1)} %get-tuple-element.43), kind=kOutput, calls=%fused_computation.15 | convolution fusion | flops 336396288 | bytes 2228224 | tf_op jit(solution)/shard_map/dot_general | solution.py:140
  164.0 9.2 %all-to-all-done.4 = bf16[64,2,1280]{2,1,0:T(2,128)(2,1)S(1)} async-done(((bf16[64,2,1280]{2,1,0:T(2,128)(2,1)}), bf16[64,2,1280]{2,1,0:T(2,128)(2,1)S(1)}, u32[]{:S(2)}, u32[]{:S(2)}) %all-to-all-start.4) | async-done | bytes 327712 | tf_op jit(solution)/shard_map/all_to_all | solution.py:207
  (94 shorter events, 52.4 us)
Async XLA Ops:
  0.6 33.5 %copy-start = (bf16[1,256,1280]{2,1,0:T(8,128)(2,1)S(1)}, bf16[1,256,1280]{2,1,0:T(8,128)(2,1)}, u32[]{:S(2)}) copy-start(bf16[1,256,1280]{2,1,0:T(8,128)(2,1)} %param.13) | copy-start | bytes 1966084
  0.6 26.4 %collective-permute-start = (bf16[1280,256]{1,0:T(8,128)(2,1)}, bf16[1280,256]{1,0:T(8,128)(2,1)S(1)}, u32[]{:S(2)}, u32[]{:S(2)}) collective-permute-start(bf16[1280,256]{1,0:T(8,128)(2,1)} %bitcast.71), channel_id=1, source_target_pairs={{0,128},{128,0},{256,384},{384,256},{1,129},{129,1},{257,385},{385... | collective-permute-start | bytes 1966088 | tf_op jit(solution)/shard_map/ppermute | solution.py:108
  3.5 46.7 %copy-start.1 = (bf16[1,1280,256]{2,1,0:T(8,128)(2,1)S(1)}, bf16[1,1280,256]{2,1,0:T(8,128)(2,1)}, u32[]{:S(2)}) copy-start(bf16[1,1280,256]{2,1,0:T(8,128)(2,1)} %param.11) | copy-start | bytes 1966084
  5.7 18.9 %all-to-all-start = ((bf16[8,8,640]{2,1,0:T(8,128)(2,1)}), bf16[8,8,640]{2,1,0:T(8,128)(2,1)S(1)}, u32[]{:S(2)}, u32[]{:S(2)}) async-start(bf16[8,8,640]{2,1,0:T(8,128)(2,1)} %shard_map.102), calls=%async_computation | async-start | bytes 163840 | tf_op jit(solution)/shard_map/all_to_all | solution.py:154
  16.0 21.2 %collective-permute-start.1 = (bf16[1280,256]{1,0:T(8,128)(2,1)}, bf16[1280,256]{1,0:T(8,128)(2,1)S(1)}, u32[]{:S(2)}, u32[]{:S(2)}) collective-permute-start(bf16[1280,256]{1,0:T(8,128)(2,1)} %bitcast.72), channel_id=1, source_target_pairs={{0,128},{128,0},{256,384},{384,256},{1,129},{129,1},{257,385},{385... | collective-permute-start | bytes 1966088 | tf_op jit(solution)/shard_map/ppermute | solution.py:108
  27.0 18.7 %all-to-all-start.1 = ((bf16[8,16,1280]{2,1,0:T(8,128)(2,1)}), bf16[8,16,1280]{2,1,0:T(8,128)(2,1)S(1)}, u32[]{:S(2)}, u32[]{:S(2)}) async-start(bf16[8,16,1280]{2,1,0:T(8,128)(2,1)} %get-tuple-element.24), calls=%async_computation.1 | async-start | bytes 655360 | tf_op jit(solution)/shard_map/all_to_all | solution.py:120
  34.1 23.6 %collective-permute-start.3 = (bf16[256,1280]{1,0:T(8,128)(2,1)S(1)}, bf16[256,1280]{1,0:T(8,128)(2,1)S(1)}, u32[]{:S(2)}, u32[]{:S(2)}) collective-permute-start(bf16[256,1280]{1,0:T(8,128)(2,1)S(1)} %bitcast.70), channel_id=1, source_target_pairs={{0,128},{128,0},{256,384},{384,256},{1,129},{129,1},{257,385},{385... | collective-permute-start | bytes 1966088 | tf_op jit(solution)/shard_map/ppermute | solution.py:108
  45.7 10.3 %collective-permute-start.2 = (bf16[128,1280]{1,0:T(8,128)(2,1)S(1)}, bf16[128,1280]{1,0:T(8,128)(2,1)S(1)}, u32[]{:S(2)}, u32[]{:S(2)}) collective-permute-start(bf16[128,1280]{1,0:T(8,128)(2,1)S(1)} %bitcast.63), channel_id=1, source_target_pairs={{0,384},{384,0},{128,256},{256,128},{1,385},{385,1},{129,257},{257... | collective-permute-start | bytes 983048 | tf_op jit(solution)/shard_map/ppermute | solution.py:112
  57.7 3.8 %collective-permute-start.4 = (bf16[256,1024]{1,0:T(8,128)(2,1)S(1)}, bf16[256,1024]{1,0:T(8,128)(2,1)S(1)}, u32[]{:S(2)}, u32[]{:S(2)}) collective-permute-start(bf16[256,1024]{1,0:T(8,128)(2,1)S(1)} %maximum_maximum_fusion), channel_id=1, source_target_pairs={{0,1},{1,0},{2,3},{3,2},{4,5},{5,4},{6,7},{7,6},{8,9},{9,8},{10,11... | collective-permute-start | bytes 1572872 | tf_op jit(solution)/shard_map/ppermute | solution.py:104
  62.9 12.9 %collective-permute-start.5 = (bf16[128,1280]{1,0:T(8,128)(2,1)S(1)}, bf16[128,1280]{1,0:T(8,128)(2,1)S(1)}, u32[]{:S(2)}, u32[]{:S(2)}) collective-permute-start(bf16[128,1280]{1,0:T(8,128)(2,1)S(1)} %fusion.9), channel_id=1, source_target_pairs={{0,384},{384,0},{128,256},{256,128},{1,385},{385,1},{129,257},{257... | collective-permute-start | bytes 983048 | tf_op jit(solution)/shard_map/ppermute | solution.py:112
  66.0 11.4 %collective-permute-start.6 = (bf16[128,1280]{1,0:T(8,128)(2,1)S(1)}, bf16[128,1280]{1,0:T(8,128)(2,1)S(1)}, u32[]{:S(2)}, u32[]{:S(2)}) collective-permute-start(bf16[128,1280]{1,0:T(8,128)(2,1)S(1)} %bitcast.68), channel_id=1, source_target_pairs={{0,128},{128,0},{256,384},{384,256},{1,129},{129,1},{257,385},{385... | collective-permute-start | bytes 983048 | tf_op jit(solution)/shard_map/ppermute | solution.py:108
  78.1 16.8 %all-to-all-start.2 = ((bf16[8,16,1280]{2,1,0:T(8,128)(2,1)}), bf16[8,16,1280]{2,1,0:T(8,128)(2,1)}, u32[]{:S(2)}, u32[]{:S(2)}) async-start(bf16[8,16,1280]{2,1,0:T(8,128)(2,1)} %bitcast.73), calls=%async_computation.2 | async-start | bytes 655360 | tf_op jit(solution)/shard_map/all_to_all | solution.py:120
  82.1 14.5 %collective-permute-start.7 = (bf16[128,1280]{1,0:T(8,128)(2,1)S(1)}, bf16[128,1280]{1,0:T(8,128)(2,1)}, u32[]{:S(2)}, u32[]{:S(2)}) collective-permute-start(bf16[128,1280]{1,0:T(8,128)(2,1)S(1)} %collective-permute-done.2), channel_id=1, source_target_pairs={{0,128},{128,0},{256,384},{384,256},{1,129},{129,1},{257,385},{385... | collective-permute-start | bytes 983048 | tf_op jit(solution)/shard_map/ppermute | solution.py:108
  96.6 15.3 %all-to-all-start.3 = ((bf16[8,16,1280]{2,1,0:T(8,128)(2,1)}), bf16[8,16,1280]{2,1,0:T(8,128)(2,1)}, u32[]{:S(2)}, u32[]{:S(2)}) async-start(bf16[8,16,1280]{2,1,0:T(8,128)(2,1)} %shard_map.104), calls=%async_computation.3 | async-start | bytes 655360 | tf_op jit(solution)/shard_map/all_to_all | solution.py:120
  100.8 6.9 %collective-permute-start.8 = (bf16[256,256]{1,0:T(8,128)(2,1)S(1)}, bf16[256,256]{1,0:T(8,128)(2,1)S(1)}, u32[]{:S(2)}, u32[]{:S(2)}) collective-permute-start(bf16[256,256]{1,0:T(8,128)(2,1)S(1)} %get-tuple-element.46), channel_id=1, source_target_pairs={{0,128},{128,0},{256,384},{384,256},{1,129},{129,1},{257,385},{385... | collective-permute-start | bytes 393224 | tf_op jit(solution)/shard_map/ppermute | solution.py:108
  111.9 10.4 %collective-permute-start.9 = (bf16[128,1280]{1,0:T(8,128)(2,1)}, bf16[128,1280]{1,0:T(8,128)(2,1)S(1)}, u32[]{:S(2)}, u32[]{:S(2)}) collective-permute-start(bf16[128,1280]{1,0:T(8,128)(2,1)} %bitcast.6), channel_id=1, source_target_pairs={{0,384},{384,0},{128,256},{256,128},{1,385},{385,1},{129,257},{257... | collective-permute-start | bytes 983048 | tf_op jit(solution)/shard_map/ppermute | solution.py:112
  117.2 9.2 %collective-permute-start.10 = (bf16[128,1280]{1,0:T(8,128)(2,1)}, bf16[128,1280]{1,0:T(8,128)(2,1)S(1)}, u32[]{:S(2)}, u32[]{:S(2)}) collective-permute-start(bf16[128,1280]{1,0:T(8,128)(2,1)} %bitcast.6), channel_id=1, source_target_pairs={{0,128},{128,0},{256,384},{384,256},{1,129},{129,1},{257,385},{385... | collective-permute-start | bytes 983048 | tf_op jit(solution)/shard_map/ppermute | solution.py:108
  120.8 7.5 %copy-start.10 = (bf16[128,1280]{1,0:T(8,128)(2,1)S(1)}, bf16[128,1280]{1,0:T(8,128)(2,1)}, u32[]{:S(2)}) copy-start(bf16[128,1280]{1,0:T(8,128)(2,1)} %copy-done.9) | copy-start | bytes 983044
  123.0 10.1 %copy-start.8 = (f32[256,1024]{1,0:T(8,128)S(1)}, f32[256,1024]{1,0:T(8,128)}, u32[]{:S(2)}) copy-start(f32[256,1024]{1,0:T(8,128)} %copy-done.7) | copy-start | bytes 3145732
  126.4 6.7 %collective-permute-start.11 = (bf16[256,512]{1,0:T(8,128)(2,1)S(1)}, bf16[256,512]{1,0:T(8,128)(2,1)S(1)}, u32[]{:S(2)}, u32[]{:S(2)}) collective-permute-start(bf16[256,512]{1,0:T(8,128)(2,1)S(1)} %maximum_maximum_fusion.1), channel_id=1, source_target_pairs={{0,1},{1,0},{2,3},{3,2},{4,5},{5,4},{6,7},{7,6},{8,9},{9,8},{10,11... | collective-permute-start | bytes 786440 | tf_op jit(solution)/shard_map/ppermute | solution.py:104
  130.8 19.6 %collective-permute-start.13 = (bf16[128,1280]{1,0:T(8,128)(2,1)S(1)}, bf16[128,1280]{1,0:T(8,128)(2,1)S(1)}, u32[]{:S(2)}, u32[]{:S(2)}) collective-permute-start(bf16[128,1280]{1,0:T(8,128)(2,1)S(1)} %collective-permute-done.9), channel_id=1, source_target_pairs={{0,128},{128,0},{256,384},{384,256},{1,129},{129,1},{257,385},{385... | collective-permute-start | bytes 983048 | tf_op jit(solution)/shard_map/ppermute | solution.py:108
  136.1 12.9 %collective-permute-start.12 = (bf16[128,1280]{1,0:T(8,128)(2,1)S(1)}, bf16[128,1280]{1,0:T(8,128)(2,1)S(1)}, u32[]{:S(2)}, u32[]{:S(2)}) collective-permute-start(bf16[128,1280]{1,0:T(8,128)(2,1)S(1)} %fusion.11), channel_id=1, source_target_pairs={{0,384},{384,0},{128,256},{256,128},{1,385},{385,1},{129,257},{257... | collective-permute-start | bytes 983048 | tf_op jit(solution)/shard_map/ppermute | solution.py:112
  140.0 17.4 %collective-permute-start.14 = (bf16[256,512]{1,0:T(8,128)(2,1)S(1)}, bf16[256,512]{1,0:T(8,128)(2,1)S(1)}, u32[]{:S(2)}, u32[]{:S(2)}) collective-permute-start(bf16[256,512]{1,0:T(8,128)(2,1)S(1)} %pad_maximum_fusion), channel_id=1, source_target_pairs={{0,128},{128,0},{256,384},{384,256},{1,129},{129,1},{257,385},{385... | collective-permute-start | bytes 786440 | tf_op jit(solution)/shard_map/ppermute | solution.py:108
  151.3 21.9 %all-to-all-start.4 = ((bf16[64,2,1280]{2,1,0:T(2,128)(2,1)}), bf16[64,2,1280]{2,1,0:T(2,128)(2,1)S(1)}, u32[]{:S(2)}, u32[]{:S(2)}) async-start(bf16[64,2,1280]{2,1,0:T(2,128)(2,1)} %reshape.44), calls=%async_computation.4 | async-start | bytes 655360 | tf_op jit(solution)/shard_map/all_to_all | solution.py:207
  (12 other events, 27.4 us)

commit v3 on v2

--- a/solution.py
+++ b/solution.py
@@ -13,6 +13,7 @@
 SWAP = [(0, 1), (1, 0)]
 PAIR = [(0, 1), (1, 0), (2, 3), (3, 2)]
 CROSS = [(0, 3), (3, 0), (1, 2), (2, 1)]
+TWO_COLUMNS = [[x * NY + y for x in columns for y in range(NY)] for columns in ((0, 3), (1, 2))]
 
 
 def silu_slope(gate_val):
@@ -82,18 +83,26 @@
     blocks_ref[...] = jnp.broadcast_to(residual[None], blocks_ref.shape)
 
 
-def combine_kernel(ids_ref, lengths_ref, tokens_ref, target_ref, pieces_ref, out_ref):
+def own_kernel(ids_ref, lengths_ref, tokens_ref, target_ref, own_ref, chosen_ref):
     row_len = tokens_ref.shape[0]
-    count = pieces_ref.shape[1]
-    chosen = one_hot(slot_matrix(ids_ref[...], lengths_ref[...], count, CAP))
+    chosen = one_hot(slot_matrix(ids_ref[...], lengths_ref[...], chosen_ref.shape[0], CAP))
+    taken = times_rows(chosen, jnp.ones((chosen.shape[0], 128), BF16))[:, :1]
+    live = iota((row_len, 1), 0) < jnp.sum(lengths_ref[...], axis=1, keepdims=True)
+    own = tokens_ref[...].astype(F32) - target_ref[...].astype(F32)
+    own_ref[...] = jnp.where(live & (taken == 0.0), own, 0.0).astype(BF16)
+    chosen_ref[...] = chosen
+
+
+def combine_kernel(own_ref, chosen_ref, pieces_ref, out_ref):
     slots = pieces_ref[0].astype(F32)
     for i in range(1, pieces_ref.shape[0]):
         slots += pieces_ref[i].astype(F32)
-    routed = lax.dot_general(chosen, slots.astype(BF16), CONTRACT_ROWS, preferred_element_type=F32)
-    taken = lax.dot_general(chosen, jnp.ones((count, 128), BF16), CONTRACT_ROWS, preferred_element_type=F32)[:, :1]
-    live = iota((row_len, 1), 0) < jnp.sum(lengths_ref[...], axis=1, keepdims=True)
-    own = tokens_ref[...].astype(F32) - target_ref[...].astype(F32)
-    out_ref[...] = (jnp.where(live & (taken == 0.0), own, 0.0) + routed).astype(BF16)
+    routed = times_rows(chosen_ref[...], slots.astype(BF16))
+    out_ref[...] = (own_ref[...].astype(F32) + routed).astype(BF16)
+
+
+def times_rows(left, right):
+    return lax.dot_general(left, right, CONTRACT_ROWS, preferred_element_type=F32)
 
 
 def array(*shape, dtype=BF16):
@@ -112,14 +121,23 @@
     return lax.ppermute(value, "x", CROSS)
 
 
-def after(value, early):
-    return lax.optimization_barrier((value, early))
+def after(*values):
+    return lax.optimization_barrier(values)
 
 
 def over_y(blocks):
     return lax.all_to_all(blocks, "y", 0, 0, tiled=True)
 
 
+def over_two_columns(blocks):
+    return lax.all_to_all(blocks, ("x", "y"), 0, 0, axis_index_groups=TWO_COLUMNS, tiled=True)
+
+
+def in_order(mine, theirs):
+    lower = lax.axis_index("x") < NX // 2
+    return jnp.where(lower, mine, theirs), jnp.where(lower, theirs, mine)
+
+
 def times(left, right):
     return jnp.dot(left, right, preferred_element_type=F32)
 
@@ -137,7 +155,7 @@
 
 
 def weight_grad(left, right):
-    return lax.dot_general(left, right, CONTRACT_ROWS, preferred_element_type=F32).astype(BF16)
+    return times_rows(left, right).astype(BF16)
 
 
 def local(tokens, target, expert_ids, doc_lengths, w_gate, w_up, w_down):
@@ -172,23 +190,30 @@
     hidden = (jax.nn.silu(gate) * up).astype(BF16)
     hidden_p = (jax.nn.silu(gate_p) * up_p).astype(BF16)
 
-    def column_sum(product):
-        theirs = cross(product(slice(column_rows, None)).astype(BF16))
-        return product(slice(0, column_rows)) + theirs.astype(F32)
-
-    column_out = column_sum(lambda s: times(hidden[s], down_w) + times(hidden_p[s], down_w_p)).astype(BF16)
-    column_out, pair_column = after(column_out, pair(column))
-    pieces = over_y(column_out.reshape(NY, slot_count, features))
-    blocks = pl.pallas_call(settle_kernel, out_shape=array(NY, slot_count, features))(pieces, my_rows, my_target)
-    blocks, pair_crossed = after(blocks, pair(crossed))
-
-    grad_column = over_y(blocks).reshape(column_rows, features)
-    grad_column, pair_hidden = after(grad_column, pair(hidden_p))
-    grad_crossed = cross(grad_column)
+    mine, theirs = slice(0, column_rows), slice(column_rows, None)
+
+    def output_part(s):
+        return times(hidden[s], down_w) + times(hidden_p[s], down_w_p)
+
+    partial = stack(*in_order(output_part(mine).astype(BF16), output_part(theirs).astype(BF16)))
+    partial, tokens_late, target_late = after(partial, tokens, target)
+    own, chosen = pl.pallas_call(own_kernel, out_shape=(array(row_len, features), array(slot_count, row_len)))(
+        ids, doc_lengths, tokens_late, target_late
+    )
+    pieces = over_two_columns(partial.reshape(2 * NY, slot_count, features))
+    pieces, own, chosen = after(pieces, own, chosen)
+    blocks = pl.pallas_call(settle_kernel, out_shape=array(2 * NY, slot_count, features))(pieces, my_rows, my_target)
+    blocks, pair_column = after(blocks, pair(column))
+
+    both = over_two_columns(blocks).reshape(2 * column_rows, features)
+    both, pair_crossed = after(both, pair(crossed))
+    grad_column, grad_crossed = in_order(both[:column_rows], both[column_rows:])
     part = stack(
         *[beside(*[times_t(g, w).astype(BF16) for w in (down_w, down_w_p)]) for g in (grad_column, grad_crossed)]
     )
-    part, pair_grad_column = after(part, pair(grad_column))
+    down_part, down_part_p = [
+        times_rows(h[:column_rows], grad_column) + times_rows(h[column_rows:], grad_crossed) for h in (hidden, hidden_p)
+    ]
     sums = part.astype(F32) + swap(part).astype(F32)
     back, back_p = jnp.split(sums, 2, axis=1)
     gate_grad = (back * up * silu_slope(gate)).astype(BF16)
@@ -200,18 +225,20 @@
         own = times_t(gate_grad[s], gate_w) + times_t(up_grad[s], up_w)
         return own + times_t(gate_grad_p[s], gate_w_p) + times_t(up_grad_p[s], up_w_p)
 
-    mine = (jnp.arange(column_rows) // slot_count) == lax.axis_index("y")
-    column_in = column_sum(input_part) + jnp.where(mine[:, None], grad_column.astype(F32), 0.0)
-    column_in, pair_grad_crossed = after(column_in.astype(BF16), pair(grad_crossed))
-    pair_in = pair(beside(gate_grad_p, up_grad_p))
+    at_home = (jnp.arange(column_rows) // slot_count) == lax.axis_index("y")
+    extra = jnp.where(at_home[:, None], grad_column.astype(F32), 0.0)
+    partial = input_part(theirs).astype(BF16)
+    partial, down_part_late = after(partial, down_part_p.astype(BF16))
+    column_in = input_part(mine) + extra + cross(partial).astype(F32)
+    pair_down = pair(down_part_late)
+    column_in, pair_in = after(column_in.astype(BF16), pair(beside(gate_grad_p, up_grad_p)))
     pieces = lax.all_to_all(column_in.reshape(NY * NZ, CAP, features), ("y", "z"), 0, 0, tiled=True)
     grad_tokens = pl.pallas_call(combine_kernel, out_shape=array(row_len, features))(
-        ids, doc_lengths, tokens, target, pieces.reshape(NY, slot_count, features)
+        own, chosen, pieces.reshape(NY, slot_count, features)
     )
 
     rows = stack(column, crossed, pair_column, pair_crossed)
-    grads = stack(grad_column, grad_crossed, pair_grad_column, pair_grad_crossed)
-    grad_down = weight_grad(stack(hidden, pair_hidden), grads)
+    grad_down = (down_part + pair_down.astype(F32)).astype(BF16)
     grad_gate = weight_grad(rows, stack(gate_grad, pair_in[:, :units]))
     grad_up = weight_grad(rows, stack(up_grad, pair_in[:, units:]))
     return (grad_tokens, grad_gate[None], grad_up[None], grad_down[None])

time: 178 us -> 170 us (0.955)
  waiting for transfers between devices: 67.1 us -> 57.7 us
  starting transfers between devices: 71.9 us -> 66.9 us
  other arithmetic: 0.79 us -> 4.78 us
  Pallas kernels: 8.2 us -> 10.4 us
    all_to_all x0 -> x2, waiting for transfers between devices: none -> 19.2 us  [over_two_columns(): lax.all_to_all(blocks, ('x', 'y'), 0, 0, axis_index_groups=TWO_COLUMNS, t...]
    all_to_all x3 -> x1, waiting for transfers between devices: 23.2 us -> 8.44 us  [over_y(): return lax.all_to_all(blocks, 'y', 0, 0, tiled=True)]
    all_to_all x0 -> x2, starting transfers between devices: none -> 12.6 us  [over_two_columns(): lax.all_to_all(blocks, ('x', 'y'), 0, 0, axis_index_groups=TWO_COLUMNS, t...]
    ppermute x4 -> x2, waiting for transfers between devices: 20.1 us -> 7.65 us  [cross(): return lax.ppermute(value, 'x', CROSS)]
    all_to_all x3 -> x1, starting transfers between devices: 15.3 us -> 7.1 us  [over_y(): return lax.all_to_all(blocks, 'y', 0, 0, tiled=True)]
    ppermute x4 -> x2, starting transfers between devices: 13.3 us -> 7.42 us  [cross(): return lax.ppermute(value, 'x', CROSS)]
    ppermute x9 -> x7, starting transfers between devices: 23.2 us -> 18.7 us  [pair(): return lax.ppermute(value, 'x', PAIR)]
    dot_general x3 -> x6, matrix products: 6.54 us -> 9.59 us  [times_rows(): lax.dot_general(left, right, CONTRACT_ROWS, preferred_element_type=F32)]
  transfers between devices with their start and end apart: 20 -> 16, of which waited for: 13 -> 10; matrix products, arithmetic and copies ran while one was open for 13% -> 12% of each run, Pallas kernels for 3% -> 5%
where the time goes in v3:
time: 170 us; the launch traced here: 168 us
  starting transfers between devices  66.9 us (39%)
  waiting for transfers between devices  57.7 us (34%)
  matrix products  18.2 us (11%)
  Pallas kernels  10.4 us (6%)
  local copies, waits for them, and re-layouts  9.42 us (6%)
  other arithmetic  4.78 us (3%)
    all_to_all x2, waiting for transfers between devices, over_two_columns(): lax.all_to_all(blocks, ('x', 'y'), 0, 0, axis_index_groups=TWO_COLUMNS, t...  19.2 us
    ppermute x7, starting transfers between devices, pair(): return lax.ppermute(value, 'x', PAIR)  18.7 us
    all_to_all x2, starting transfers between devices, over_two_columns(): lax.all_to_all(blocks, ('x', 'y'), 0, 0, axis_index_groups=TWO_COLUMNS, t...  12.6 us
    all_to_all x1, starting transfers between devices, local(): arrived = lax.all_to_all(message, 'z', 0, 0, tiled=True)  10.3 us
    dot_general x6, matrix products, times_rows(): lax.dot_general(left, right, CONTRACT_ROWS, preferred_element_type=F32)  9.59 us
    all_to_all x1, waiting for transfers between devices, over_y(): return lax.all_to_all(blocks, 'y', 0, 0, tiled=True)  8.44 us
    ppermute x7, waiting for transfers between devices, pair(): return lax.ppermute(value, 'x', PAIR)  8.34 us
    ppermute x2, waiting for transfers between devices, cross(): return lax.ppermute(value, 'x', CROSS)  7.65 us
  transfers between devices with their start and end apart: 16, of which 10 were waited for; matrix products, arithmetic and copies ran while one was open for 12% of the time, Pallas kernels for 5%

profile of v3, /device:TPU:6, one launch (start us, length us, event | category | flops | bytes accessed | tf_op | source)
XLA Modules:
  0.0 168.4 jit_solution(16482614666005439590)
XLA Ops:
  0.6 2.9 %collective-permute-start = (bf16[1280,256]{1,0:T(8,128)(2,1)}, bf16[1280,256]{1,0:T(8,128)(2,1)S(1)}, u32[]{:S(2)}, u32[]{:S(2)}) collective-permute-start(bf16[1280,256]{1,0:T(8,128)(2,1)} %bitcast.75), channel_id=1, source_target_pairs={{0,128},{128,0},{256,384},{384,256},{1,129},{129,1},{257,385},{385... | collective-permute-start | bytes 1966088 | tf_op jit(solution)/shard_map/ppermute | solution.py:117
  5.7 10.3 %all-to-all-start = ((bf16[8,8,640]{2,1,0:T(8,128)(2,1)}), bf16[8,8,640]{2,1,0:T(8,128)(2,1)S(1)}, u32[]{:S(2)}, u32[]{:S(2)}) async-start(bf16[8,8,640]{2,1,0:T(8,128)(2,1)} %shard_map.102), calls=%async_computation | async-start | bytes 163840 | tf_op jit(solution)/shard_map/all_to_all | solution.py:172
  16.0 3.1 %collective-permute-start.1 = (bf16[1280,256]{1,0:T(8,128)(2,1)}, bf16[1280,256]{1,0:T(8,128)(2,1)S(1)}, u32[]{:S(2)}, u32[]{:S(2)}) collective-permute-start(bf16[1280,256]{1,0:T(8,128)(2,1)} %bitcast.76), channel_id=1, source_target_pairs={{0,128},{128,0},{256,384},{384,256},{1,129},{129,1},{257,385},{385... | collective-permute-start | bytes 1966088 | tf_op jit(solution)/shard_map/ppermute | solution.py:117
  19.1 5.5 %all-to-all-done.arrived_ref = bf16[8,8,640]{2,1,0:T(8,128)(2,1)S(1)} async-done(((bf16[8,8,640]{2,1,0:T(8,128)(2,1)}), bf16[8,8,640]{2,1,0:T(8,128)(2,1)S(1)}, u32[]{:S(2)}, u32[]{:S(2)}) %all-to-all-start) | async-done | bytes 81952 | tf_op jit(solution)/shard_map/all_to_all | solution.py:172
  27.0 7.1 %all-to-all-start.1 = ((bf16[8,16,1280]{2,1,0:T(8,128)(2,1)}), bf16[8,16,1280]{2,1,0:T(8,128)(2,1)S(1)}, u32[]{:S(2)}, u32[]{:S(2)}) async-start(bf16[8,16,1280]{2,1,0:T(8,128)(2,1)} %get-tuple-element.30), calls=%async_computation.1 | async-start | bytes 655360 | tf_op jit(solution)/shard_map/all_to_all | solution.py:129
  34.1 3.1 %collective-permute-start.3 = (bf16[256,1280]{1,0:T(8,128)(2,1)S(1)}, bf16[256,1280]{1,0:T(8,128)(2,1)S(1)}, u32[]{:S(2)}, u32[]{:S(2)}) collective-permute-start(bf16[256,1280]{1,0:T(8,128)(2,1)S(1)} %bitcast.74), channel_id=1, source_target_pairs={{0,128},{128,0},{256,384},{384,256},{1,129},{129,1},{257,385},{385... | collective-permute-start | bytes 1966088 | tf_op jit(solution)/shard_map/ppermute | solution.py:117
  37.2 8.4 %all-to-all-done.1 = bf16[8,16,1280]{2,1,0:T(8,128)(2,1)S(1)} async-done(((bf16[8,16,1280]{2,1,0:T(8,128)(2,1)}), bf16[8,16,1280]{2,1,0:T(8,128)(2,1)S(1)}, u32[]{:S(2)}, u32[]{:S(2)}) %all-to-all-start.1) | async-done | bytes 327712 | tf_op jit(solution)/shard_map/all_to_all | solution.py:129
  45.7 3.2 %collective-permute-start.2 = (bf16[128,1280]{1,0:T(8,128)(2,1)S(1)}, bf16[128,1280]{1,0:T(8,128)(2,1)S(1)}, u32[]{:S(2)}, u32[]{:S(2)}) collective-permute-start(bf16[128,1280]{1,0:T(8,128)(2,1)S(1)} %bitcast.67), channel_id=1, source_target_pairs={{0,384},{384,0},{128,256},{256,128},{1,385},{385,1},{129,257},{257... | collective-permute-start | bytes 983048 | tf_op jit(solution)/shard_map/ppermute | solution.py:121
  51.0 4.9 %collective-permute-done.2 = bf16[128,1280]{1,0:T(8,128)(2,1)S(1)} collective-permute-done((bf16[128,1280]{1,0:T(8,128)(2,1)S(1)}, bf16[128,1280]{1,0:T(8,128)(2,1)S(1)}, u32[]{:S(2)}, u32[]{:S(2)}) %collective-permute-start.2) | collective-permute-done | bytes 327712 | tf_op jit(solution)/shard_map/ppermute | solution.py:121
  59.8 2.2 %collective-permute-done.4 = bf16[256,1024]{1,0:T(8,128)(2,1)} collective-permute-done((bf16[256,1024]{1,0:T(8,128)(2,1)}, bf16[256,1024]{1,0:T(8,128)(2,1)}, u32[]{:S(2)}, u32[]{:S(2)}) %collective-permute-start.4) | collective-permute-done | bytes 524320 | tf_op jit(solution)/shard_map/ppermute | solution.py:113
  66.1 5.2 %all-to-all-start.2 = ((bf16[16,16,1280]{2,1,0:T(8,128)(2,1)}), bf16[16,16,1280]{2,1,0:T(8,128)(2,1)}, u32[]{:S(2)}, u32[]{:S(2)}) async-start(bf16[16,16,1280]{2,1,0:T(8,128)(2,1)} %bitcast.77), calls=%async_computation.2 | async-start | bytes 1310720 | tf_op jit(solution)/shard_map/all_to_all | solution.py:133
  73.2 2.3 %shard_map.104 = (bf16[128,1280]{1,0:T(8,128)(2,1)}, bf16[16,128]{1,0:T(8,128)(2,1)}) custom-call(s32[1,128]{1,0:T(1,128)} %bitcast.79, s32[1,8]{1,0:T(1,128)} %lengths_ref.3, bf16[128,1280]{1,0:T(8,128)(2,1)} %tokens_ref.2, bf16[128,1280]{1,0:T(8,128)(2,1)} %target_ref.2), custom_call_target="tpu_custom_call" | custom-call | tf_op jit(solution)/shard_map/pallas_call | solution.py:200
  75.4 13.4 %all-to-all-done.2.pieces_ref = bf16[16,16,1280]{2,1,0:T(8,128)(2,1)} async-done(((bf16[16,16,1280]{2,1,0:T(8,128)(2,1)}), bf16[16,16,1280]{2,1,0:T(8,128)(2,1)}, u32[]{:S(2)}, u32[]{:S(2)}) %all-to-all-start.2) | async-done | bytes 655392 | tf_op jit(solution)/shard_map/all_to_all | solution.py:133
  90.9 7.4 %all-to-all-start.3 = ((bf16[16,16,1280]{2,1,0:T(8,128)(2,1)}), bf16[16,16,1280]{2,1,0:T(8,128)(2,1)}, u32[]{:S(2)}, u32[]{:S(2)}) async-start(bf16[16,16,1280]{2,1,0:T(8,128)(2,1)} %shard_map.105), calls=%async_computation.3 | async-start | bytes 1310720 | tf_op jit(solution)/shard_map/all_to_all | solution.py:133
  103.5 6.5 %collective-permute-done.6 = bf16[128,1280]{1,0:T(8,128)(2,1)S(1)} collective-permute-done((bf16[128,1280]{1,0:T(8,128)(2,1)S(1)}, bf16[128,1280]{1,0:T(8,128)(2,1)S(1)}, u32[]{:S(2)}, u32[]{:S(2)}) %collective-permute-start.6) | collective-permute-done | bytes 327712 | tf_op jit(solution)/shard_map/ppermute | solution.py:117
  110.0 5.8 %all-to-all-done.3 = bf16[16,16,1280]{2,1,0:T(8,128)(2,1)} async-done(((bf16[16,16,1280]{2,1,0:T(8,128)(2,1)}), bf16[16,16,1280]{2,1,0:T(8,128)(2,1)}, u32[]{:S(2)}, u32[]{:S(2)}) %all-to-all-start.3) | async-done | bytes 655392 | tf_op jit(solution)/shard_map/all_to_all | solution.py:133
  127.3 4.3 %collective-permute-start.8 = (bf16[128,1280]{1,0:T(8,128)(2,1)S(1)}, bf16[128,1280]{1,0:T(8,128)(2,1)S(1)}, u32[]{:S(2)}, u32[]{:S(2)}) collective-permute-start(bf16[128,1280]{1,0:T(8,128)(2,1)S(1)} %fusion.10), channel_id=1, source_target_pairs={{0,384},{384,0},{128,256},{256,128},{1,385},{385,1},{129,257},{257... | collective-permute-start | bytes 983048 | tf_op jit(solution)/shard_map/ppermute | solution.py:121
  133.5 3.9 %collective-permute-start.10 = (bf16[256,1280]{1,0:T(8,128)(2,1)}, bf16[256,1280]{1,0:T(8,128)(2,1)}, u32[]{:S(2)}, u32[]{:S(2)}) collective-permute-start(bf16[256,1280]{1,0:T(8,128)(2,1)} %fusion), channel_id=1, source_target_pairs={{0,128},{128,0},{256,384},{384,256},{1,129},{129,1},{257,385},{385... | collective-permute-start | bytes 1966088 | tf_op jit(solution)/shard_map/ppermute | solution.py:117
  137.8 2.7 %collective-permute-done.8 = bf16[128,1280]{1,0:T(8,128)(2,1)S(1)} collective-permute-done((bf16[128,1280]{1,0:T(8,128)(2,1)S(1)}, bf16[128,1280]{1,0:T(8,128)(2,1)S(1)}, u32[]{:S(2)}, u32[]{:S(2)}) %collective-permute-start.8) | collective-permute-done | bytes 327712 | tf_op jit(solution)/shard_map/ppermute | solution.py:121
  143.6 6.8 %all-to-all-start.4 = ((bf16[64,2,1280]{2,1,0:T(2,128)(2,1)}), bf16[64,2,1280]{2,1,0:T(2,128)(2,1)S(1)}, u32[]{:S(2)}, u32[]{:S(2)}) async-start(bf16[64,2,1280]{2,1,0:T(2,128)(2,1)} %reshape.44), calls=%async_computation.4 | async-start | bytes 655360 | tf_op jit(solution)/shard_map/all_to_all | solution.py:235
  151.4 2.7 %fusion.5 = bf16[1,1280,256]{2,1,0:T(8,128)(2,1)} fusion(bf16[512,1280]{1,0:T(8,128)(2,1)} %constant_dynamic-update-slice_fusion, bf16[256,256]{1,0:T(8,128)(2,1)S(1)} %get-tuple-element.65, bf16[256,256]{1,0:T(8,128)(2,1)S(1)} %get-tuple-element.57), kind=kOutput, calls=%fused_computation.15 | convolution fusion | flops 336396288 | bytes 2228224 | tf_op jit(solution)/shard_map/dot_general | solution.py:105
  154.1 2.7 %fusion.6 = bf16[1,1280,256]{2,1,0:T(8,128)(2,1)} fusion(bf16[512,1280]{1,0:T(8,128)(2,1)} %constant_dynamic-update-slice_fusion, bf16[256,256]{1,0:T(8,128)(2,1)S(1)} %get-tuple-element.64, bf16[256,256]{1,0:T(8,128)(2,1)S(1)} %get-tuple-element.55), kind=kOutput, calls=%fused_computation.16 | convolution fusion | flops 336396288 | bytes 2228224 | tf_op jit(solution)/shard_map/dot_general | solution.py:105
  156.8 2.3 %fusion.11 = bf16[1,256,1280]{2,1,0:T(8,128)(2,1)} fusion(bf16[256,1280]{1,0:T(8,128)(2,1)} %collective-permute-done.10, f32[256,1280]{1,0:T(8,128)S(1)} %fusion.42, bf16[128,1280]{1,0:T(8,128)(2,1)S(1)} %get-tuple-element.61, bf16[256,256]{1,0:T(8,128)(2,1)S(1)} %get-tuple-element.59), kind=kOutput, calls=%fused_computation.35 | convolution fusion | flops 85196800 | bytes 3014656 | tf_op jit(solution)/shard_map/dot_general | solution.py:105
  159.1 6.4 %all-to-all-done.4 = bf16[64,2,1280]{2,1,0:T(2,128)(2,1)S(1)} async-done(((bf16[64,2,1280]{2,1,0:T(2,128)(2,1)}), bf16[64,2,1280]{2,1,0:T(2,128)(2,1)S(1)}, u32[]{:S(2)}, u32[]{:S(2)}) %all-to-all-start.4) | async-done | bytes 327712 | tf_op jit(solution)/shard_map/all_to_all | solution.py:235
  (84 shorter events, 44.3 us)
Async XLA Ops:
  0.6 33.5 %copy-start = (bf16[1,256,1280]{2,1,0:T(8,128)(2,1)S(1)}, bf16[1,256,1280]{2,1,0:T(8,128)(2,1)}, u32[]{:S(2)}) copy-start(bf16[1,256,1280]{2,1,0:T(8,128)(2,1)} %param.13) | copy-start | bytes 1966084
  0.6 26.4 %collective-permute-start = (bf16[1280,256]{1,0:T(8,128)(2,1)}, bf16[1280,256]{1,0:T(8,128)(2,1)S(1)}, u32[]{:S(2)}, u32[]{:S(2)}) collective-permute-start(bf16[1280,256]{1,0:T(8,128)(2,1)} %bitcast.75), channel_id=1, source_target_pairs={{0,128},{128,0},{256,384},{384,256},{1,129},{129,1},{257,385},{385... | collective-permute-start | bytes 1966088 | tf_op jit(solution)/shard_map/ppermute | solution.py:117
  3.5 46.7 %copy-start.1 = (bf16[1,1280,256]{2,1,0:T(8,128)(2,1)S(1)}, bf16[1,1280,256]{2,1,0:T(8,128)(2,1)}, u32[]{:S(2)}) copy-start(bf16[1,1280,256]{2,1,0:T(8,128)(2,1)} %param.11) | copy-start | bytes 1966084
  5.7 18.9 %all-to-all-start = ((bf16[8,8,640]{2,1,0:T(8,128)(2,1)}), bf16[8,8,640]{2,1,0:T(8,128)(2,1)S(1)}, u32[]{:S(2)}, u32[]{:S(2)}) async-start(bf16[8,8,640]{2,1,0:T(8,128)(2,1)} %shard_map.102), calls=%async_computation | async-start | bytes 163840 | tf_op jit(solution)/shard_map/all_to_all | solution.py:172
  16.0 21.2 %collective-permute-start.1 = (bf16[1280,256]{1,0:T(8,128)(2,1)}, bf16[1280,256]{1,0:T(8,128)(2,1)S(1)}, u32[]{:S(2)}, u32[]{:S(2)}) collective-permute-start(bf16[1280,256]{1,0:T(8,128)(2,1)} %bitcast.76), channel_id=1, source_target_pairs={{0,128},{128,0},{256,384},{384,256},{1,129},{129,1},{257,385},{385... | collective-permute-start | bytes 1966088 | tf_op jit(solution)/shard_map/ppermute | solution.py:117
  27.0 7.1 %copy-start.4 = (bf16[1280,256]{1,0:T(8,128)(2,1)}, bf16[1280,256]{1,0:T(8,128)(2,1)S(1)}, u32[]{:S(2)}) copy-start(bf16[1280,256]{1,0:T(8,128)(2,1)S(1)} %collective-permute-done) | copy-start | bytes 1966084
  27.0 18.7 %all-to-all-start.1 = ((bf16[8,16,1280]{2,1,0:T(8,128)(2,1)}), bf16[8,16,1280]{2,1,0:T(8,128)(2,1)S(1)}, u32[]{:S(2)}, u32[]{:S(2)}) async-start(bf16[8,16,1280]{2,1,0:T(8,128)(2,1)} %get-tuple-element.30), calls=%async_computation.1 | async-start | bytes 655360 | tf_op jit(solution)/shard_map/all_to_all | solution.py:129
  34.1 23.8 %collective-permute-start.3 = (bf16[256,1280]{1,0:T(8,128)(2,1)S(1)}, bf16[256,1280]{1,0:T(8,128)(2,1)S(1)}, u32[]{:S(2)}, u32[]{:S(2)}) collective-permute-start(bf16[256,1280]{1,0:T(8,128)(2,1)S(1)} %bitcast.74), channel_id=1, source_target_pairs={{0,128},{128,0},{256,384},{384,256},{1,129},{129,1},{257,385},{385... | collective-permute-start | bytes 1966088 | tf_op jit(solution)/shard_map/ppermute | solution.py:117
  45.7 5.1 %copy-start.5 = (bf16[1280,256]{1,0:T(8,128)(2,1)S(1)}, bf16[1280,256]{1,0:T(8,128)(2,1)}, u32[]{:S(2)}) copy-start(bf16[1280,256]{1,0:T(8,128)(2,1)} %copy-done.4) | copy-start | bytes 1966084
  45.7 10.3 %collective-permute-start.2 = (bf16[128,1280]{1,0:T(8,128)(2,1)S(1)}, bf16[128,1280]{1,0:T(8,128)(2,1)S(1)}, u32[]{:S(2)}, u32[]{:S(2)}) collective-permute-start(bf16[128,1280]{1,0:T(8,128)(2,1)S(1)} %bitcast.67), channel_id=1, source_target_pairs={{0,384},{384,0},{128,256},{256,128},{1,385},{385,1},{129,257},{257... | collective-permute-start | bytes 983048 | tf_op jit(solution)/shard_map/ppermute | solution.py:121
  50.8 5.8 %copy-start.2 = (bf16[1,1280,256]{2,1,0:T(8,128)(2,1)S(1)}, bf16[1,1280,256]{2,1,0:T(8,128)(2,1)}, u32[]{:S(2)}) copy-start(bf16[1,1280,256]{2,1,0:T(8,128)(2,1)} %param.12) | copy-start | bytes 1966084
  57.9 4.1 %collective-permute-start.4 = (bf16[256,1024]{1,0:T(8,128)(2,1)}, bf16[256,1024]{1,0:T(8,128)(2,1)}, u32[]{:S(2)}, u32[]{:S(2)}) collective-permute-start(bf16[256,1024]{1,0:T(8,128)(2,1)} %maximum_maximum_fusion), channel_id=1, source_target_pairs={{0,1},{1,0},{2,3},{3,2},{4,5},{5,4},{6,7},{7,6},{8,9},{9,8},{10,11... | collective-permute-start | bytes 1572872 | tf_op jit(solution)/shard_map/ppermute | solution.py:113
  66.1 22.8 %all-to-all-start.2 = ((bf16[16,16,1280]{2,1,0:T(8,128)(2,1)}), bf16[16,16,1280]{2,1,0:T(8,128)(2,1)}, u32[]{:S(2)}, u32[]{:S(2)}) async-start(bf16[16,16,1280]{2,1,0:T(8,128)(2,1)} %bitcast.77), calls=%async_computation.2 | async-start | bytes 1310720 | tf_op jit(solution)/shard_map/all_to_all | solution.py:133
  71.3 19.6 %collective-permute-start.5 = (bf16[128,1280]{1,0:T(8,128)(2,1)S(1)}, bf16[128,1280]{1,0:T(8,128)(2,1)}, u32[]{:S(2)}, u32[]{:S(2)}) collective-permute-start(bf16[128,1280]{1,0:T(8,128)(2,1)S(1)} %bitcast.72), channel_id=1, source_target_pairs={{0,128},{128,0},{256,384},{384,256},{1,129},{129,1},{257,385},{385... | collective-permute-start | bytes 983048 | tf_op jit(solution)/shard_map/ppermute | solution.py:117
  90.9 24.9 %all-to-all-start.3 = ((bf16[16,16,1280]{2,1,0:T(8,128)(2,1)}), bf16[16,16,1280]{2,1,0:T(8,128)(2,1)}, u32[]{:S(2)}, u32[]{:S(2)}) async-start(bf16[16,16,1280]{2,1,0:T(8,128)(2,1)} %shard_map.105), calls=%async_computation.3 | async-start | bytes 1310720 | tf_op jit(solution)/shard_map/all_to_all | solution.py:133
  99.1 10.9 %collective-permute-start.6 = (bf16[128,1280]{1,0:T(8,128)(2,1)S(1)}, bf16[128,1280]{1,0:T(8,128)(2,1)S(1)}, u32[]{:S(2)}, u32[]{:S(2)}) collective-permute-start(bf16[128,1280]{1,0:T(8,128)(2,1)S(1)} %collective-permute-done.2), channel_id=1, source_target_pairs={{0,128},{128,0},{256,384},{384,256},{1,129},{129,1},{257,385},{385... | collective-permute-start | bytes 983048 | tf_op jit(solution)/shard_map/ppermute | solution.py:117
  110.0 5.8 %copy-start.9 = (bf16[128,1280]{1,0:T(8,128)(2,1)}, bf16[128,1280]{1,0:T(8,128)(2,1)S(1)}, u32[]{:S(2)}) copy-start(bf16[128,1280]{1,0:T(8,128)(2,1)S(1)} %collective-permute-done.6) | copy-start | bytes 983044
  118.8 3.3 %copy-start.10 = (bf16[128,1280]{1,0:T(8,128)(2,1)S(1)}, bf16[128,1280]{1,0:T(8,128)(2,1)}, u32[]{:S(2)}) copy-start(bf16[128,1280]{1,0:T(8,128)(2,1)} %copy-done.9) | copy-start | bytes 983044
  118.8 4.3 %collective-permute-start.7 = (bf16[256,512]{1,0:T(8,128)(2,1)S(1)}, bf16[256,512]{1,0:T(8,128)(2,1)S(1)}, u32[]{:S(2)}, u32[]{:S(2)}) collective-permute-start(bf16[256,512]{1,0:T(8,128)(2,1)S(1)} %maximum_maximum_fusion.1), channel_id=1, source_target_pairs={{0,1},{1,0},{2,3},{3,2},{4,5},{5,4},{6,7},{7,6},{8,9},{9,8},{10,11... | collective-permute-start | bytes 786440 | tf_op jit(solution)/shard_map/ppermute | solution.py:113
  122.8 1.2 copy-start.8
  127.3 13.2 %collective-permute-start.8 = (bf16[128,1280]{1,0:T(8,128)(2,1)S(1)}, bf16[128,1280]{1,0:T(8,128)(2,1)S(1)}, u32[]{:S(2)}, u32[]{:S(2)}) collective-permute-start(bf16[128,1280]{1,0:T(8,128)(2,1)S(1)} %fusion.10), channel_id=1, source_target_pairs={{0,384},{384,0},{128,256},{256,128},{1,385},{385,1},{129,257},{257... | collective-permute-start | bytes 983048 | tf_op jit(solution)/shard_map/ppermute | solution.py:121
  131.6 11.1 %collective-permute-start.9 = (bf16[256,512]{1,0:T(8,128)(2,1)S(1)}, bf16[256,512]{1,0:T(8,128)(2,1)}, u32[]{:S(2)}, u32[]{:S(2)}) collective-permute-start(bf16[256,512]{1,0:T(8,128)(2,1)S(1)} %pad_maximum_fusion.1), channel_id=1, source_target_pairs={{0,128},{128,0},{256,384},{384,256},{1,129},{129,1},{257,385},{385... | collective-permute-start | bytes 786440 | tf_op jit(solution)/shard_map/ppermute | solution.py:117
  133.5 23.3 %collective-permute-start.10 = (bf16[256,1280]{1,0:T(8,128)(2,1)}, bf16[256,1280]{1,0:T(8,128)(2,1)}, u32[]{:S(2)}, u32[]{:S(2)}) collective-permute-start(bf16[256,1280]{1,0:T(8,128)(2,1)} %fusion), channel_id=1, source_target_pairs={{0,128},{128,0},{256,384},{384,256},{1,129},{129,1},{257,385},{385... | collective-permute-start | bytes 1966088 | tf_op jit(solution)/shard_map/ppermute | solution.py:117
  143.6 21.9 %all-to-all-start.4 = ((bf16[64,2,1280]{2,1,0:T(2,128)(2,1)}), bf16[64,2,1280]{2,1,0:T(2,128)(2,1)S(1)}, u32[]{:S(2)}, u32[]{:S(2)}) async-start(bf16[64,2,1280]{2,1,0:T(2,128)(2,1)} %reshape.44), calls=%async_computation.4 | async-start | bytes 655360 | tf_op jit(solution)/shard_map/all_to_all | solution.py:235
  (4 other events, 3.8 us)

commit v4 on v3

--- a/solution.py
+++ b/solution.py
@@ -183,19 +183,18 @@
         return beside(*[times(rows, w).astype(BF16) for w in (gate_w, up_w, gate_w_p, up_w_p)])
 
     crossed = cross(column)
-    part = stack(products(column), products(crossed))
+    part = stack(*in_order(products(column), products(crossed)))
+    rows0, rows1 = in_order(column, crossed)
     part, down_w_p = after(part, pair(down_w))
     sums = part.astype(F32) + swap(part).astype(F32)
     gate, up, gate_p, up_p = jnp.split(sums, 4, axis=1)
     hidden = (jax.nn.silu(gate) * up).astype(BF16)
     hidden_p = (jax.nn.silu(gate_p) * up_p).astype(BF16)
 
-    mine, theirs = slice(0, column_rows), slice(column_rows, None)
-
     def output_part(s):
         return times(hidden[s], down_w) + times(hidden_p[s], down_w_p)
 
-    partial = stack(*in_order(output_part(mine).astype(BF16), output_part(theirs).astype(BF16)))
+    partial = output_part(slice(None)).astype(BF16)
     partial, tokens_late, target_late = after(partial, tokens, target)
     own, chosen = pl.pallas_call(own_kernel, out_shape=(array(row_len, features), array(slot_count, row_len)))(
         ids, doc_lengths, tokens_late, target_late
@@ -203,16 +202,14 @@
     pieces = over_two_columns(partial.reshape(2 * NY, slot_count, features))
     pieces, own, chosen = after(pieces, own, chosen)
     blocks = pl.pallas_call(settle_kernel, out_shape=array(2 * NY, slot_count, features))(pieces, my_rows, my_target)
-    blocks, pair_column = after(blocks, pair(column))
+    blocks, pair_column = after(blocks, pair(rows0))
 
     both = over_two_columns(blocks).reshape(2 * column_rows, features)
-    both, pair_crossed = after(both, pair(crossed))
-    grad_column, grad_crossed = in_order(both[:column_rows], both[column_rows:])
-    part = stack(
-        *[beside(*[times_t(g, w).astype(BF16) for w in (down_w, down_w_p)]) for g in (grad_column, grad_crossed)]
-    )
+    both, pair_crossed = after(both, pair(rows1))
+    grad_column, _ = in_order(both[:column_rows], both[column_rows:])
+    part = beside(*[times_t(both, w).astype(BF16) for w in (down_w, down_w_p)])
     down_part, down_part_p = [
-        times_rows(h[:column_rows], grad_column) + times_rows(h[column_rows:], grad_crossed) for h in (hidden, hidden_p)
+        times_rows(h, both) for h in (hidden, hidden_p)
     ]
     sums = part.astype(F32) + swap(part).astype(F32)
     back, back_p = jnp.split(sums, 2, axis=1)
@@ -221,9 +218,13 @@
     gate_grad_p = (back_p * up_p * silu_slope(gate_p)).astype(BF16)
     up_grad_p = (back_p * jax.nn.silu(gate_p)).astype(BF16)
 
-    def input_part(s):
-        own = times_t(gate_grad[s], gate_w) + times_t(up_grad[s], up_w)
-        return own + times_t(gate_grad_p[s], gate_w_p) + times_t(up_grad_p[s], up_w_p)
+    in_grads = beside(gate_grad, up_grad, gate_grad_p, up_grad_p)
+    mine, theirs = in_order(in_grads[:column_rows], in_grads[column_rows:])
+
+    def input_part(grads):
+        grads = jnp.split(grads, 4, axis=1)
+        own = times_t(grads[0], gate_w) + times_t(grads[1], up_w)
+        return own + times_t(grads[2], gate_w_p) + times_t(grads[3], up_w_p)
 
     at_home = (jnp.arange(column_rows) // slot_count) == lax.axis_index("y")
     extra = jnp.where(at_home[:, None], grad_column.astype(F32), 0.0)
@@ -231,13 +232,13 @@
     partial, down_part_late = after(partial, down_part_p.astype(BF16))
     column_in = input_part(mine) + extra + cross(partial).astype(F32)
     pair_down = pair(down_part_late)
-    column_in, pair_in = after(column_in.astype(BF16), pair(beside(gate_grad_p, up_grad_p)))
+    column_in, pair_in = column_in.astype(BF16), pair(beside(gate_grad_p, up_grad_p))
     pieces = lax.all_to_all(column_in.reshape(NY * NZ, CAP, features), ("y", "z"), 0, 0, tiled=True)
     grad_tokens = pl.pallas_call(combine_kernel, out_shape=array(row_len, features))(
         own, chosen, pieces.reshape(NY, slot_count, features)
     )
 
-    rows = stack(column, crossed, pair_column, pair_crossed)
+    rows = stack(rows0, rows1, pair_column, pair_crossed)
     grad_down = (down_part + pair_down.astype(F32)).astype(BF16)
     grad_gate = weight_grad(rows, stack(gate_grad, pair_in[:, :units]))
     grad_up = weight_grad(rows, stack(up_grad, pair_in[:, units:]))

time: 170 us -> 166 us (0.976)
  local copies, waits for them, and re-layouts: 9.42 us -> 5.07 us
  other arithmetic: 4.78 us -> 2.54 us
    ppermute x7, waiting for transfers between devices: 8.34 us -> 16 us  [pair(): return lax.ppermute(value, 'x', PAIR)]
    all_to_all x1, waiting for transfers between devices: 6.45 us -> 0.68 us  [local(): lax.all_to_all(column_in.reshape(NY * NZ, CAP, features), ('y', 'z'), 0,...]
    unnamed x27 -> x24, local copies, waits for them, and re-layouts: 6 us -> 2.39 us
    concatenate x3 -> x1, other arithmetic: 1.76 us -> 0.04 us  [stack(): return jnp.concatenate(parts, axis=0)]
    all_to_all x1, starting transfers between devices: 6.79 us -> 8.5 us  [local(): lax.all_to_all(column_in.reshape(NY * NZ, CAP, features), ('y', 'z'), 0,...]
    dot_general x6 -> x4, matrix products: 9.59 us -> 8.45 us  [times_rows(): lax.dot_general(left, right, CONTRACT_ROWS, preferred_element_type=F32)]
    dot_general x12 -> x10, matrix products: 4.42 us -> 4.92 us  [times_t(): lax.dot_general(left, right, CONTRACT_COLS, preferred_element_type=F32)]
    dot_general x12 -> x10, matrix products: 4.17 us -> 4.66 us  [times(): return jnp.dot(left, right, preferred_element_type=F32)]
  transfers between devices with their start and end apart: 16 -> 16, of which waited for: 10 -> 11; matrix products, arithmetic and copies ran while one was open for 12% -> 9% of each run, Pallas kernels for 5% -> 5%
where the time goes in v4:
time: 166 us; the launch traced here: 165 us
  starting transfers between devices  68.6 us (41%)
  waiting for transfers between devices  59.1 us (36%)
  matrix products  18 us (11%)
  Pallas kernels  10.4 us (6%)
  local copies, waits for them, and re-layouts  5.07 us (3%)
  other arithmetic  2.54 us (2%)
    ppermute x7, starting transfers between devices, pair(): return lax.ppermute(value, 'x', PAIR)  18.7 us
    all_to_all x2, waiting for transfers between devices, over_two_columns(): lax.all_to_all(blocks, ('x', 'y'), 0, 0, axis_index_groups=TWO_COLUMNS, t...  18.6 us
    ppermute x7, waiting for transfers between devices, pair(): return lax.ppermute(value, 'x', PAIR)  16 us
    all_to_all x2, starting transfers between devices, over_two_columns(): lax.all_to_all(blocks, ('x', 'y'), 0, 0, axis_index_groups=TWO_COLUMNS, t...  12.6 us
    all_to_all x1, starting transfers between devices, local(): arrived = lax.all_to_all(message, 'z', 0, 0, tiled=True)  10.3 us
    all_to_all x1, starting transfers between devices, local(): lax.all_to_all(column_in.reshape(NY * NZ, CAP, features), ('y', 'z'), 0,...  8.5 us
    all_to_all x1, waiting for transfers between devices, over_y(): return lax.all_to_all(blocks, 'y', 0, 0, tiled=True)  8.46 us
    dot_general x4, matrix products, times_rows(): lax.dot_general(left, right, CONTRACT_ROWS, preferred_element_type=F32)  8.45 us
  transfers between devices with their start and end apart: 16, of which 11 were waited for; matrix products, arithmetic and copies ran while one was open for 9% of the time, Pallas kernels for 5%

profile of v4, /device:TPU:6, one launch (start us, length us, event | category | flops | bytes accessed | tf_op | source)
XLA Modules:
  0.0 164.8 jit_solution(889046367476666772)
XLA Ops:
  0.6 2.9 %collective-permute-start = (bf16[1280,256]{1,0:T(8,128)(2,1)}, bf16[1280,256]{1,0:T(8,128)(2,1)S(1)}, u32[]{:S(2)}, u32[]{:S(2)}) collective-permute-start(bf16[1280,256]{1,0:T(8,128)(2,1)} %bitcast.70), channel_id=1, source_target_pairs={{0,128},{128,0},{256,384},{384,256},{1,129},{129,1},{257,385},{385... | collective-permute-start | bytes 1966088 | tf_op jit(solution)/shard_map/ppermute | solution.py:117
  3.5 2.2 %shard_map.102 = bf16[8,8,640]{2,1,0:T(8,128)(2,1)} custom-call(s32[1,128]{1,0:T(1,128)} %bitcast.74, s32[1,8]{1,0:T(1,128)} %lengths_ref.3, bf16[128,1280]{1,0:T(8,128)(2,1)} %tokens_ref.2, bf16[128,1280]{1,0:T(8,128)(2,1)} %target_ref.2), custom_call_target="tpu_custom_call" | custom-call | tf_op jit(solution)/shard_map/pallas_call | solution.py:169
  5.7 10.3 %all-to-all-start = ((bf16[8,8,640]{2,1,0:T(8,128)(2,1)}), bf16[8,8,640]{2,1,0:T(8,128)(2,1)S(1)}, u32[]{:S(2)}, u32[]{:S(2)}) async-start(bf16[8,8,640]{2,1,0:T(8,128)(2,1)} %shard_map.102), calls=%async_computation | async-start | bytes 163840 | tf_op jit(solution)/shard_map/all_to_all | solution.py:172
  16.0 3.1 %collective-permute-start.1 = (bf16[1280,256]{1,0:T(8,128)(2,1)}, bf16[1280,256]{1,0:T(8,128)(2,1)S(1)}, u32[]{:S(2)}, u32[]{:S(2)}) collective-permute-start(bf16[1280,256]{1,0:T(8,128)(2,1)} %bitcast.71), channel_id=1, source_target_pairs={{0,128},{128,0},{256,384},{384,256},{1,129},{129,1},{257,385},{385... | collective-permute-start | bytes 1966088 | tf_op jit(solution)/shard_map/ppermute | solution.py:117
  19.1 5.5 %all-to-all-done.arrived_ref = bf16[8,8,640]{2,1,0:T(8,128)(2,1)S(1)} async-done(((bf16[8,8,640]{2,1,0:T(8,128)(2,1)}), bf16[8,8,640]{2,1,0:T(8,128)(2,1)S(1)}, u32[]{:S(2)}, u32[]{:S(2)}) %all-to-all-start) | async-done | bytes 81952 | tf_op jit(solution)/shard_map/all_to_all | solution.py:172
  27.0 7.1 %all-to-all-start.1 = ((bf16[8,16,1280]{2,1,0:T(8,128)(2,1)}), bf16[8,16,1280]{2,1,0:T(8,128)(2,1)S(1)}, u32[]{:S(2)}, u32[]{:S(2)}) async-start(bf16[8,16,1280]{2,1,0:T(8,128)(2,1)} %get-tuple-element.28), calls=%async_computation.1 | async-start | bytes 655360 | tf_op jit(solution)/shard_map/all_to_all | solution.py:129
  34.1 3.1 %collective-permute-start.3 = (bf16[256,1280]{1,0:T(8,128)(2,1)}, bf16[256,1280]{1,0:T(8,128)(2,1)}, u32[]{:S(2)}, u32[]{:S(2)}) collective-permute-start(bf16[256,1280]{1,0:T(8,128)(2,1)} %bitcast.72), channel_id=1, source_target_pairs={{0,128},{128,0},{256,384},{384,256},{1,129},{129,1},{257,385},{385... | collective-permute-start | bytes 1966088 | tf_op jit(solution)/shard_map/ppermute | solution.py:117
  37.2 8.5 %all-to-all-done.1 = bf16[8,16,1280]{2,1,0:T(8,128)(2,1)S(1)} async-done(((bf16[8,16,1280]{2,1,0:T(8,128)(2,1)}), bf16[8,16,1280]{2,1,0:T(8,128)(2,1)S(1)}, u32[]{:S(2)}, u32[]{:S(2)}) %all-to-all-start.1) | async-done | bytes 327712 | tf_op jit(solution)/shard_map/all_to_all | solution.py:129
  45.7 3.0 %collective-permute-start.2 = (bf16[128,1280]{1,0:T(8,128)(2,1)S(1)}, bf16[128,1280]{1,0:T(8,128)(2,1)S(1)}, u32[]{:S(2)}, u32[]{:S(2)}) collective-permute-start(bf16[128,1280]{1,0:T(8,128)(2,1)S(1)} %bitcast.64), channel_id=1, source_target_pairs={{0,384},{384,0},{128,256},{256,128},{1,385},{385,1},{129,257},{257... | collective-permute-start | bytes 983048 | tf_op jit(solution)/shard_map/ppermute | solution.py:121
  49.8 6.0 %collective-permute-done.2 = bf16[128,1280]{1,0:T(8,128)(2,1)S(1)} collective-permute-done((bf16[128,1280]{1,0:T(8,128)(2,1)S(1)}, bf16[128,1280]{1,0:T(8,128)(2,1)S(1)}, u32[]{:S(2)}, u32[]{:S(2)}) %collective-permute-start.2) | collective-permute-done | bytes 327712 | tf_op jit(solution)/shard_map/ppermute | solution.py:121
  62.2 2.3 %fusion = bf16[256,1280]{1,0:T(8,128)(2,1)} fusion(f32[256,1280]{1,0:T(8,128)S(1)} %fusion.35, bf16[256,256]{1,0:T(8,128)(2,1)S(1)} %get-tuple-element.54, bf16[256,1280]{1,0:T(8,128)(2,1)} %collective-permute-done.3), kind=kOutput, calls=%fused_computation.2 | convolution fusion | flops 168427520 | bytes 2752512 | tf_op jit(solution)/shard_map/dot_general | solution.py:142
  64.4 5.2 %all-to-all-start.2 = ((bf16[16,16,1280]{2,1,0:T(8,128)(2,1)}), bf16[16,16,1280]{2,1,0:T(8,128)(2,1)}, u32[]{:S(2)}, u32[]{:S(2)}) async-start(bf16[16,16,1280]{2,1,0:T(8,128)(2,1)} %bitcast.73), calls=%async_computation.2 | async-start | bytes 1310720 | tf_op jit(solution)/shard_map/all_to_all | solution.py:133
  72.4 2.3 %shard_map.104 = (bf16[128,1280]{1,0:T(8,128)(2,1)}, bf16[16,128]{1,0:T(8,128)(2,1)}) custom-call(s32[1,128]{1,0:T(1,128)} %bitcast.75, s32[1,8]{1,0:T(1,128)} %lengths_ref.3, bf16[128,1280]{1,0:T(8,128)(2,1)} %tokens_ref.2, bf16[128,1280]{1,0:T(8,128)(2,1)} %target_ref.2), custom_call_target="tpu_custom_call" | custom-call | tf_op jit(solution)/shard_map/pallas_call | solution.py:199
  74.7 12.5 %all-to-all-done.2.pieces_ref = bf16[16,16,1280]{2,1,0:T(8,128)(2,1)} async-done(((bf16[16,16,1280]{2,1,0:T(8,128)(2,1)}), bf16[16,16,1280]{2,1,0:T(8,128)(2,1)}, u32[]{:S(2)}, u32[]{:S(2)}) %all-to-all-start.2) | async-done | bytes 655392 | tf_op jit(solution)/shard_map/all_to_all | solution.py:133
  90.0 7.4 %all-to-all-start.3 = ((bf16[16,16,1280]{2,1,0:T(8,128)(2,1)}), bf16[16,16,1280]{2,1,0:T(8,128)(2,1)S(1)}, u32[]{:S(2)}, u32[]{:S(2)}) async-start(bf16[16,16,1280]{2,1,0:T(8,128)(2,1)} %shard_map.105), calls=%async_computation.3 | async-start | bytes 1310720 | tf_op jit(solution)/shard_map/all_to_all | solution.py:133
  99.3 9.3 %collective-permute-done.6 = bf16[128,1280]{1,0:T(8,128)(2,1)} collective-permute-done((bf16[128,1280]{1,0:T(8,128)(2,1)}, bf16[128,1280]{1,0:T(8,128)(2,1)}, u32[]{:S(2)}, u32[]{:S(2)}) %collective-permute-start.6) | collective-permute-done | bytes 327712 | tf_op jit(solution)/shard_map/ppermute | solution.py:117
  108.7 6.1 %all-to-all-done.3 = bf16[16,16,1280]{2,1,0:T(8,128)(2,1)S(1)} async-done(((bf16[16,16,1280]{2,1,0:T(8,128)(2,1)}), bf16[16,16,1280]{2,1,0:T(8,128)(2,1)S(1)}, u32[]{:S(2)}, u32[]{:S(2)}) %all-to-all-start.3) | async-done | bytes 655392 | tf_op jit(solution)/shard_map/all_to_all | solution.py:133
  123.6 4.3 %collective-permute-start.8 = (bf16[128,1280]{1,0:T(8,128)(2,1)S(1)}, bf16[128,1280]{1,0:T(8,128)(2,1)S(1)}, u32[]{:S(2)}, u32[]{:S(2)}) collective-permute-start(bf16[128,1280]{1,0:T(8,128)(2,1)S(1)} %fusion.10), channel_id=1, source_target_pairs={{0,384},{384,0},{128,256},{256,128},{1,385},{385,1},{129,257},{257... | collective-permute-start | bytes 983048 | tf_op jit(solution)/shard_map/ppermute | solution.py:121
  130.5 3.9 %collective-permute-start.9 = (bf16[256,512]{1,0:T(8,128)(2,1)}, bf16[256,512]{1,0:T(8,128)(2,1)}, u32[]{:S(2)}, u32[]{:S(2)}) collective-permute-start(bf16[256,512]{1,0:T(8,128)(2,1)} %pad_maximum_fusion.6), channel_id=1, source_target_pairs={{0,128},{128,0},{256,384},{384,256},{1,129},{129,1},{257,385},{385... | collective-permute-start | bytes 786440 | tf_op jit(solution)/shard_map/ppermute | solution.py:117
  137.8 8.5 %all-to-all-start.4 = ((bf16[64,2,1280]{2,1,0:T(2,128)(2,1)}), bf16[64,2,1280]{2,1,0:T(2,128)(2,1)S(1)}, u32[]{:S(2)}, u32[]{:S(2)}) async-start(bf16[64,2,1280]{2,1,0:T(2,128)(2,1)} %reshape.44), calls=%async_computation.4 | async-start | bytes 655360 | tf_op jit(solution)/shard_map/all_to_all | solution.py:236
  146.3 6.6 %collective-permute-done.9 = bf16[256,512]{1,0:T(8,128)(2,1)} collective-permute-done((bf16[256,512]{1,0:T(8,128)(2,1)}, bf16[256,512]{1,0:T(8,128)(2,1)}, u32[]{:S(2)}, u32[]{:S(2)}) %collective-permute-start.9) | collective-permute-done | bytes 262176 | tf_op jit(solution)/shard_map/ppermute | solution.py:117
  154.0 2.5 %fusion.7 = bf16[1,1280,256]{2,1,0:T(8,128)(2,1)} fusion(bf16[256,256]{1,0:T(8,128)(2,1)S(1)} %get-tuple-element.62, bf16[256,256]{1,0:T(8,128)(2,1)S(1)} %copy-done.7, bf16[128,1280]{1,0:T(8,128)(2,1)} %collective-permute-done.6, bf16[128,1280]{1,0:T(8,128)(2,1)S(1)} %copy-done.11, bf16[128,1280]{1,0:T(8,128)(2,1)S(1)} %copy-done.9, ...), kind=kOutput, calls=%fused_computation.16 | convolution fusion | flops 341639168 | bytes 2228224 | tf_op jit(solution)/shard_map/dot_general | solution.py:105
  156.5 2.5 %fusion.6 = bf16[1,1280,256]{2,1,0:T(8,128)(2,1)} fusion(bf16[256,256]{1,0:T(8,128)(2,1)S(1)} %get-tuple-element.63, bf16[256,256]{1,0:T(8,128)(2,1)S(1)} %get-tuple-element.50, bf16[128,1280]{1,0:T(8,128)(2,1)} %collective-permute-done.6, bf16[128,1280]{1,0:T(8,128)(2,1)S(1)} %copy-done.11, bf16[128,1280]{1,0:T(8,128)(2,1)S(1)} %copy-done.9, ...), kind=kOutput, calls=%fused_computation.15 | convolution fusion | flops 341639168 | bytes 2228224 | tf_op jit(solution)/shard_map/dot_general | solution.py:105
  158.9 2.3 %fusion.8 = bf16[1,256,1280]{2,1,0:T(8,128)(2,1)} fusion(bf16[256,256]{1,0:T(8,128)(2,1)S(1)} %get-tuple-element.55, bf16[256,1280]{1,0:T(8,128)(2,1)S(1)} %bitcast.63, bf16[256,1280]{1,0:T(8,128)(2,1)} %collective-permute-done.10), kind=kOutput, calls=%fused_computation.17 | convolution fusion | flops 168755200 | bytes 2097152 | tf_op jit(solution)/shard_map/dot_general | solution.py:105
  (76 shorter events, 36.5 us)
Async XLA Ops:
  0.6 48.1 %copy-start.1 = (bf16[1,1280,256]{2,1,0:T(8,128)(2,1)S(1)}, bf16[1,1280,256]{2,1,0:T(8,128)(2,1)}, u32[]{:S(2)}) copy-start(bf16[1,1280,256]{2,1,0:T(8,128)(2,1)} %param.12) | copy-start | bytes 1966084
  0.6 26.4 %collective-permute-start = (bf16[1280,256]{1,0:T(8,128)(2,1)}, bf16[1280,256]{1,0:T(8,128)(2,1)S(1)}, u32[]{:S(2)}, u32[]{:S(2)}) collective-permute-start(bf16[1280,256]{1,0:T(8,128)(2,1)} %bitcast.70), channel_id=1, source_target_pairs={{0,128},{128,0},{256,384},{384,256},{1,129},{129,1},{257,385},{385... | collective-permute-start | bytes 1966088 | tf_op jit(solution)/shard_map/ppermute | solution.py:117
  3.5 45.5 %copy-start = (bf16[1,1280,256]{2,1,0:T(8,128)(2,1)S(1)}, bf16[1,1280,256]{2,1,0:T(8,128)(2,1)}, u32[]{:S(2)}) copy-start(bf16[1,1280,256]{2,1,0:T(8,128)(2,1)} %param.11) | copy-start | bytes 1966084
  5.7 18.9 %all-to-all-start = ((bf16[8,8,640]{2,1,0:T(8,128)(2,1)}), bf16[8,8,640]{2,1,0:T(8,128)(2,1)S(1)}, u32[]{:S(2)}, u32[]{:S(2)}) async-start(bf16[8,8,640]{2,1,0:T(8,128)(2,1)} %shard_map.102), calls=%async_computation | async-start | bytes 163840 | tf_op jit(solution)/shard_map/all_to_all | solution.py:172
  16.0 21.2 %collective-permute-start.1 = (bf16[1280,256]{1,0:T(8,128)(2,1)}, bf16[1280,256]{1,0:T(8,128)(2,1)S(1)}, u32[]{:S(2)}, u32[]{:S(2)}) collective-permute-start(bf16[1280,256]{1,0:T(8,128)(2,1)} %bitcast.71), channel_id=1, source_target_pairs={{0,128},{128,0},{256,384},{384,256},{1,129},{129,1},{257,385},{385... | collective-permute-start | bytes 1966088 | tf_op jit(solution)/shard_map/ppermute | solution.py:117
  27.0 18.7 %all-to-all-start.1 = ((bf16[8,16,1280]{2,1,0:T(8,128)(2,1)}), bf16[8,16,1280]{2,1,0:T(8,128)(2,1)S(1)}, u32[]{:S(2)}, u32[]{:S(2)}) async-start(bf16[8,16,1280]{2,1,0:T(8,128)(2,1)} %get-tuple-element.28), calls=%async_computation.1 | async-start | bytes 655360 | tf_op jit(solution)/shard_map/all_to_all | solution.py:129
  34.1 23.0 %collective-permute-start.3 = (bf16[256,1280]{1,0:T(8,128)(2,1)}, bf16[256,1280]{1,0:T(8,128)(2,1)}, u32[]{:S(2)}, u32[]{:S(2)}) collective-permute-start(bf16[256,1280]{1,0:T(8,128)(2,1)} %bitcast.72), channel_id=1, source_target_pairs={{0,128},{128,0},{256,384},{384,256},{1,129},{129,1},{257,385},{385... | collective-permute-start | bytes 1966088 | tf_op jit(solution)/shard_map/ppermute | solution.py:117
  45.7 10.2 %collective-permute-start.2 = (bf16[128,1280]{1,0:T(8,128)(2,1)S(1)}, bf16[128,1280]{1,0:T(8,128)(2,1)S(1)}, u32[]{:S(2)}, u32[]{:S(2)}) collective-permute-start(bf16[128,1280]{1,0:T(8,128)(2,1)S(1)} %bitcast.64), channel_id=1, source_target_pairs={{0,384},{384,0},{128,256},{256,128},{1,385},{385,1},{129,257},{257... | collective-permute-start | bytes 983048 | tf_op jit(solution)/shard_map/ppermute | solution.py:121
  57.1 4.3 %copy-start.4 = (bf16[1,256,1280]{2,1,0:T(8,128)(2,1)S(1)}, bf16[1,256,1280]{2,1,0:T(8,128)(2,1)}, u32[]{:S(2)}) copy-start(bf16[1,256,1280]{2,1,0:T(8,128)(2,1)} %param.13) | copy-start | bytes 1966084
  57.1 3.9 %collective-permute-start.4 = (bf16[256,1024]{1,0:T(8,128)(2,1)S(1)}, bf16[256,1024]{1,0:T(8,128)(2,1)S(1)}, u32[]{:S(2)}, u32[]{:S(2)}) collective-permute-start(bf16[256,1024]{1,0:T(8,128)(2,1)S(1)} %pad_maximum_fusion.1), channel_id=1, source_target_pairs={{0,1},{1,0},{2,3},{3,2},{4,5},{5,4},{6,7},{7,6},{8,9},{9,8},{10,11... | collective-permute-start | bytes 1572872 | tf_op jit(solution)/shard_map/ppermute | solution.py:113
  64.4 22.7 %all-to-all-start.2 = ((bf16[16,16,1280]{2,1,0:T(8,128)(2,1)}), bf16[16,16,1280]{2,1,0:T(8,128)(2,1)}, u32[]{:S(2)}, u32[]{:S(2)}) async-start(bf16[16,16,1280]{2,1,0:T(8,128)(2,1)} %bitcast.73), calls=%async_computation.2 | async-start | bytes 1310720 | tf_op jit(solution)/shard_map/all_to_all | solution.py:133
  70.5 18.8 %collective-permute-start.5 = (bf16[128,1280]{1,0:T(8,128)(2,1)}, bf16[128,1280]{1,0:T(8,128)(2,1)S(1)}, u32[]{:S(2)}, u32[]{:S(2)}) collective-permute-start(bf16[128,1280]{1,0:T(8,128)(2,1)} %get-tuple-element.57), channel_id=1, source_target_pairs={{0,128},{128,0},{256,384},{384,256},{1,129},{129,1},{257,385},{385... | collective-permute-start | bytes 983048 | tf_op jit(solution)/shard_map/ppermute | solution.py:117
  90.0 24.8 %all-to-all-start.3 = ((bf16[16,16,1280]{2,1,0:T(8,128)(2,1)}), bf16[16,16,1280]{2,1,0:T(8,128)(2,1)S(1)}, u32[]{:S(2)}, u32[]{:S(2)}) async-start(bf16[16,16,1280]{2,1,0:T(8,128)(2,1)} %shard_map.105), calls=%async_computation.3 | async-start | bytes 1310720 | tf_op jit(solution)/shard_map/all_to_all | solution.py:133
  97.4 11.3 %collective-permute-start.6 = (bf16[128,1280]{1,0:T(8,128)(2,1)}, bf16[128,1280]{1,0:T(8,128)(2,1)}, u32[]{:S(2)}, u32[]{:S(2)}) collective-permute-start(bf16[128,1280]{1,0:T(8,128)(2,1)} %get-tuple-element.56), channel_id=1, source_target_pairs={{0,128},{128,0},{256,384},{384,256},{1,129},{129,1},{257,385},{385... | collective-permute-start | bytes 983048 | tf_op jit(solution)/shard_map/ppermute | solution.py:117
  114.8 1.5 copy-start.5
  116.7 3.6 %copy-start.3 = (f32[256,1024]{1,0:T(8,128)S(1)}, f32[256,1024]{1,0:T(8,128)}, u32[]{:S(2)}) copy-start(f32[256,1024]{1,0:T(8,128)} %copy-done.2) | copy-start | bytes 3145732
  116.7 3.6 %collective-permute-start.7 = (bf16[256,512]{1,0:T(8,128)(2,1)S(1)}, bf16[256,512]{1,0:T(8,128)(2,1)S(1)}, u32[]{:S(2)}, u32[]{:S(2)}) collective-permute-start(bf16[256,512]{1,0:T(8,128)(2,1)S(1)} %pad_maximum_fusion.5), channel_id=1, source_target_pairs={{0,1},{1,0},{2,3},{3,2},{4,5},{5,4},{6,7},{7,6},{8,9},{9,8},{10,11... | collective-permute-start | bytes 786440 | tf_op jit(solution)/shard_map/ppermute | solution.py:113
  123.6 12.9 %collective-permute-start.8 = (bf16[128,1280]{1,0:T(8,128)(2,1)S(1)}, bf16[128,1280]{1,0:T(8,128)(2,1)S(1)}, u32[]{:S(2)}, u32[]{:S(2)}) collective-permute-start(bf16[128,1280]{1,0:T(8,128)(2,1)S(1)} %fusion.10), channel_id=1, source_target_pairs={{0,384},{384,0},{128,256},{256,128},{1,385},{385,1},{129,257},{257... | collective-permute-start | bytes 983048 | tf_op jit(solution)/shard_map/ppermute | solution.py:121
  128.6 30.4 %collective-permute-start.10 = (bf16[256,1280]{1,0:T(8,128)(2,1)}, bf16[256,1280]{1,0:T(8,128)(2,1)}, u32[]{:S(2)}, u32[]{:S(2)}) collective-permute-start(bf16[256,1280]{1,0:T(8,128)(2,1)} %convolution_convert_fusion.2), channel_id=1, source_target_pairs={{0,128},{128,0},{256,384},{384,256},{1,129},{129,1},{257,385},{385... | collective-permute-start | bytes 1966088 | tf_op jit(solution)/shard_map/ppermute | solution.py:117
  130.5 22.5 %collective-permute-start.9 = (bf16[256,512]{1,0:T(8,128)(2,1)}, bf16[256,512]{1,0:T(8,128)(2,1)}, u32[]{:S(2)}, u32[]{:S(2)}) collective-permute-start(bf16[256,512]{1,0:T(8,128)(2,1)} %pad_maximum_fusion.6), channel_id=1, source_target_pairs={{0,128},{128,0},{256,384},{384,256},{1,129},{129,1},{257,385},{385... | collective-permute-start | bytes 786440 | tf_op jit(solution)/shard_map/ppermute | solution.py:117
  136.9 17.0 %copy-start.7 = (bf16[256,256]{1,0:T(8,128)(2,1)S(1)}, bf16[256,256]{1,0:T(8,128)(2,1)}, u32[]{:S(2)}) copy-start(bf16[256,256]{1,0:T(8,128)(2,1)} %copy-done.6) | copy-start | bytes 393220
  137.0 17.0 %copy-start.9 = (bf16[128,1280]{1,0:T(8,128)(2,1)S(1)}, bf16[128,1280]{1,0:T(8,128)(2,1)}, u32[]{:S(2)}) copy-start(bf16[128,1280]{1,0:T(8,128)(2,1)} %get-tuple-element.56) | copy-start | bytes 983044
  137.0 17.0 %copy-start.11 = (bf16[128,1280]{1,0:T(8,128)(2,1)S(1)}, bf16[128,1280]{1,0:T(8,128)(2,1)}, u32[]{:S(2)}) copy-start(bf16[128,1280]{1,0:T(8,128)(2,1)} %copy-done.10) | copy-start | bytes 983044
  137.8 24.1 %all-to-all-start.4 = ((bf16[64,2,1280]{2,1,0:T(2,128)(2,1)}), bf16[64,2,1280]{2,1,0:T(2,128)(2,1)S(1)}, u32[]{:S(2)}, u32[]{:S(2)}) async-start(bf16[64,2,1280]{2,1,0:T(2,128)(2,1)} %reshape.44), calls=%async_computation.4 | async-start | bytes 655360 | tf_op jit(solution)/shard_map/all_to_all | solution.py:236
  (4 other events, 3.0 us)

commit v5 on v4

--- a/solution.py
+++ b/solution.py
@@ -74,15 +74,6 @@
     blocks_ref[...] = jnp.broadcast_to(mine[None], blocks_ref.shape)
 
 
-def settle_kernel(pieces_ref, rows_ref, target_ref, blocks_ref):
-    total = pieces_ref[0].astype(F32)
-    for i in range(1, pieces_ref.shape[0]):
-        total += pieces_ref[i].astype(F32)
-    output = rows_ref[...].astype(F32) + total.astype(BF16).astype(F32)
-    residual = (output - target_ref[...].astype(F32)).astype(BF16)
-    blocks_ref[...] = jnp.broadcast_to(residual[None], blocks_ref.shape)
-
-
 def own_kernel(ids_ref, lengths_ref, tokens_ref, target_ref, own_ref, chosen_ref):
     row_len = tokens_ref.shape[0]
     chosen = one_hot(slot_matrix(ids_ref[...], lengths_ref[...], chosen_ref.shape[0], CAP))
@@ -93,14 +84,6 @@
     chosen_ref[...] = chosen
 
 
-def combine_kernel(own_ref, chosen_ref, pieces_ref, out_ref):
-    slots = pieces_ref[0].astype(F32)
-    for i in range(1, pieces_ref.shape[0]):
-        slots += pieces_ref[i].astype(F32)
-    routed = times_rows(chosen_ref[...], slots.astype(BF16))
-    out_ref[...] = (own_ref[...].astype(F32) + routed).astype(BF16)
-
-
 def times_rows(left, right):
     return lax.dot_general(left, right, CONTRACT_ROWS, preferred_element_type=F32)
 
@@ -201,7 +184,9 @@
     )
     pieces = over_two_columns(partial.reshape(2 * NY, slot_count, features))
     pieces, own, chosen = after(pieces, own, chosen)
-    blocks = pl.pallas_call(settle_kernel, out_shape=array(2 * NY, slot_count, features))(pieces, my_rows, my_target)
+    expert_rows = jnp.sum(pieces.astype(F32), axis=0).astype(BF16)
+    residual = (my_rows.astype(F32) + expert_rows.astype(F32) - my_target.astype(F32)).astype(BF16)
+    blocks = jnp.broadcast_to(residual[None], pieces.shape)
     blocks, pair_column = after(blocks, pair(rows0))
 
     both = over_two_columns(blocks).reshape(2 * column_rows, features)
@@ -229,19 +214,23 @@
     at_home = (jnp.arange(column_rows) // slot_count) == lax.axis_index("y")
     extra = jnp.where(at_home[:, None], grad_column.astype(F32), 0.0)
     partial = input_part(theirs).astype(BF16)
-    partial, down_part_late = after(partial, down_part_p.astype(BF16))
+    half = features // 2
+    partial, first, second = after(
+        partial,
+        beside(gate_grad_p, up_grad_p, down_part_p[:, :half].astype(BF16)),
+        down_part_p[:, half:].astype(BF16),
+    )
     column_in = input_part(mine) + extra + cross(partial).astype(F32)
-    pair_down = pair(down_part_late)
-    column_in, pair_in = column_in.astype(BF16), pair(beside(gate_grad_p, up_grad_p))
+    column_in, pair_in, pair_rest = column_in.astype(BF16), pair(first), pair(second)
     pieces = lax.all_to_all(column_in.reshape(NY * NZ, CAP, features), ("y", "z"), 0, 0, tiled=True)
-    grad_tokens = pl.pallas_call(combine_kernel, out_shape=array(row_len, features))(
-        own, chosen, pieces.reshape(NY, slot_count, features)
-    )
+    slots = jnp.sum(pieces.reshape(NY, slot_count, features).astype(F32), axis=0).astype(BF16)
+    grad_tokens = (own.astype(F32) + times_rows(chosen, slots)).astype(BF16)
 
     rows = stack(rows0, rows1, pair_column, pair_crossed)
+    pair_down = beside(pair_in[:, 2 * units :], pair_rest)
     grad_down = (down_part + pair_down.astype(F32)).astype(BF16)
     grad_gate = weight_grad(rows, stack(gate_grad, pair_in[:, :units]))
-    grad_up = weight_grad(rows, stack(up_grad, pair_in[:, units:]))
+    grad_up = weight_grad(rows, stack(up_grad, pair_in[:, units : 2 * units]))
     return (grad_tokens, grad_gate[None], grad_up[None], grad_down[None])
 
 

time: 166 us -> 165 us (level)
  Pallas kernels: 10.4 us -> 6.22 us
    all_to_all x1, waiting for transfers between devices: 0.68 us -> 7.48 us  [local(): lax.all_to_all(column_in.reshape(NY * NZ, CAP, features), ('y', 'z'), 0,...]
    ppermute x7, waiting for transfers between devices: 16 us -> 9.5 us  [pair(): return lax.ppermute(value, 'x', PAIR)]
    pallas_call x2 -> x0, Pallas kernels: 4.14 us -> none  [the longest x1 2.07 us: local(): pl.pallas_call(combine_kernel, out_shape=array(row_len, features))]
    slice x1 -> x3, local copies, waits for them, and re-layouts: 0.99 us -> 2.77 us  [the longest x1 1 us: local(): pair_down = beside(pair_in[:, 2 * units:], pair_rest)]
    dot_general x4 -> x5, matrix products: 8.45 us -> 7.53 us  [times_rows(): lax.dot_general(left, right, CONTRACT_ROWS, preferred_element_type=F32)]
  transfers between devices with their start and end apart: 16 -> 16, of which waited for: 11 -> 11; matrix products, arithmetic and copies ran while one was open for 9% -> 10% of each run, Pallas kernels for 5% -> 4%
where the time goes in v5:
time: 165 us; the launch traced here: 163 us
  starting transfers between devices  68.1 us (41%)
  waiting for transfers between devices  60.5 us (37%)
  matrix products  17.1 us (10%)
  Pallas kernels  6.22 us (4%)
  local copies, waits for them, and re-layouts  6.16 us (4%)
  other arithmetic  3.97 us (2%)
    ppermute x7, starting transfers between devices, pair(): return lax.ppermute(value, 'x', PAIR)  18.8 us
    all_to_all x2, waiting for transfers between devices, over_two_columns(): lax.all_to_all(blocks, ('x', 'y'), 0, 0, axis_index_groups=TWO_COLUMNS, t...  18.5 us
    all_to_all x2, starting transfers between devices, over_two_columns(): lax.all_to_all(blocks, ('x', 'y'), 0, 0, axis_index_groups=TWO_COLUMNS, t...  12.6 us
    all_to_all x1, starting transfers between devices, local(): arrived = lax.all_to_all(message, 'z', 0, 0, tiled=True)  10.3 us
    ppermute x7, waiting for transfers between devices, pair(): return lax.ppermute(value, 'x', PAIR)  9.5 us
    ppermute x2, waiting for transfers between devices, cross(): return lax.ppermute(value, 'x', CROSS)  8.94 us
    all_to_all x1, waiting for transfers between devices, over_y(): return lax.all_to_all(blocks, 'y', 0, 0, tiled=True)  8.46 us
    all_to_all x1, starting transfers between devices, local(): lax.all_to_all(column_in.reshape(NY * NZ, CAP, features), ('y', 'z'), 0,...  7.94 us
  transfers between devices with their start and end apart: 16, of which 11 were waited for; matrix products, arithmetic and copies ran while one was open for 10% of the time, Pallas kernels for 4%

profile of v5, /device:TPU:6, one launch (start us, length us, event | category | flops | bytes accessed | tf_op | source)
XLA Modules:
  0.0 163.1 jit_solution(33037469132958937)
XLA Ops:
  0.6 2.9 %collective-permute-start = (bf16[1280,256]{1,0:T(8,128)(2,1)}, bf16[1280,256]{1,0:T(8,128)(2,1)S(1)}, u32[]{:S(2)}, u32[]{:S(2)}) collective-permute-start(bf16[1280,256]{1,0:T(8,128)(2,1)} %bitcast.72), channel_id=1, source_target_pairs={{0,128},{128,0},{256,384},{384,256},{1,129},{129,1},{257,385},{385... | collective-permute-start | bytes 1966088 | tf_op jit(solution)/shard_map/ppermute | solution.py:100
  3.5 2.2 %shard_map.102 = bf16[8,8,640]{2,1,0:T(8,128)(2,1)} custom-call(s32[1,128]{1,0:T(1,128)} %bitcast.76, s32[1,8]{1,0:T(1,128)} %lengths_ref.3, bf16[128,1280]{1,0:T(8,128)(2,1)} %tokens_ref.2, bf16[128,1280]{1,0:T(8,128)(2,1)} %target_ref.2), custom_call_target="tpu_custom_call" | custom-call | tf_op jit(solution)/shard_map/pallas_call | solution.py:152
  5.7 10.3 %all-to-all-start = ((bf16[8,8,640]{2,1,0:T(8,128)(2,1)}), bf16[8,8,640]{2,1,0:T(8,128)(2,1)S(1)}, u32[]{:S(2)}, u32[]{:S(2)}) async-start(bf16[8,8,640]{2,1,0:T(8,128)(2,1)} %shard_map.102), calls=%async_computation | async-start | bytes 163840 | tf_op jit(solution)/shard_map/all_to_all | solution.py:155
  16.0 3.1 %collective-permute-start.1 = (bf16[1280,256]{1,0:T(8,128)(2,1)}, bf16[1280,256]{1,0:T(8,128)(2,1)S(1)}, u32[]{:S(2)}, u32[]{:S(2)}) collective-permute-start(bf16[1280,256]{1,0:T(8,128)(2,1)} %bitcast.73), channel_id=1, source_target_pairs={{0,128},{128,0},{256,384},{384,256},{1,129},{129,1},{257,385},{385... | collective-permute-start | bytes 1966088 | tf_op jit(solution)/shard_map/ppermute | solution.py:100
  19.1 5.5 %all-to-all-done.arrived_ref = bf16[8,8,640]{2,1,0:T(8,128)(2,1)S(1)} async-done(((bf16[8,8,640]{2,1,0:T(8,128)(2,1)}), bf16[8,8,640]{2,1,0:T(8,128)(2,1)S(1)}, u32[]{:S(2)}, u32[]{:S(2)}) %all-to-all-start) | async-done | bytes 81952 | tf_op jit(solution)/shard_map/all_to_all | solution.py:155
  27.0 7.1 %all-to-all-start.1 = ((bf16[8,16,1280]{2,1,0:T(8,128)(2,1)}), bf16[8,16,1280]{2,1,0:T(8,128)(2,1)S(1)}, u32[]{:S(2)}, u32[]{:S(2)}) async-start(bf16[8,16,1280]{2,1,0:T(8,128)(2,1)} %get-tuple-element.29), calls=%async_computation.1 | async-start | bytes 655360 | tf_op jit(solution)/shard_map/all_to_all | solution.py:112
  34.1 3.1 %collective-permute-start.3 = (bf16[256,1280]{1,0:T(8,128)(2,1)}, bf16[256,1280]{1,0:T(8,128)(2,1)}, u32[]{:S(2)}, u32[]{:S(2)}) collective-permute-start(bf16[256,1280]{1,0:T(8,128)(2,1)} %bitcast.74), channel_id=1, source_target_pairs={{0,128},{128,0},{256,384},{384,256},{1,129},{129,1},{257,385},{385... | collective-permute-start | bytes 1966088 | tf_op jit(solution)/shard_map/ppermute | solution.py:100
  37.2 8.5 %all-to-all-done.1 = bf16[8,16,1280]{2,1,0:T(8,128)(2,1)S(1)} async-done(((bf16[8,16,1280]{2,1,0:T(8,128)(2,1)}), bf16[8,16,1280]{2,1,0:T(8,128)(2,1)S(1)}, u32[]{:S(2)}, u32[]{:S(2)}) %all-to-all-start.1) | async-done | bytes 327712 | tf_op jit(solution)/shard_map/all_to_all | solution.py:112
  46.2 3.0 %collective-permute-start.2 = (bf16[128,1280]{1,0:T(8,128)(2,1)S(1)}, bf16[128,1280]{1,0:T(8,128)(2,1)S(1)}, u32[]{:S(2)}, u32[]{:S(2)}) collective-permute-start(bf16[128,1280]{1,0:T(8,128)(2,1)S(1)} %bitcast.68), channel_id=1, source_target_pairs={{0,384},{384,0},{128,256},{256,128},{1,385},{385,1},{129,257},{257... | collective-permute-start | bytes 983048 | tf_op jit(solution)/shard_map/ppermute | solution.py:104
  49.8 6.6 %collective-permute-done.2 = bf16[128,1280]{1,0:T(8,128)(2,1)S(1)} collective-permute-done((bf16[128,1280]{1,0:T(8,128)(2,1)S(1)}, bf16[128,1280]{1,0:T(8,128)(2,1)S(1)}, u32[]{:S(2)}, u32[]{:S(2)}) %collective-permute-start.2) | collective-permute-done | bytes 327712 | tf_op jit(solution)/shard_map/ppermute | solution.py:104
  62.7 2.3 %fusion = bf16[256,1280]{1,0:T(8,128)(2,1)} fusion(f32[256,1280]{1,0:T(8,128)S(1)} %fusion.36, bf16[256,256]{1,0:T(8,128)(2,1)S(1)} %get-tuple-element.56, bf16[256,1280]{1,0:T(8,128)(2,1)} %collective-permute-done.3), kind=kOutput, calls=%fused_computation.2 | convolution fusion | flops 168427520 | bytes 2752512 | tf_op jit(solution)/shard_map/dot_general | solution.py:125
  65.0 5.2 %all-to-all-start.2 = ((bf16[16,16,1280]{2,1,0:T(8,128)(2,1)}), bf16[16,16,1280]{2,1,0:T(8,128)(2,1)}, u32[]{:S(2)}, u32[]{:S(2)}) async-start(bf16[16,16,1280]{2,1,0:T(8,128)(2,1)} %bitcast.75), calls=%async_computation.2 | async-start | bytes 1310720 | tf_op jit(solution)/shard_map/all_to_all | solution.py:116
  73.1 2.3 %shard_map.104 = (bf16[128,1280]{1,0:T(8,128)(2,1)}, bf16[16,128]{1,0:T(8,128)(2,1)}) custom-call(s32[1,128]{1,0:T(1,128)} %bitcast.77, s32[1,8]{1,0:T(1,128)} %lengths_ref.3, bf16[128,1280]{1,0:T(8,128)(2,1)} %tokens_ref.2, bf16[128,1280]{1,0:T(8,128)(2,1)} %target_ref.2), custom_call_target="tpu_custom_call" | custom-call | tf_op jit(solution)/shard_map/pallas_call | solution.py:182
  75.4 12.4 %all-to-all-done.2 = bf16[16,16,1280]{2,1,0:T(8,128)(2,1)} async-done(((bf16[16,16,1280]{2,1,0:T(8,128)(2,1)}), bf16[16,16,1280]{2,1,0:T(8,128)(2,1)}, u32[]{:S(2)}, u32[]{:S(2)}) %all-to-all-start.2) | async-done | bytes 655392 | tf_op jit(solution)/shard_map/all_to_all | solution.py:116
  89.9 7.4 %all-to-all-start.3 = ((bf16[16,16,1280]{2,1,0:T(8,128)(2,1)}), bf16[16,16,1280]{2,1,0:T(8,128)(2,1)S(1)}, u32[]{:S(2)}, u32[]{:S(2)}) async-start(bf16[16,16,1280]{2,1,0:T(8,128)(2,1)} %broadcast_in_dim.28), calls=%async_computation.3 | async-start | bytes 1310720 | tf_op jit(solution)/shard_map/all_to_all | solution.py:116
  99.3 9.3 %collective-permute-done.6 = bf16[128,1280]{1,0:T(8,128)(2,1)} collective-permute-done((bf16[128,1280]{1,0:T(8,128)(2,1)}, bf16[128,1280]{1,0:T(8,128)(2,1)}, u32[]{:S(2)}, u32[]{:S(2)}) %collective-permute-start.6) | collective-permute-done | bytes 327712 | tf_op jit(solution)/shard_map/ppermute | solution.py:100
  108.6 6.1 %all-to-all-done.3 = bf16[16,16,1280]{2,1,0:T(8,128)(2,1)S(1)} async-done(((bf16[16,16,1280]{2,1,0:T(8,128)(2,1)}), bf16[16,16,1280]{2,1,0:T(8,128)(2,1)S(1)}, u32[]{:S(2)}, u32[]{:S(2)}) %all-to-all-start.3) | async-done | bytes 655392 | tf_op jit(solution)/shard_map/all_to_all | solution.py:116
  123.6 4.3 %collective-permute-start.8 = (bf16[128,1280]{1,0:T(8,128)(2,1)S(1)}, bf16[128,1280]{1,0:T(8,128)(2,1)S(1)}, u32[]{:S(2)}, u32[]{:S(2)}) collective-permute-start(bf16[128,1280]{1,0:T(8,128)(2,1)S(1)} %fusion.10), channel_id=1, source_target_pairs={{0,384},{384,0},{128,256},{256,128},{1,385},{385,1},{129,257},{257... | collective-permute-start | bytes 983048 | tf_op jit(solution)/shard_map/ppermute | solution.py:104
  130.2 3.9 %collective-permute-start.10 = (bf16[256,640]{1,0:T(8,128)(2,1)}, bf16[256,640]{1,0:T(8,128)(2,1)S(1)}, u32[]{:S(2)}, u32[]{:S(2)}) collective-permute-start(bf16[256,640]{1,0:T(8,128)(2,1)} %get-tuple-element.51), channel_id=1, source_target_pairs={{0,128},{128,0},{256,384},{384,256},{1,129},{129,1},{257,385},{385... | collective-permute-start | bytes 983048 | tf_op jit(solution)/shard_map/ppermute | solution.py:100
  134.5 2.3 %collective-permute-done.8 = bf16[128,1280]{1,0:T(8,128)(2,1)S(1)} collective-permute-done((bf16[128,1280]{1,0:T(8,128)(2,1)S(1)}, bf16[128,1280]{1,0:T(8,128)(2,1)S(1)}, u32[]{:S(2)}, u32[]{:S(2)}) %collective-permute-start.8) | collective-permute-done | bytes 327712 | tf_op jit(solution)/shard_map/ppermute | solution.py:104
  138.2 7.9 %all-to-all-start.4 = ((bf16[64,2,1280]{2,1,0:T(2,128)(2,1)}), bf16[64,2,1280]{2,1,0:T(2,128)(2,1)S(1)}, u32[]{:S(2)}, u32[]{:S(2)}) async-start(bf16[64,2,1280]{2,1,0:T(2,128)(2,1)} %reshape.45), calls=%async_computation.4 | async-start | bytes 655360 | tf_op jit(solution)/shard_map/all_to_all | solution.py:225
  148.3 2.5 %fusion.7 = bf16[1,1280,256]{2,1,0:T(8,128)(2,1)} fusion(bf16[256,256]{1,0:T(8,128)(2,1)S(1)} %get-tuple-element.62, bf16[256,256]{1,0:T(8,128)(2,1)S(1)} %copy-done.7, bf16[128,1280]{1,0:T(8,128)(2,1)} %collective-permute-done.6, bf16[128,1280]{1,0:T(8,128)(2,1)S(1)} %copy-done.15, bf16[128,1280]{1,0:T(8,128)(2,1)S(1)} %copy-done.10, ...), kind=kOutput, calls=%fused_computation.17 | convolution fusion | flops 341639168 | bytes 2228224 | tf_op jit(solution)/shard_map/dot_general | solution.py:88
  150.8 2.5 %fusion.6 = bf16[1,1280,256]{2,1,0:T(8,128)(2,1)} fusion(bf16[256,256]{1,0:T(8,128)(2,1)S(1)} %get-tuple-element.63, bf16[256,256]{1,0:T(8,128)(2,1)S(1)} %get-tuple-element.52, bf16[128,1280]{1,0:T(8,128)(2,1)} %collective-permute-done.6, bf16[128,1280]{1,0:T(8,128)(2,1)S(1)} %copy-done.15, bf16[128,1280]{1,0:T(8,128)(2,1)S(1)} %copy-done.10, ...), kind=kOutput, calls=%fused_computation.16 | convolution fusion | flops 341639168 | bytes 2228224 | tf_op jit(solution)/shard_map/dot_general | solution.py:88
  154.5 7.5 %all-to-all-done.4 = bf16[64,2,1280]{2,1,0:T(2,128)(2,1)S(1)} async-done(((bf16[64,2,1280]{2,1,0:T(2,128)(2,1)}), bf16[64,2,1280]{2,1,0:T(2,128)(2,1)S(1)}, u32[]{:S(2)}, u32[]{:S(2)}) %all-to-all-start.4) | async-done | bytes 327712 | tf_op jit(solution)/shard_map/all_to_all | solution.py:225
  (89 shorter events, 34.0 us)
Async XLA Ops:
  0.6 45.1 %copy-start.1 = (bf16[1,1280,256]{2,1,0:T(8,128)(2,1)S(1)}, bf16[1,1280,256]{2,1,0:T(8,128)(2,1)}, u32[]{:S(2)}) copy-start(bf16[1,1280,256]{2,1,0:T(8,128)(2,1)} %param.12) | copy-start | bytes 1966084
  0.6 26.4 %collective-permute-start = (bf16[1280,256]{1,0:T(8,128)(2,1)}, bf16[1280,256]{1,0:T(8,128)(2,1)S(1)}, u32[]{:S(2)}, u32[]{:S(2)}) collective-permute-start(bf16[1280,256]{1,0:T(8,128)(2,1)} %bitcast.72), channel_id=1, source_target_pairs={{0,128},{128,0},{256,384},{384,256},{1,129},{129,1},{257,385},{385... | collective-permute-start | bytes 1966088 | tf_op jit(solution)/shard_map/ppermute | solution.py:100
  3.5 42.4 %copy-start = (bf16[1,1280,256]{2,1,0:T(8,128)(2,1)S(1)}, bf16[1,1280,256]{2,1,0:T(8,128)(2,1)}, u32[]{:S(2)}) copy-start(bf16[1,1280,256]{2,1,0:T(8,128)(2,1)} %param.11) | copy-start | bytes 1966084
  5.7 18.9 %all-to-all-start = ((bf16[8,8,640]{2,1,0:T(8,128)(2,1)}), bf16[8,8,640]{2,1,0:T(8,128)(2,1)S(1)}, u32[]{:S(2)}, u32[]{:S(2)}) async-start(bf16[8,8,640]{2,1,0:T(8,128)(2,1)} %shard_map.102), calls=%async_computation | async-start | bytes 163840 | tf_op jit(solution)/shard_map/all_to_all | solution.py:155
  16.0 21.2 %collective-permute-start.1 = (bf16[1280,256]{1,0:T(8,128)(2,1)}, bf16[1280,256]{1,0:T(8,128)(2,1)S(1)}, u32[]{:S(2)}, u32[]{:S(2)}) collective-permute-start(bf16[1280,256]{1,0:T(8,128)(2,1)} %bitcast.73), channel_id=1, source_target_pairs={{0,128},{128,0},{256,384},{384,256},{1,129},{129,1},{257,385},{385... | collective-permute-start | bytes 1966088 | tf_op jit(solution)/shard_map/ppermute | solution.py:100
  27.0 18.7 %all-to-all-start.1 = ((bf16[8,16,1280]{2,1,0:T(8,128)(2,1)}), bf16[8,16,1280]{2,1,0:T(8,128)(2,1)S(1)}, u32[]{:S(2)}, u32[]{:S(2)}) async-start(bf16[8,16,1280]{2,1,0:T(8,128)(2,1)} %get-tuple-element.29), calls=%async_computation.1 | async-start | bytes 655360 | tf_op jit(solution)/shard_map/all_to_all | solution.py:112
  34.1 23.5 %collective-permute-start.3 = (bf16[256,1280]{1,0:T(8,128)(2,1)}, bf16[256,1280]{1,0:T(8,128)(2,1)}, u32[]{:S(2)}, u32[]{:S(2)}) collective-permute-start(bf16[256,1280]{1,0:T(8,128)(2,1)} %bitcast.74), channel_id=1, source_target_pairs={{0,128},{128,0},{256,384},{384,256},{1,129},{129,1},{257,385},{385... | collective-permute-start | bytes 1966088 | tf_op jit(solution)/shard_map/ppermute | solution.py:100
  46.2 10.2 %collective-permute-start.2 = (bf16[128,1280]{1,0:T(8,128)(2,1)S(1)}, bf16[128,1280]{1,0:T(8,128)(2,1)S(1)}, u32[]{:S(2)}, u32[]{:S(2)}) collective-permute-start(bf16[128,1280]{1,0:T(8,128)(2,1)S(1)} %bitcast.68), channel_id=1, source_target_pairs={{0,384},{384,0},{128,256},{256,128},{1,385},{385,1},{129,257},{257... | collective-permute-start | bytes 983048 | tf_op jit(solution)/shard_map/ppermute | solution.py:104
  57.6 3.9 %collective-permute-start.4 = (bf16[256,1024]{1,0:T(8,128)(2,1)S(1)}, bf16[256,1024]{1,0:T(8,128)(2,1)S(1)}, u32[]{:S(2)}, u32[]{:S(2)}) collective-permute-start(bf16[256,1024]{1,0:T(8,128)(2,1)S(1)} %pad_maximum_fusion.2), channel_id=1, source_target_pairs={{0,1},{1,0},{2,3},{3,2},{4,5},{5,4},{6,7},{7,6},{8,9},{9,8},{10,11... | collective-permute-start | bytes 1572872 | tf_op jit(solution)/shard_map/ppermute | solution.py:96
  65.0 22.7 %all-to-all-start.2 = ((bf16[16,16,1280]{2,1,0:T(8,128)(2,1)}), bf16[16,16,1280]{2,1,0:T(8,128)(2,1)}, u32[]{:S(2)}, u32[]{:S(2)}) async-start(bf16[16,16,1280]{2,1,0:T(8,128)(2,1)} %bitcast.75), calls=%async_computation.2 | async-start | bytes 1310720 | tf_op jit(solution)/shard_map/all_to_all | solution.py:116
  71.1 17.9 %copy-start.11 = (bf16[16,1280]{1,0:T(8,128)(2,1)S(1)}, bf16[16,1280]{1,0:T(8,128)(2,1)}, u32[]{:S(2)}) copy-start(bf16[16,1280]{1,0:T(8,128)(2,1)} %get-tuple-element.42) | copy-start | bytes 122884
  71.1 17.9 %copy-start.12 = (bf16[16,1280]{1,0:T(8,128)(2,1)S(1)}, bf16[16,1280]{1,0:T(8,128)(2,1)}, u32[]{:S(2)}) copy-start(bf16[16,1280]{1,0:T(8,128)(2,1)} %get-tuple-element.44) | copy-start | bytes 122884
  71.1 17.9 %collective-permute-start.5 = (bf16[128,1280]{1,0:T(8,128)(2,1)}, bf16[128,1280]{1,0:T(8,128)(2,1)S(1)}, u32[]{:S(2)}, u32[]{:S(2)}) collective-permute-start(bf16[128,1280]{1,0:T(8,128)(2,1)} %get-tuple-element.61), channel_id=1, source_target_pairs={{0,128},{128,0},{256,384},{384,256},{1,129},{129,1},{257,385},{385... | collective-permute-start | bytes 983048 | tf_op jit(solution)/shard_map/ppermute | solution.py:100
  89.9 24.8 %all-to-all-start.3 = ((bf16[16,16,1280]{2,1,0:T(8,128)(2,1)}), bf16[16,16,1280]{2,1,0:T(8,128)(2,1)S(1)}, u32[]{:S(2)}, u32[]{:S(2)}) async-start(bf16[16,16,1280]{2,1,0:T(8,128)(2,1)} %broadcast_in_dim.28), calls=%async_computation.3 | async-start | bytes 1310720 | tf_op jit(solution)/shard_map/all_to_all | solution.py:116
  97.4 11.3 %collective-permute-start.6 = (bf16[128,1280]{1,0:T(8,128)(2,1)}, bf16[128,1280]{1,0:T(8,128)(2,1)}, u32[]{:S(2)}, u32[]{:S(2)}) collective-permute-start(bf16[128,1280]{1,0:T(8,128)(2,1)} %get-tuple-element.60), channel_id=1, source_target_pairs={{0,128},{128,0},{256,384},{384,256},{1,129},{129,1},{257,385},{385... | collective-permute-start | bytes 983048 | tf_op jit(solution)/shard_map/ppermute | solution.py:100
  116.7 3.4 %collective-permute-start.7 = (bf16[256,512]{1,0:T(8,128)(2,1)S(1)}, bf16[256,512]{1,0:T(8,128)(2,1)S(1)}, u32[]{:S(2)}, u32[]{:S(2)}) collective-permute-start(bf16[256,512]{1,0:T(8,128)(2,1)S(1)} %pad_maximum_fusion.6), channel_id=1, source_target_pairs={{0,1},{1,0},{2,3},{3,2},{4,5},{5,4},{6,7},{7,6},{8,9},{9,8},{10,11... | collective-permute-start | bytes 786440 | tf_op jit(solution)/shard_map/ppermute | solution.py:96
  123.6 13.2 %collective-permute-start.8 = (bf16[128,1280]{1,0:T(8,128)(2,1)S(1)}, bf16[128,1280]{1,0:T(8,128)(2,1)S(1)}, u32[]{:S(2)}, u32[]{:S(2)}) collective-permute-start(bf16[128,1280]{1,0:T(8,128)(2,1)S(1)} %fusion.10), channel_id=1, source_target_pairs={{0,384},{384,0},{128,256},{256,128},{1,385},{385,1},{129,257},{257... | collective-permute-start | bytes 983048 | tf_op jit(solution)/shard_map/ppermute | solution.py:104
  127.9 18.4 %collective-permute-start.9 = (bf16[256,1152]{1,0:T(8,128)(2,1)}, bf16[256,1152]{1,0:T(8,128)(2,1)}, u32[]{:S(2)}, u32[]{:S(2)}) collective-permute-start(bf16[256,1152]{1,0:T(8,128)(2,1)} %pad_maximum_fusion.1), channel_id=1, source_target_pairs={{0,128},{128,0},{256,384},{384,256},{1,129},{129,1},{257,385},{385... | collective-permute-start | bytes 1769480 | tf_op jit(solution)/shard_map/ppermute | solution.py:100
  130.2 23.0 %collective-permute-start.10 = (bf16[256,640]{1,0:T(8,128)(2,1)}, bf16[256,640]{1,0:T(8,128)(2,1)S(1)}, u32[]{:S(2)}, u32[]{:S(2)}) collective-permute-start(bf16[256,640]{1,0:T(8,128)(2,1)} %get-tuple-element.51), channel_id=1, source_target_pairs={{0,128},{128,0},{256,384},{384,256},{1,129},{129,1},{257,385},{385... | collective-permute-start | bytes 983048 | tf_op jit(solution)/shard_map/ppermute | solution.py:100
  137.2 11.0 %copy-start.7 = (bf16[256,256]{1,0:T(8,128)(2,1)S(1)}, bf16[256,256]{1,0:T(8,128)(2,1)}, u32[]{:S(2)}) copy-start(bf16[256,256]{1,0:T(8,128)(2,1)} %copy-done.6) | copy-start | bytes 393220
  137.3 11.0 %copy-start.10 = (bf16[128,1280]{1,0:T(8,128)(2,1)S(1)}, bf16[128,1280]{1,0:T(8,128)(2,1)}, u32[]{:S(2)}) copy-start(bf16[128,1280]{1,0:T(8,128)(2,1)} %get-tuple-element.60) | copy-start | bytes 983044
  137.3 11.0 %copy-start.15 = (bf16[128,1280]{1,0:T(8,128)(2,1)S(1)}, bf16[128,1280]{1,0:T(8,128)(2,1)}, u32[]{:S(2)}) copy-start(bf16[128,1280]{1,0:T(8,128)(2,1)} %copy-done.14) | copy-start | bytes 983044
  138.2 23.8 %all-to-all-start.4 = ((bf16[64,2,1280]{2,1,0:T(2,128)(2,1)}), bf16[64,2,1280]{2,1,0:T(2,128)(2,1)S(1)}, u32[]{:S(2)}, u32[]{:S(2)}) async-start(bf16[64,2,1280]{2,1,0:T(2,128)(2,1)} %reshape.45), calls=%async_computation.4 | async-start | bytes 655360 | tf_op jit(solution)/shard_map/all_to_all | solution.py:225
  153.2 8.9 %copy-start.13 = (bf16[16,128]{1,0:T(8,128)(2,1)S(1)}, bf16[16,128]{1,0:T(8,128)(2,1)}, u32[]{:S(2)}) copy-start(bf16[16,128]{1,0:T(8,128)(2,1)} %get-tuple-element.41) | copy-start | bytes 12292
  (8 other events, 19.3 us)

commit v6 on v5

--- a/solution.py
+++ b/solution.py
@@ -222,7 +222,7 @@
     )
     column_in = input_part(mine) + extra + cross(partial).astype(F32)
     column_in, pair_in, pair_rest = column_in.astype(BF16), pair(first), pair(second)
-    pieces = lax.all_to_all(column_in.reshape(NY * NZ, CAP, features), ("y", "z"), 0, 0, tiled=True)
+    pieces = lax.all_to_all(column_in, ("y", "z"), 0, 0, tiled=True)
     slots = jnp.sum(pieces.reshape(NY, slot_count, features).astype(F32), axis=0).astype(BF16)
     grad_tokens = (own.astype(F32) + times_rows(chosen, slots)).astype(BF16)
 

time: 165 us -> 165 us (level)
  transfers between devices with their start and end apart: 16 -> 16, of which waited for: 11 -> 11; matrix products, arithmetic and copies ran while one was open for 10% -> 9% of each run, Pallas kernels for 4% -> 4%
where the time goes in v6:
time: 165 us; the launch traced here: 163 us
  starting transfers between devices  68.1 us (41%)
  waiting for transfers between devices  60.5 us (37%)
  matrix products  17.1 us (10%)
  Pallas kernels  6.22 us (4%)
  local copies, waits for them, and re-layouts  6.16 us (4%)
  other arithmetic  3.97 us (2%)
    ppermute x7, starting transfers between devices, pair(): return lax.ppermute(value, 'x', PAIR)  18.8 us
    all_to_all x2, waiting for transfers between devices, over_two_columns(): lax.all_to_all(blocks, ('x', 'y'), 0, 0, axis_index_groups=TWO_COLUMNS, t...  18.5 us
    all_to_all x2, starting transfers between devices, over_two_columns(): lax.all_to_all(blocks, ('x', 'y'), 0, 0, axis_index_groups=TWO_COLUMNS, t...  12.6 us
    all_to_all x1, starting transfers between devices, local(): arrived = lax.all_to_all(message, 'z', 0, 0, tiled=True)  10.3 us
    ppermute x7, waiting for transfers between devices, pair(): return lax.ppermute(value, 'x', PAIR)  9.5 us
    ppermute x2, waiting for transfers between devices, cross(): return lax.ppermute(value, 'x', CROSS)  8.94 us
    all_to_all x1, waiting for transfers between devices, over_y(): return lax.all_to_all(blocks, 'y', 0, 0, tiled=True)  8.46 us
    all_to_all x1, starting transfers between devices, local(): pieces = lax.all_to_all(column_in, ('y', 'z'), 0, 0, tiled=True)  7.94 us
  transfers between devices with their start and end apart: 16, of which 11 were waited for; matrix products, arithmetic and copies ran while one was open for 9% of the time, Pallas kernels for 4%

profile of v6, /device:TPU:6, one launch (start us, length us, event | category | flops | bytes accessed | tf_op | source)
XLA Modules:
  0.0 163.1 jit_solution(33037469132958937)
XLA Ops:
  0.6 2.9 %collective-permute-start = (bf16[1280,256]{1,0:T(8,128)(2,1)}, bf16[1280,256]{1,0:T(8,128)(2,1)S(1)}, u32[]{:S(2)}, u32[]{:S(2)}) collective-permute-start(bf16[1280,256]{1,0:T(8,128)(2,1)} %bitcast.72), channel_id=1, source_target_pairs={{0,128},{128,0},{256,384},{384,256},{1,129},{129,1},{257,385},{385... | collective-permute-start | bytes 1966088 | tf_op jit(solution)/shard_map/ppermute | solution.py:100
  3.5 2.2 %shard_map.102 = bf16[8,8,640]{2,1,0:T(8,128)(2,1)} custom-call(s32[1,128]{1,0:T(1,128)} %bitcast.76, s32[1,8]{1,0:T(1,128)} %lengths_ref.3, bf16[128,1280]{1,0:T(8,128)(2,1)} %tokens_ref.2, bf16[128,1280]{1,0:T(8,128)(2,1)} %target_ref.2), custom_call_target="tpu_custom_call" | custom-call | tf_op jit(solution)/shard_map/pallas_call | solution.py:152
  5.7 10.3 %all-to-all-start = ((bf16[8,8,640]{2,1,0:T(8,128)(2,1)}), bf16[8,8,640]{2,1,0:T(8,128)(2,1)S(1)}, u32[]{:S(2)}, u32[]{:S(2)}) async-start(bf16[8,8,640]{2,1,0:T(8,128)(2,1)} %shard_map.102), calls=%async_computation | async-start | bytes 163840 | tf_op jit(solution)/shard_map/all_to_all | solution.py:155
  16.0 3.1 %collective-permute-start.1 = (bf16[1280,256]{1,0:T(8,128)(2,1)}, bf16[1280,256]{1,0:T(8,128)(2,1)S(1)}, u32[]{:S(2)}, u32[]{:S(2)}) collective-permute-start(bf16[1280,256]{1,0:T(8,128)(2,1)} %bitcast.73), channel_id=1, source_target_pairs={{0,128},{128,0},{256,384},{384,256},{1,129},{129,1},{257,385},{385... | collective-permute-start | bytes 1966088 | tf_op jit(solution)/shard_map/ppermute | solution.py:100
  19.1 5.5 %all-to-all-done.arrived_ref = bf16[8,8,640]{2,1,0:T(8,128)(2,1)S(1)} async-done(((bf16[8,8,640]{2,1,0:T(8,128)(2,1)}), bf16[8,8,640]{2,1,0:T(8,128)(2,1)S(1)}, u32[]{:S(2)}, u32[]{:S(2)}) %all-to-all-start) | async-done | bytes 81952 | tf_op jit(solution)/shard_map/all_to_all | solution.py:155
  27.0 7.1 %all-to-all-start.1 = ((bf16[8,16,1280]{2,1,0:T(8,128)(2,1)}), bf16[8,16,1280]{2,1,0:T(8,128)(2,1)S(1)}, u32[]{:S(2)}, u32[]{:S(2)}) async-start(bf16[8,16,1280]{2,1,0:T(8,128)(2,1)} %get-tuple-element.29), calls=%async_computation.1 | async-start | bytes 655360 | tf_op jit(solution)/shard_map/all_to_all | solution.py:112
  34.1 3.1 %collective-permute-start.3 = (bf16[256,1280]{1,0:T(8,128)(2,1)}, bf16[256,1280]{1,0:T(8,128)(2,1)}, u32[]{:S(2)}, u32[]{:S(2)}) collective-permute-start(bf16[256,1280]{1,0:T(8,128)(2,1)} %bitcast.74), channel_id=1, source_target_pairs={{0,128},{128,0},{256,384},{384,256},{1,129},{129,1},{257,385},{385... | collective-permute-start | bytes 1966088 | tf_op jit(solution)/shard_map/ppermute | solution.py:100
  37.2 8.5 %all-to-all-done.1 = bf16[8,16,1280]{2,1,0:T(8,128)(2,1)S(1)} async-done(((bf16[8,16,1280]{2,1,0:T(8,128)(2,1)}), bf16[8,16,1280]{2,1,0:T(8,128)(2,1)S(1)}, u32[]{:S(2)}, u32[]{:S(2)}) %all-to-all-start.1) | async-done | bytes 327712 | tf_op jit(solution)/shard_map/all_to_all | solution.py:112
  46.2 3.0 %collective-permute-start.2 = (bf16[128,1280]{1,0:T(8,128)(2,1)S(1)}, bf16[128,1280]{1,0:T(8,128)(2,1)S(1)}, u32[]{:S(2)}, u32[]{:S(2)}) collective-permute-start(bf16[128,1280]{1,0:T(8,128)(2,1)S(1)} %bitcast.68), channel_id=1, source_target_pairs={{0,384},{384,0},{128,256},{256,128},{1,385},{385,1},{129,257},{257... | collective-permute-start | bytes 983048 | tf_op jit(solution)/shard_map/ppermute | solution.py:104
  49.8 6.6 %collective-permute-done.2 = bf16[128,1280]{1,0:T(8,128)(2,1)S(1)} collective-permute-done((bf16[128,1280]{1,0:T(8,128)(2,1)S(1)}, bf16[128,1280]{1,0:T(8,128)(2,1)S(1)}, u32[]{:S(2)}, u32[]{:S(2)}) %collective-permute-start.2) | collective-permute-done | bytes 327712 | tf_op jit(solution)/shard_map/ppermute | solution.py:104
  62.7 2.3 %fusion = bf16[256,1280]{1,0:T(8,128)(2,1)} fusion(f32[256,1280]{1,0:T(8,128)S(1)} %fusion.36, bf16[256,256]{1,0:T(8,128)(2,1)S(1)} %get-tuple-element.56, bf16[256,1280]{1,0:T(8,128)(2,1)} %collective-permute-done.3), kind=kOutput, calls=%fused_computation.2 | convolution fusion | flops 168427520 | bytes 2752512 | tf_op jit(solution)/shard_map/dot_general | solution.py:125
  65.0 5.2 %all-to-all-start.2 = ((bf16[16,16,1280]{2,1,0:T(8,128)(2,1)}), bf16[16,16,1280]{2,1,0:T(8,128)(2,1)}, u32[]{:S(2)}, u32[]{:S(2)}) async-start(bf16[16,16,1280]{2,1,0:T(8,128)(2,1)} %bitcast.75), calls=%async_computation.2 | async-start | bytes 1310720 | tf_op jit(solution)/shard_map/all_to_all | solution.py:116
  73.1 2.3 %shard_map.104 = (bf16[128,1280]{1,0:T(8,128)(2,1)}, bf16[16,128]{1,0:T(8,128)(2,1)}) custom-call(s32[1,128]{1,0:T(1,128)} %bitcast.77, s32[1,8]{1,0:T(1,128)} %lengths_ref.3, bf16[128,1280]{1,0:T(8,128)(2,1)} %tokens_ref.2, bf16[128,1280]{1,0:T(8,128)(2,1)} %target_ref.2), custom_call_target="tpu_custom_call" | custom-call | tf_op jit(solution)/shard_map/pallas_call | solution.py:182
  75.4 12.4 %all-to-all-done.2 = bf16[16,16,1280]{2,1,0:T(8,128)(2,1)} async-done(((bf16[16,16,1280]{2,1,0:T(8,128)(2,1)}), bf16[16,16,1280]{2,1,0:T(8,128)(2,1)}, u32[]{:S(2)}, u32[]{:S(2)}) %all-to-all-start.2) | async-done | bytes 655392 | tf_op jit(solution)/shard_map/all_to_all | solution.py:116
  89.9 7.4 %all-to-all-start.3 = ((bf16[16,16,1280]{2,1,0:T(8,128)(2,1)}), bf16[16,16,1280]{2,1,0:T(8,128)(2,1)S(1)}, u32[]{:S(2)}, u32[]{:S(2)}) async-start(bf16[16,16,1280]{2,1,0:T(8,128)(2,1)} %broadcast_in_dim.28), calls=%async_computation.3 | async-start | bytes 1310720 | tf_op jit(solution)/shard_map/all_to_all | solution.py:116
  99.3 9.3 %collective-permute-done.6 = bf16[128,1280]{1,0:T(8,128)(2,1)} collective-permute-done((bf16[128,1280]{1,0:T(8,128)(2,1)}, bf16[128,1280]{1,0:T(8,128)(2,1)}, u32[]{:S(2)}, u32[]{:S(2)}) %collective-permute-start.6) | collective-permute-done | bytes 327712 | tf_op jit(solution)/shard_map/ppermute | solution.py:100
  108.6 6.1 %all-to-all-done.3 = bf16[16,16,1280]{2,1,0:T(8,128)(2,1)S(1)} async-done(((bf16[16,16,1280]{2,1,0:T(8,128)(2,1)}), bf16[16,16,1280]{2,1,0:T(8,128)(2,1)S(1)}, u32[]{:S(2)}, u32[]{:S(2)}) %all-to-all-start.3) | async-done | bytes 655392 | tf_op jit(solution)/shard_map/all_to_all | solution.py:116
  123.6 4.3 %collective-permute-start.8 = (bf16[128,1280]{1,0:T(8,128)(2,1)S(1)}, bf16[128,1280]{1,0:T(8,128)(2,1)S(1)}, u32[]{:S(2)}, u32[]{:S(2)}) collective-permute-start(bf16[128,1280]{1,0:T(8,128)(2,1)S(1)} %fusion.10), channel_id=1, source_target_pairs={{0,384},{384,0},{128,256},{256,128},{1,385},{385,1},{129,257},{257... | collective-permute-start | bytes 983048 | tf_op jit(solution)/shard_map/ppermute | solution.py:104
  130.2 3.9 %collective-permute-start.10 = (bf16[256,640]{1,0:T(8,128)(2,1)}, bf16[256,640]{1,0:T(8,128)(2,1)S(1)}, u32[]{:S(2)}, u32[]{:S(2)}) collective-permute-start(bf16[256,640]{1,0:T(8,128)(2,1)} %get-tuple-element.51), channel_id=1, source_target_pairs={{0,128},{128,0},{256,384},{384,256},{1,129},{129,1},{257,385},{385... | collective-permute-start | bytes 983048 | tf_op jit(solution)/shard_map/ppermute | solution.py:100
  134.5 2.3 %collective-permute-done.8 = bf16[128,1280]{1,0:T(8,128)(2,1)S(1)} collective-permute-done((bf16[128,1280]{1,0:T(8,128)(2,1)S(1)}, bf16[128,1280]{1,0:T(8,128)(2,1)S(1)}, u32[]{:S(2)}, u32[]{:S(2)}) %collective-permute-start.8) | collective-permute-done | bytes 327712 | tf_op jit(solution)/shard_map/ppermute | solution.py:104
  138.2 7.9 %all-to-all-start.4 = ((bf16[64,2,1280]{2,1,0:T(2,128)(2,1)}), bf16[64,2,1280]{2,1,0:T(2,128)(2,1)S(1)}, u32[]{:S(2)}, u32[]{:S(2)}) async-start(bf16[64,2,1280]{2,1,0:T(2,128)(2,1)} %all_to_all.22), calls=%async_computation.4 | async-start | bytes 655360 | tf_op jit(solution)/shard_map/all_to_all | solution.py:225
  148.3 2.5 %fusion.7 = bf16[1,1280,256]{2,1,0:T(8,128)(2,1)} fusion(bf16[256,256]{1,0:T(8,128)(2,1)S(1)} %get-tuple-element.62, bf16[256,256]{1,0:T(8,128)(2,1)S(1)} %copy-done.7, bf16[128,1280]{1,0:T(8,128)(2,1)} %collective-permute-done.6, bf16[128,1280]{1,0:T(8,128)(2,1)S(1)} %copy-done.15, bf16[128,1280]{1,0:T(8,128)(2,1)S(1)} %copy-done.10, ...), kind=kOutput, calls=%fused_computation.17 | convolution fusion | flops 341639168 | bytes 2228224 | tf_op jit(solution)/shard_map/dot_general | solution.py:88
  150.8 2.5 %fusion.6 = bf16[1,1280,256]{2,1,0:T(8,128)(2,1)} fusion(bf16[256,256]{1,0:T(8,128)(2,1)S(1)} %get-tuple-element.63, bf16[256,256]{1,0:T(8,128)(2,1)S(1)} %get-tuple-element.52, bf16[128,1280]{1,0:T(8,128)(2,1)} %collective-permute-done.6, bf16[128,1280]{1,0:T(8,128)(2,1)S(1)} %copy-done.15, bf16[128,1280]{1,0:T(8,128)(2,1)S(1)} %copy-done.10, ...), kind=kOutput, calls=%fused_computation.16 | convolution fusion | flops 341639168 | bytes 2228224 | tf_op jit(solution)/shard_map/dot_general | solution.py:88
  154.5 7.5 %all-to-all-done.4 = bf16[64,2,1280]{2,1,0:T(2,128)(2,1)S(1)} async-done(((bf16[64,2,1280]{2,1,0:T(2,128)(2,1)}), bf16[64,2,1280]{2,1,0:T(2,128)(2,1)S(1)}, u32[]{:S(2)}, u32[]{:S(2)}) %all-to-all-start.4) | async-done | bytes 327712 | tf_op jit(solution)/shard_map/all_to_all | solution.py:225
  (89 shorter events, 34.0 us)
Async XLA Ops:
  0.6 45.1 %copy-start.1 = (bf16[1,1280,256]{2,1,0:T(8,128)(2,1)S(1)}, bf16[1,1280,256]{2,1,0:T(8,128)(2,1)}, u32[]{:S(2)}) copy-start(bf16[1,1280,256]{2,1,0:T(8,128)(2,1)} %param.12) | copy-start | bytes 1966084
  0.6 26.4 %collective-permute-start = (bf16[1280,256]{1,0:T(8,128)(2,1)}, bf16[1280,256]{1,0:T(8,128)(2,1)S(1)}, u32[]{:S(2)}, u32[]{:S(2)}) collective-permute-start(bf16[1280,256]{1,0:T(8,128)(2,1)} %bitcast.72), channel_id=1, source_target_pairs={{0,128},{128,0},{256,384},{384,256},{1,129},{129,1},{257,385},{385... | collective-permute-start | bytes 1966088 | tf_op jit(solution)/shard_map/ppermute | solution.py:100
  3.5 42.4 %copy-start = (bf16[1,1280,256]{2,1,0:T(8,128)(2,1)S(1)}, bf16[1,1280,256]{2,1,0:T(8,128)(2,1)}, u32[]{:S(2)}) copy-start(bf16[1,1280,256]{2,1,0:T(8,128)(2,1)} %param.11) | copy-start | bytes 1966084
  5.7 18.9 %all-to-all-start = ((bf16[8,8,640]{2,1,0:T(8,128)(2,1)}), bf16[8,8,640]{2,1,0:T(8,128)(2,1)S(1)}, u32[]{:S(2)}, u32[]{:S(2)}) async-start(bf16[8,8,640]{2,1,0:T(8,128)(2,1)} %shard_map.102), calls=%async_computation | async-start | bytes 163840 | tf_op jit(solution)/shard_map/all_to_all | solution.py:155
  16.0 21.2 %collective-permute-start.1 = (bf16[1280,256]{1,0:T(8,128)(2,1)}, bf16[1280,256]{1,0:T(8,128)(2,1)S(1)}, u32[]{:S(2)}, u32[]{:S(2)}) collective-permute-start(bf16[1280,256]{1,0:T(8,128)(2,1)} %bitcast.73), channel_id=1, source_target_pairs={{0,128},{128,0},{256,384},{384,256},{1,129},{129,1},{257,385},{385... | collective-permute-start | bytes 1966088 | tf_op jit(solution)/shard_map/ppermute | solution.py:100
  27.0 18.7 %all-to-all-start.1 = ((bf16[8,16,1280]{2,1,0:T(8,128)(2,1)}), bf16[8,16,1280]{2,1,0:T(8,128)(2,1)S(1)}, u32[]{:S(2)}, u32[]{:S(2)}) async-start(bf16[8,16,1280]{2,1,0:T(8,128)(2,1)} %get-tuple-element.29), calls=%async_computation.1 | async-start | bytes 655360 | tf_op jit(solution)/shard_map/all_to_all | solution.py:112
  34.1 23.5 %collective-permute-start.3 = (bf16[256,1280]{1,0:T(8,128)(2,1)}, bf16[256,1280]{1,0:T(8,128)(2,1)}, u32[]{:S(2)}, u32[]{:S(2)}) collective-permute-start(bf16[256,1280]{1,0:T(8,128)(2,1)} %bitcast.74), channel_id=1, source_target_pairs={{0,128},{128,0},{256,384},{384,256},{1,129},{129,1},{257,385},{385... | collective-permute-start | bytes 1966088 | tf_op jit(solution)/shard_map/ppermute | solution.py:100
  46.2 10.2 %collective-permute-start.2 = (bf16[128,1280]{1,0:T(8,128)(2,1)S(1)}, bf16[128,1280]{1,0:T(8,128)(2,1)S(1)}, u32[]{:S(2)}, u32[]{:S(2)}) collective-permute-start(bf16[128,1280]{1,0:T(8,128)(2,1)S(1)} %bitcast.68), channel_id=1, source_target_pairs={{0,384},{384,0},{128,256},{256,128},{1,385},{385,1},{129,257},{257... | collective-permute-start | bytes 983048 | tf_op jit(solution)/shard_map/ppermute | solution.py:104
  57.6 3.9 %collective-permute-start.4 = (bf16[256,1024]{1,0:T(8,128)(2,1)S(1)}, bf16[256,1024]{1,0:T(8,128)(2,1)S(1)}, u32[]{:S(2)}, u32[]{:S(2)}) collective-permute-start(bf16[256,1024]{1,0:T(8,128)(2,1)S(1)} %pad_maximum_fusion.2), channel_id=1, source_target_pairs={{0,1},{1,0},{2,3},{3,2},{4,5},{5,4},{6,7},{7,6},{8,9},{9,8},{10,11... | collective-permute-start | bytes 1572872 | tf_op jit(solution)/shard_map/ppermute | solution.py:96
  65.0 22.7 %all-to-all-start.2 = ((bf16[16,16,1280]{2,1,0:T(8,128)(2,1)}), bf16[16,16,1280]{2,1,0:T(8,128)(2,1)}, u32[]{:S(2)}, u32[]{:S(2)}) async-start(bf16[16,16,1280]{2,1,0:T(8,128)(2,1)} %bitcast.75), calls=%async_computation.2 | async-start | bytes 1310720 | tf_op jit(solution)/shard_map/all_to_all | solution.py:116
  71.1 17.9 %copy-start.11 = (bf16[16,1280]{1,0:T(8,128)(2,1)S(1)}, bf16[16,1280]{1,0:T(8,128)(2,1)}, u32[]{:S(2)}) copy-start(bf16[16,1280]{1,0:T(8,128)(2,1)} %get-tuple-element.42) | copy-start | bytes 122884
  71.1 17.9 %copy-start.12 = (bf16[16,1280]{1,0:T(8,128)(2,1)S(1)}, bf16[16,1280]{1,0:T(8,128)(2,1)}, u32[]{:S(2)}) copy-start(bf16[16,1280]{1,0:T(8,128)(2,1)} %get-tuple-element.44) | copy-start | bytes 122884
  71.1 17.9 %collective-permute-start.5 = (bf16[128,1280]{1,0:T(8,128)(2,1)}, bf16[128,1280]{1,0:T(8,128)(2,1)S(1)}, u32[]{:S(2)}, u32[]{:S(2)}) collective-permute-start(bf16[128,1280]{1,0:T(8,128)(2,1)} %get-tuple-element.61), channel_id=1, source_target_pairs={{0,128},{128,0},{256,384},{384,256},{1,129},{129,1},{257,385},{385... | collective-permute-start | bytes 983048 | tf_op jit(solution)/shard_map/ppermute | solution.py:100
  89.9 24.8 %all-to-all-start.3 = ((bf16[16,16,1280]{2,1,0:T(8,128)(2,1)}), bf16[16,16,1280]{2,1,0:T(8,128)(2,1)S(1)}, u32[]{:S(2)}, u32[]{:S(2)}) async-start(bf16[16,16,1280]{2,1,0:T(8,128)(2,1)} %broadcast_in_dim.28), calls=%async_computation.3 | async-start | bytes 1310720 | tf_op jit(solution)/shard_map/all_to_all | solution.py:116
  97.4 11.3 %collective-permute-start.6 = (bf16[128,1280]{1,0:T(8,128)(2,1)}, bf16[128,1280]{1,0:T(8,128)(2,1)}, u32[]{:S(2)}, u32[]{:S(2)}) collective-permute-start(bf16[128,1280]{1,0:T(8,128)(2,1)} %get-tuple-element.60), channel_id=1, source_target_pairs={{0,128},{128,0},{256,384},{384,256},{1,129},{129,1},{257,385},{385... | collective-permute-start | bytes 983048 | tf_op jit(solution)/shard_map/ppermute | solution.py:100
  116.7 3.4 %collective-permute-start.7 = (bf16[256,512]{1,0:T(8,128)(2,1)S(1)}, bf16[256,512]{1,0:T(8,128)(2,1)S(1)}, u32[]{:S(2)}, u32[]{:S(2)}) collective-permute-start(bf16[256,512]{1,0:T(8,128)(2,1)S(1)} %pad_maximum_fusion.6), channel_id=1, source_target_pairs={{0,1},{1,0},{2,3},{3,2},{4,5},{5,4},{6,7},{7,6},{8,9},{9,8},{10,11... | collective-permute-start | bytes 786440 | tf_op jit(solution)/shard_map/ppermute | solution.py:96
  123.6 13.2 %collective-permute-start.8 = (bf16[128,1280]{1,0:T(8,128)(2,1)S(1)}, bf16[128,1280]{1,0:T(8,128)(2,1)S(1)}, u32[]{:S(2)}, u32[]{:S(2)}) collective-permute-start(bf16[128,1280]{1,0:T(8,128)(2,1)S(1)} %fusion.10), channel_id=1, source_target_pairs={{0,384},{384,0},{128,256},{256,128},{1,385},{385,1},{129,257},{257... | collective-permute-start | bytes 983048 | tf_op jit(solution)/shard_map/ppermute | solution.py:104
  127.9 18.4 %collective-permute-start.9 = (bf16[256,1152]{1,0:T(8,128)(2,1)}, bf16[256,1152]{1,0:T(8,128)(2,1)}, u32[]{:S(2)}, u32[]{:S(2)}) collective-permute-start(bf16[256,1152]{1,0:T(8,128)(2,1)} %pad_maximum_fusion.1), channel_id=1, source_target_pairs={{0,128},{128,0},{256,384},{384,256},{1,129},{129,1},{257,385},{385... | collective-permute-start | bytes 1769480 | tf_op jit(solution)/shard_map/ppermute | solution.py:100
  130.2 23.0 %collective-permute-start.10 = (bf16[256,640]{1,0:T(8,128)(2,1)}, bf16[256,640]{1,0:T(8,128)(2,1)S(1)}, u32[]{:S(2)}, u32[]{:S(2)}) collective-permute-start(bf16[256,640]{1,0:T(8,128)(2,1)} %get-tuple-element.51), channel_id=1, source_target_pairs={{0,128},{128,0},{256,384},{384,256},{1,129},{129,1},{257,385},{385... | collective-permute-start | bytes 983048 | tf_op jit(solution)/shard_map/ppermute | solution.py:100
  137.2 11.0 %copy-start.7 = (bf16[256,256]{1,0:T(8,128)(2,1)S(1)}, bf16[256,256]{1,0:T(8,128)(2,1)}, u32[]{:S(2)}) copy-start(bf16[256,256]{1,0:T(8,128)(2,1)} %copy-done.6) | copy-start | bytes 393220
  137.3 11.0 %copy-start.10 = (bf16[128,1280]{1,0:T(8,128)(2,1)S(1)}, bf16[128,1280]{1,0:T(8,128)(2,1)}, u32[]{:S(2)}) copy-start(bf16[128,1280]{1,0:T(8,128)(2,1)} %get-tuple-element.60) | copy-start | bytes 983044
  137.3 11.0 %copy-start.15 = (bf16[128,1280]{1,0:T(8,128)(2,1)S(1)}, bf16[128,1280]{1,0:T(8,128)(2,1)}, u32[]{:S(2)}) copy-start(bf16[128,1280]{1,0:T(8,128)(2,1)} %copy-done.14) | copy-start | bytes 983044
  138.2 23.8 %all-to-all-start.4 = ((bf16[64,2,1280]{2,1,0:T(2,128)(2,1)}), bf16[64,2,1280]{2,1,0:T(2,128)(2,1)S(1)}, u32[]{:S(2)}, u32[]{:S(2)}) async-start(bf16[64,2,1280]{2,1,0:T(2,128)(2,1)} %all_to_all.22), calls=%async_computation.4 | async-start | bytes 655360 | tf_op jit(solution)/shard_map/all_to_all | solution.py:225
  153.2 8.9 %copy-start.13 = (bf16[16,128]{1,0:T(8,128)(2,1)S(1)}, bf16[16,128]{1,0:T(8,128)(2,1)}, u32[]{:S(2)}) copy-start(bf16[16,128]{1,0:T(8,128)(2,1)} %get-tuple-element.41) | copy-start | bytes 12292
  (8 other events, 19.3 us)
